TPU v7x, 32 devices: a whole 2x2x4 slice. The times are simulated.
32 devices in a mesh: fsdp: 8 (over z, x), ctx: 4 (over y, core).
Axes of the slice: x: 2, y: 2, z: 4, core: 2. Of those that a mesh axis runs over, the one named last changes fastest.
Arguments:
- hidden_in: bfloat16 [16, 256, 1536], P('fsdp', 'ctx'), may hold values from -6 to 6
- lengths: int32 [16], P('fsdp'), may hold values from 64 to 256, as said below
- span_order: int32 [8], replicated, may hold values from 0 to 7, as said below
- attn_gain: bfloat16 [1536], P(('fsdp', 'ctx')), may hold values from 0.25 to 1.75
- w_query: bfloat16 [1536, 1536], P(('fsdp', 'ctx')), may hold values from -0.21875 to 0.21875
- w_key: bfloat16 [1536, 768], P(('fsdp', 'ctx')), may hold values from -0.21875 to 0.21875
- w_value: bfloat16 [1536, 768], P(('fsdp', 'ctx')), may hold values from -0.15625 to 0.15625
- w_out: bfloat16 [1536, 1536], P(('fsdp', 'ctx')), may hold values from -0.625 to 0.625
- mlp_gain: bfloat16 [1536], P(('fsdp', 'ctx')), may hold values from 0.25 to 1.75
- w_gate: bfloat16 [1536, 4096], P(('fsdp', 'ctx')), may hold values from -0.15625 to 0.15625
- w_up: bfloat16 [1536, 4096], P(('fsdp', 'ctx')), may hold values from -0.15625 to 0.15625
- w_down: bfloat16 [4096, 1536], P(('fsdp', 'ctx')), may hold values from -0.09375 to 0.09375
- out_grad: bfloat16 [16, 256, 1536], P('fsdp', 'ctx'), may hold values from -6 to 6
Outputs:
- block_out: bfloat16 [16, 256, 1536], P('fsdp', 'ctx')
- grad_in: bfloat16 [16, 256, 1536], P('fsdp', 'ctx')
- grad_attn_gain: float32 [1536], P(('fsdp', 'ctx'))
- grad_query: float32 [1536, 1536], P(('fsdp', 'ctx'))
- grad_key: float32 [1536, 768], P(('fsdp', 'ctx'))
- grad_value: float32 [1536, 768], P(('fsdp', 'ctx'))
- grad_out: float32 [1536, 1536], P(('fsdp', 'ctx'))
- grad_mlp_gain: float32 [1536], P(('fsdp', 'ctx'))
- grad_gate: float32 [1536, 4096], P(('fsdp', 'ctx'))
- grad_up: float32 [1536, 4096], P(('fsdp', 'ctx'))
- grad_down: float32 [4096, 1536], P(('fsdp', 'ctx'))
Inputs may be any that keep to these rules, and one draw needn't show every extreme that they name: `lengths`: of the 2 sequences of each fsdp index, one chosen at random has length 256. `span_order`: paired spans: for each index d of ctx, the stored spans 2 d and 2 d + 1 hold the spans c and 7 - c of the sequence, for some c below 4, each c once; each span has 32 slots.
All inputs are finite; a program needn't handle non-finite values.
Results may differ from a plain program's by a relative error of at most 0.02.
Values may be sent and summed in bfloat16 or wider, within the bound.
No kernel may reach another device: no remote copies, remote signals or barrier semaphores. Data moves between devices by JAX's collectives and lax.ppermute only.
A program may use at most 192 MiB of HBM per device.

v0:
```python
import jax
import jax.numpy as jnp
import numpy as np
from jax import lax
from jax.experimental import pallas as pl
from jax.experimental.pallas import tpu as pltpu
from jax.sharding import PartitionSpec as P

H = 16
KV = 8
HD = 96
GROUP = H // KV
QW = GROUP * HD
AXES = ("fsdp", "ctx")

epsilon = 1e-05
rope_base = 100000.0
masked_score = -1e30
scale = HD ** (-0.5)
BF = jnp.bfloat16
F32 = jnp.float32


def mm(left, right):
    return jnp.dot(left, right, preferred_element_type=F32)


def mm_lt(left, right):
    return lax.dot_general(left, right, (((0,), (0,)), ((), ())), preferred_element_type=F32)


def mm_rt(left, right):
    return lax.dot_general(left, right, (((1,), (1,)), ((), ())), preferred_element_type=F32)


def plus(a, b):
    return a + b


def send(x, pairs):
    return lax.ppermute(x, AXES, pairs)


def unit_of_work(go, body, *args):
    def idle(*args):
        return jax.tree.map(lambda leaf: jnp.zeros(leaf.shape, leaf.dtype), jax.eval_shape(body, *args))

    return lax.cond(go, body, idle, *args)


def fence(*items):
    return lax.optimization_barrier(items)


class Layout:
    def __init__(self):
        self.ctx = lax.axis_size("ctx")
        self.fsdp = lax.axis_size("fsdp")
        self.tpf = KV // self.ctx
        self.nz = self.fsdp // self.tpf
        self.total = self.fsdp * self.ctx
        self.fast = self.ctx == 4 and self.tpf == 2 and self.nz == 4
        self.f = lax.axis_index("fsdp")
        self.c = lax.axis_index("ctx")
        self.z = self.f // self.tpf
        self.place = [(b, (b % self.nz) * KV + b // self.nz) for b in range(self.total)]
        self.back = [(d, s) for s, d in self.place]

    def exchange(self, x):
        if self.tpf == 1:
            return lax.all_to_all(x, "ctx", split_axis=0, concat_axis=0, tiled=True)
        groups = [[z * KV + i for i in range(KV)] for z in range(self.nz)]
        return lax.all_to_all(
            x, AXES, split_axis=0, concat_axis=0, tiled=True, axis_index_groups=groups
        )

    def lines(self):
        return [[z * KV + i for z in range(self.nz)] for i in range(KV)]

    def spread(self, x):
        if self.tpf == 1:
            return lax.all_gather(x, "fsdp", axis=0, tiled=True)
        return lax.all_gather(x, AXES, axis=0, tiled=True, axis_index_groups=self.lines())

    def gather_sum(self, x):
        x = x.astype(BF)
        if self.tpf == 1:
            return lax.psum_scatter(x, "fsdp", scatter_dimension=0, tiled=True)
        return lax.psum_scatter(
            x, AXES, scatter_dimension=0, tiled=True, axis_index_groups=self.lines()
        )


class Line(Layout):
    def __init__(self):
        super().__init__()
        total = self.total
        self.core = [(d, d ^ 1) for d in range(total)]
        self.first = [(d, d ^ (2 if d & 1 else 4)) for d in range(total)]
        self.second = [(d, d ^ (4 if d & 1 else 2)) for d in range(total)]
        self.xflip = [(d, d ^ 4) for d in range(total)]

        def planes(pairs):
            return [(s * KV + i, d * KV + i) for s, d in pairs for i in range(KV)]

        self.pair = planes([(0, 1), (1, 0), (2, 3), (3, 2)])
        self.inner = planes([(1, 2), (2, 1)])
        self.outward = planes([(1, 0), (2, 3)])
        self.inward = planes([(0, 1), (3, 2)])
        z = self.z
        low = z < 2
        self.order = [z, z ^ 1, jnp.where(low, 2, 1), jnp.where(low, 3, 0)]
        table = ((0, 1, 3, 3), (1, 0, 2, 2), (2, 2, 0, 1), (3, 3, 1, 0))
        self.slot = [
            jnp.where(z == 0, r[0], jnp.where(z == 1, r[1], jnp.where(z == 2, r[2], r[3])))
            for r in table
        ]

    def take_columns(self, x, blocks):
        width = x.shape[-1] // self.nz
        return jnp.concatenate(
            [lax.dynamic_slice_in_dim(x, k * width, width, axis=-1) for k in blocks], axis=-1
        )

    def take_rows(self, pieces):
        full = jnp.stack(pieces)
        return jnp.concatenate(
            [lax.dynamic_index_in_dim(full, k, axis=0, keepdims=False) for k in self.slot], axis=0
        )

    def to_pieces(self, x):
        full = x.reshape((self.nz, x.shape[0] // self.nz) + x.shape[1:])
        return [lax.dynamic_index_in_dim(full, k, axis=0, keepdims=False) for k in self.order]

    def all_tokens(self, x):
        x = jnp.stack([x, send(x, self.first)])
        x = jnp.stack([x, send(x, self.second)])
        x = jnp.stack([x, send(x, self.core)])
        return x.reshape(-1, x.shape[-1])

    def plane_tokens(self, x):
        x = jnp.stack([x, send(x, self.first)])
        x = jnp.stack([x, send(x, self.second)])
        other = send(x, self.core)
        return x.reshape(-1, x.shape[-1]), other.reshape(-1, x.shape[-1])

    def collect_tokens(self, x, slots):
        x = x.reshape(2, 2, 2, 2, slots, x.shape[-1])
        x = plus(x[0], send(x[1], self.core))
        x = plus(x[0], send(x[1], self.second))
        return x[0].astype(F32) + send(x[1], self.first).astype(F32)

    def to_seqs(self, x, slots):
        x = x.reshape(2, 2, 2, 2, slots, x.shape[-1])
        halves = []
        for dc in range(2):
            even = ((self.c & 1) ^ dc) == 0
            h = x[dc]
            halves.append(jnp.where(even, jnp.swapaxes(h, 0, 1), h))
        x = jnp.stack(halves, axis=0)
        x = jnp.transpose(x, (1, 3, 0, 2, 4, 5))
        return x.reshape(4, 4 * slots, x.shape[-1])

    def from_seqs(self, x, slots):
        x = x.reshape(2, 2, 2, 2, slots, x.shape[-1])
        x = jnp.transpose(x, (2, 0, 3, 1, 4, 5))
        halves = []
        for dc in range(2):
            even = ((self.c & 1) ^ dc) == 0
            h = x[dc]
            halves.append(jnp.where(even, jnp.swapaxes(h, 0, 1), h))
        return jnp.stack(halves, axis=0).reshape(16 * slots, x.shape[-1])


def positions_of(span_order, index, slots):
    span_len = slots // 2
    at = jnp.arange(slots, dtype=jnp.int32)
    pair = lax.dynamic_slice_in_dim(span_order, 2 * index, 2)
    return jnp.where(at < span_len, pair[0], pair[1]) * span_len + at % span_len


def rope_tables(pos):
    frequency = rope_base ** (-2.0 * jnp.arange(HD // 2, dtype=F32) / HD)
    angles = pos.astype(F32)[:, None] * frequency[None, :]
    return jnp.cos(angles), jnp.sin(angles)


def rotate(v, cosines, sines):
    half = HD // 2
    co, si = cosines[None, :, None, :], sines[None, :, None, :]
    one, two = v[..., :half], v[..., half:]
    return jnp.concatenate([one * co - two * si, two * co + one * si], axis=-1)


def unit_rows(x):
    inverse = lax.rsqrt(jnp.mean(x * x, axis=-1, keepdims=True) + epsilon)
    return x * inverse, inverse


def unit_back(scaled, unit, inverse):
    return inverse * (scaled - unit * jnp.mean(scaled * unit, axis=-1, keepdims=True))


def attend(pre, pos, seq_len, cosines, sines):
    seqs, length, _ = pre.shape
    q = rotate(pre[..., :QW].reshape(seqs, length, GROUP, HD), cosines, sines).astype(BF)
    k = rotate(pre[..., QW : QW + HD].reshape(seqs, length, 1, HD), cosines, sines)[:, :, 0].astype(BF)
    v = pre[..., QW + HD :].astype(BF)
    allowed = (pos[None, None, :] <= pos[None, :, None]) & (
        pos[None, None, :] < seq_len[:, None, None]
    )
    scores = jnp.einsum("sqgd,snd->sgqn", q, k, preferred_element_type=F32) * scale
    scores = jnp.where(allowed[:, None], scores, masked_score)
    top = jnp.max(scores, axis=-1, keepdims=True)
    expo = jnp.exp(scores - top)
    probs = expo / jnp.sum(expo, axis=-1, keepdims=True)
    low = probs.astype(BF)
    attended = jnp.einsum("sgqn,snd->sqgd", low, v, preferred_element_type=F32)
    return attended.astype(BF).reshape(seqs, length, QW), (q, k, v, probs, low)


def attend_back(g_att, kept, cosines, sines):
    q, k, v, probs, low = kept
    seqs, length, _ = g_att.shape
    g_att = g_att.reshape(seqs, length, GROUP, HD)
    g_probs = jnp.einsum("sqgd,snd->sgqn", g_att, v, preferred_element_type=F32)
    inner = jnp.sum(probs * g_probs, axis=-1, keepdims=True)
    g_scores = (probs * (g_probs - inner)).astype(BF)
    g_q = jnp.einsum("sgqn,snd->sqgd", g_scores, k, preferred_element_type=F32) * scale
    g_k = jnp.einsum("sgqn,sqgd->snd", g_scores, q, preferred_element_type=F32) * scale
    g_v = jnp.einsum("sgqn,sqgd->snd", low, g_att, preferred_element_type=F32)
    return jnp.concatenate(
        [
            rotate(g_q, cosines, -sines).astype(BF).reshape(seqs, length, QW),
            rotate(g_k[:, :, None], cosines, -sines).astype(BF)[:, :, 0],
            g_v.astype(BF),
        ],
        axis=-1,
    )


def swiglu(gate_up):
    half = gate_up.shape[-1] // 2
    gate, up = gate_up[:, :half], gate_up[:, half:]
    return (jax.nn.silu(gate) * up).astype(BF)


def swiglu_back(gate_up, g_hidden):
    half = gate_up.shape[-1] // 2
    gate, up = gate_up[:, :half], gate_up[:, half:]
    sig = jax.nn.sigmoid(gate)
    g_gate = (g_hidden * up * sig * (1.0 + gate * (1.0 - sig))).astype(BF)
    g_up = (g_hidden * gate * sig).astype(BF)
    return jnp.concatenate([g_gate, g_up], axis=-1)


def pack_attention(w_query, w_key, w_value, gain):
    rows = w_query.shape[0]
    parts = [
        (w.astype(F32) * gain).astype(BF).reshape(rows, KV, w.shape[1] // KV)
        for w in (w_query, w_key, w_value)
    ]
    return jnp.transpose(jnp.concatenate(parts, axis=2), (1, 0, 2))


def unpack_attention(u):
    u = jnp.transpose(u, (1, 0, 2)).astype(F32)
    rows = u.shape[0]
    return (
        u[..., :QW].reshape(rows, KV * QW),
        u[..., QW : QW + HD].reshape(rows, KV * HD),
        u[..., QW + HD :].reshape(rows, KV * HD),
    )


def pack_mlp(w_gate, w_up, gain, nz):
    rows = w_gate.shape[0]

    def columns(w):
        w = (w.astype(F32) * gain).astype(BF).reshape(rows, nz, KV, -1)
        return jnp.transpose(w, (2, 0, 1, 3)).reshape(KV, rows, -1)

    return jnp.concatenate([columns(w_gate), columns(w_up)], axis=2)


def unpack_mlp(u, nz):
    rows = u.shape[1]
    u = u.reshape(KV, rows, 2, nz, -1)
    u = jnp.transpose(u, (2, 1, 3, 0, 4)).reshape(2, rows, -1).astype(F32)
    return u[0], u[1]


SMEM = pl.BlockSpec(memory_space=pltpu.SMEM)
VMEM = pl.BlockSpec(memory_space=pltpu.VMEM)
WIDE = QW + 2 * HD
FREE = pl.CostEstimate(flops=0, bytes_accessed=0, transcendentals=0)
ROOM = pltpu.CompilerParams(vmem_limit_bytes=56 * 1024 * 1024)


def shaped(*shape, dtype=BF):
    return jax.ShapeDtypeStruct(shape, dtype)


def kernel_call(body, outs, scratch=()):
    def call(scalars, *arrays):
        return pl.pallas_call(
            body,
            out_shape=outs,
            in_specs=[SMEM] * len(scalars) + [VMEM] * len(arrays),
            out_specs=jax.tree.map(lambda _: VMEM, outs),
            scratch_shapes=list(scratch),
            compiler_params=ROOM,
            cost_estimate=FREE,
        )(*scalars, *arrays)

    return call


def moving_call(body, outs, scratch=(), copies=1):
    def call(scalars, *arrays):
        anywhere_spec = pl.BlockSpec(memory_space=pl.ANY)
        return pl.pallas_call(
            body,
            out_shape=outs,
            in_specs=[SMEM] * len(scalars) + [pl.BlockSpec(memory_space=pltpu.HBM)] * len(arrays),
            out_specs=jax.tree.map(lambda _: anywhere_spec, outs),
            scratch_shapes=list(scratch) + [pltpu.SemaphoreType.DMA((copies,))],
            compiler_params=ROOM,
            cost_estimate=FREE,
        )(*scalars, *arrays)

    return call


class Copies:
    def __init__(self, sems):
        self.sems = sems
        self.used = 0

    def start(self, source, target):
        copy = pltpu.make_async_copy(source, target, self.sems.at[self.used])
        self.used += 1
        copy.start()
        return copy


def vmem(*arrays):
    return [pltpu.VMEM(a.shape, a.dtype) for a in arrays]


def dot(a, b, dims=((1,), (0,))):
    return lax.dot_general(a, b, (dims, ((), ())), preferred_element_type=F32)


LEFT_T = ((0,), (0,))
RIGHT_T = ((1,), (1,))


def block_rows(core, seq, dc, dy, slots):
    dx, m = seq // 2, seq % 2
    even = (core ^ dc) == 0
    s1 = jnp.where(even, dx, dy)
    s2 = jnp.where(even, dy, dx)
    return pl.multiple_of(((s2 * 2 + s1) * 2 + m) * slots, slots)


def blocks_of(slots):
    for dc in range(2):
        for dy in range(2):
            b = dc * 2 + dy
            yield dc, dy, slice(b * slots, (b + 1) * slots)


def spans_of(spans, ctx):
    out = []
    for dc in range(2):
        for dy in range(2):
            other = ctx ^ (dy * 2 + dc)
            out += [spans[2 * other], spans[2 * other + 1]]
    return out


def along(held, length, axis, shape):
    at = lax.broadcasted_iota(jnp.int32, shape, axis) % length
    step = length // len(held)
    pos = at % step
    for i, span in enumerate(held):
        pos = pos + jnp.where(at // step == i, span * step, 0)
    return pos


def rotary_rows(held, table, out):
    step = out.shape[0] // len(held)
    for i, span in enumerate(held):
        out[i * step : (i + 1) * step, :] = table[pl.ds(pl.multiple_of(span * step, step), step), :]


def rotary_copies(copies, held, table, out):
    step = out.shape[0] // len(held)
    return [
        copies.start(table.at[pl.ds(pl.multiple_of(span * step, step), step)], out.at[pl.ds(i * step, step)])
        for i, span in enumerate(held)
    ]


def turn(x, cosines, sines):
    half, width = HD // 2, x.shape[1]
    lane = lax.broadcasted_iota(jnp.int32, x.shape, 1) % HD
    partner = jnp.where(lane < half, pltpu.roll(x, width - half, 1), pltpu.roll(x, half, 1))
    return x * cosines + partner * sines


def probabilities(q, k, allowed):
    scores = jnp.where(allowed, dot(q, k, RIGHT_T) * scale, masked_score)
    expo = jnp.exp(scores - jnp.max(scores, axis=-1, keepdims=True))
    return expo / jnp.sum(expo, axis=-1, keepdims=True)


def heads_of(x):
    return [x[:, h * HD : (h + 1) * HD] for h in range(x.shape[1] // HD)]


def assemble(meta, pieces, out):
    p0, p1, p2, p3, p4, p5 = pieces
    step = p0.shape[0]
    for s, parts in enumerate(((p0,), (p1,), (p2, p3), (p4, p5))):
        piece = parts[0][...]
        if len(parts) > 1:
            piece = piece + parts[1][...]
        out[pl.ds(pl.multiple_of(meta[s] * step, step), step), :] = piece


def fetch_qkv(full, out):
    step = full.shape[2]
    for z in range(full.shape[0]):
        out[z * step : (z + 1) * step, :] = full[z, :step, :]


def fetch_out(full, out):
    nz, total, step = full.shape
    count = out.shape[1] // step
    rows = (total - step) // count
    for z in range(nz):
        for k in range(count):
            out[z * rows : (z + 1) * rows, k * step : (k + 1) * step] = full[
                z, step + k * rows : step + (k + 1) * rows, :
            ]


def stacked_columns(x, cut):
    return jnp.concatenate([x[:, k : k + cut] for k in range(0, x.shape[1], cut)], axis=0)


def column(row):
    n = row.shape[1]
    same = lax.broadcasted_iota(jnp.int32, (n, n), 0) == lax.broadcasted_iota(jnp.int32, (n, n), 1)
    return jnp.sum(jnp.where(same, row, 0.0), axis=1, keepdims=True)


def row_of(col):
    n = col.shape[0]
    same = lax.broadcasted_iota(jnp.int32, (n, n), 0) == lax.broadcasted_iota(jnp.int32, (n, n), 1)
    return jnp.sum(jnp.where(same, col, 0.0), axis=0, keepdims=True)


def pack_attention_kernel(wq, wk, wv, gain, out):
    g = column(gain[...].astype(F32))
    q, k, v = ((w[...].astype(F32) * g).astype(BF) for w in (wq, wk, wv))
    for j in range(KV):
        out[j] = jnp.concatenate(
            [q[:, j * QW : (j + 1) * QW], k[:, j * HD : (j + 1) * HD], v[:, j * HD : (j + 1) * HD]], axis=1
        )


def pack_mlp_kernel(wg, wu, gain, out):
    g = column(gain[...].astype(F32))
    half = out.shape[2] // 2
    blocks = 4
    hid = half // blocks
    for h, w in enumerate((wg, wu)):
        x = (w[...].astype(F32) * g).astype(BF)
        for z in range(blocks):
            for j in range(KV):
                out[j, :, h * half + z * hid : h * half + (z + 1) * hid] = x[
                    :, (z * KV + j) * hid : (z * KV + j + 1) * hid
                ]


def unpack_attention_kernel(u, wq, wk, wv, gain, gq, gk, gv, total):
    g = column(gain[...].astype(F32))
    acc = jnp.zeros(g.shape, F32)
    for w, out, lo, n in ((wq, gq, 0, QW), (wk, gk, QW, HD), (wv, gv, QW + HD, HD)):
        part = jnp.concatenate([u[j, :, lo : lo + n] for j in range(KV)], axis=1).astype(F32)
        out[...] = part * g
        acc += jnp.sum(part * w[...].astype(F32), axis=1, keepdims=True)
    total[...] = row_of(acc)


def unpack_mlp_kernel(u, wg, wu, gain, gg, gu, total):
    g = column(gain[...].astype(F32))
    acc = jnp.zeros(g.shape, F32)
    half = wg.shape[1] // KV
    blocks = 4
    hid = half // blocks
    for j in range(KV):
        x = u[j].astype(F32)
        for h, (w, out) in enumerate(((wg, gg), (wu, gu))):
            for z in range(blocks):
                at = slice((z * KV + j) * hid, (z * KV + j + 1) * hid)
                part = x[:, h * half + z * hid : h * half + (z + 1) * hid]
                out[:, at] = part * g
                acc += jnp.sum(part * w[:, at].astype(F32), axis=1, keepdims=True)
    total[...] = row_of(acc)


def usable_rows(lens, spans, ctx, shape):
    at = lax.broadcasted_iota(jnp.int32, shape, 0)
    slots = shape[0] // 2
    slot, step = at % slots, slots // 2
    pos = jnp.where(slot < step, spans[2 * ctx], spans[2 * ctx + 1]) * step + slot % step
    length = jnp.where(at < slots, lens[0], lens[1])
    return (pos < length).astype(F32)


def prepare_kernel(meta, lens, spans, x, g, xhat, inverse, g_low):
    v = x[...].astype(F32)
    inv = lax.rsqrt(jnp.mean(v * v, axis=-1, keepdims=True) + epsilon)
    inverse[...] = inv
    xhat[...] = (v * inv).astype(BF)
    g_low[...] = (g[...].astype(F32) * usable_rows(lens, spans, meta[5], inverse.shape)).astype(BF)


def finish_kernel(meta, lens, spans, residual, a, b, out):
    total = residual[...] + a[...].astype(F32) + b[...].astype(F32)
    out[...] = (total * usable_rows(lens, spans, meta[5], (total.shape[0], 1))).astype(BF)


def attention_kernel(
    meta, lens, spans, xa, xb, full, cos_table, sin_table, wqkv, qkv, att, xseq, cosines, sines
):
    core, ctx = meta[4], meta[5]
    slots = xa.shape[0] // 8
    length = xseq.shape[0]
    fetch_qkv(full, wqkv)
    held = spans_of(spans, ctx)
    rotary_rows(held, cos_table, cosines)
    rotary_rows(held, sin_table, sines)
    posc = along(held, length, 0, (GROUP * length, length))
    posr = along(held, length, 1, (GROUP * length, length))
    causal = posr <= posc

    def one(seq, carry):
        for dc, dy, rows in blocks_of(slots):
            xseq[rows, :] = (xa, xb)[dc][pl.ds(block_rows(core, seq, dc, dy, slots), slots), :]
        low = turn(dot(xseq[...], wqkv[...]), cosines[...], sines[...]).astype(BF)
        qkv[seq] = low
        one_q, two_q, k, v = heads_of(low)
        q = jnp.concatenate([one_q, two_q], axis=0)
        allowed = causal & (posr < lens[seq])
        mixed = dot(probabilities(q, k, allowed).astype(BF), v)
        out = jnp.concatenate([mixed[:length], mixed[length:]], axis=1).astype(BF)
        for dc, dy, rows in blocks_of(slots):
            att[dc, pl.ds(block_rows(core, seq, dc, dy, slots), slots), :] = out[rows]
        return carry

    lax.fori_loop(0, 4, one, 0, unroll=True)


def project_kernel(att, full, wout, mine, theirs):
    fetch_out(full, wout)
    theirs[...] = dot(att[1], wout[...]).astype(BF)
    mine[...] = dot(att[0], wout[...]).astype(BF)


def attention_back_kernel(
    meta, lens, spans,
    h_ga, h_gb, h_att, h_wout, h_wqkv, h_qkv, h_xa, h_xb, cos_table, sin_table,
    o_mine, o_theirs, o0, o1, o2, o3,
    ga, gb, att, wout, wqkv, qkv, xa, xb, mine, theirs, u0, u1, u2, u3, g_pre, gseq, cosines, sines, out_grad, sems,
):
    copies = Copies(sems)
    held = spans_of(spans, meta[5])
    first = [copies.start(h, v) for h, v in ((h_wout, wout), (h_qkv, qkv), (h_ga, ga), (h_gb, gb))]
    first += rotary_copies(copies, held, cos_table, cosines) + rotary_copies(copies, held, sin_table, sines)
    for c in first:
        c.wait()
    later = [copies.start(h, v) for h, v in ((h_xa, xa), (h_xb, xb), (h_att, att), (h_wqkv, wqkv))]
    core, ctx = meta[4], meta[5]
    slots = ga.shape[0] // 8
    length = gseq.shape[0]
    posc = along(held, length, 0, (GROUP * length, length))
    posr = along(held, length, 1, (GROUP * length, length))
    causal = posr <= posc

    def one(seq, carry):
        for dc, dy, rows in blocks_of(slots):
            gseq[rows, :] = (ga, gb)[dc][pl.ds(block_rows(core, seq, dc, dy, slots), slots), :]
        g_att = dot(gseq[...], wout[...], RIGHT_T).astype(BF)
        one_q, two_q, k, v = heads_of(qkv[seq])
        q = jnp.concatenate([one_q, two_q], axis=0)
        g = jnp.concatenate(heads_of(g_att), axis=0)
        allowed = causal & (posr < lens[seq])
        p = probabilities(q, k, allowed)
        g_p = dot(g, v, RIGHT_T)
        g_s = (p * (g_p - jnp.sum(p * g_p, axis=-1, keepdims=True))).astype(BF)
        g_q = dot(g_s, k) * scale
        g_k = dot(g_s, q, LEFT_T) * scale
        g_v = dot(p.astype(BF), g, LEFT_T)
        full = jnp.concatenate([g_q[:length], g_q[length:], g_k, g_v], axis=1)
        out = turn(full, cosines[...], -sines[...]).astype(BF)
        for dc, dy, rows in blocks_of(slots):
            g_pre[dc, pl.ds(block_rows(core, seq, dc, dy, slots), slots), :] = out[rows]
        return carry

    lax.fori_loop(0, 4, one, 0, unroll=True)
    for c in later:
        c.wait()
    gone = []
    out_grad[...] = (dot(att[0], ga[...], LEFT_T) + dot(att[1], gb[...], LEFT_T)).astype(BF)
    step = xa.shape[1] // 4
    block = u0.shape[1]
    count = out_grad.shape[1] // block
    low = out_grad.shape[0] // 4
    for s, u, o in ((3, u3, o3), (2, u2, o2), (1, u1, o1), (0, u0, o0)):
        at = pl.ds(pl.multiple_of(meta[s] * step, step), step)
        u[:step, :] = (dot(xa[:, at], g_pre[0], LEFT_T) + dot(xb[:, at], g_pre[1], LEFT_T)).astype(BF)
        at = pl.ds(pl.multiple_of(meta[s] * low, low), low)
        for k in range(count):
            u[step + k * low : step + (k + 1) * low, :] = out_grad[at, k * block : (k + 1) * block]
        gone.append(copies.start(u, o))
    theirs[...] = dot(g_pre[1], wqkv[...], RIGHT_T).astype(BF)
    gone.append(copies.start(theirs, o_theirs))
    mine[...] = dot(g_pre[0], wqkv[...], RIGHT_T).astype(BF)
    gone.append(copies.start(mine, o_mine))
    for c in gone:
        c.wait()


def mlp_kernel(
    meta,
    h_ma, h_mb, h_ea, h_eb, h_wgu, h0, h1, h2, h3, h4, h5,
    o_down_mine, o_down_theirs, o_mine, o_theirs, o_u,
    ma, mb, ea, eb, wgu, d0, d1, d2, d3, d4, d5, down_mine, down_theirs, mine, theirs, u, hidden, g_gu, wdown, sems,
):
    copies = Copies(sems)
    came = [copies.start(h_wgu, wgu), copies.start(h_mb, mb)]
    pieces = (d0, d1, d2, d3, d4, d5)
    downs = [copies.start(h, d) for h, d in zip((h0, h1, h2, h3, h4, h5), pieces)]
    came_eb = copies.start(h_eb, eb)
    came_ma = copies.start(h_ma, ma)
    came_ea = copies.start(h_ea, ea)
    gone = []
    half = wgu.shape[1] // 2
    for c in came:
        c.wait()
    for part, x, g, down, back, o_down, o_back in (
        (1, mb, eb, down_theirs, theirs, o_down_theirs, o_theirs),
        (0, ma, ea, down_mine, mine, o_down_mine, o_mine),
    ):
        if part == 0:
            came_ma.wait()
        gate_up = dot(x[...], wgu[...])
        gate, up = gate_up[:, :half], gate_up[:, half:]
        sig = 1.0 / (1.0 + jnp.exp(-gate))
        act = gate * sig
        hid = (act * up).astype(BF)
        hidden[part] = hid
        if part == 1:
            for c in downs:
                c.wait()
            assemble(meta, pieces, wdown)
            came_eb.wait()
        else:
            came_ea.wait()
        g_hidden = dot(g[...], wdown[...], RIGHT_T)
        g_gu[part, :, :half] = (g_hidden * up * sig * (1.0 + gate * (1.0 - sig))).astype(BF)
        g_gu[part, :, half:] = (g_hidden * act).astype(BF)
        back[...] = dot(g_gu[part], wgu[...], RIGHT_T).astype(BF)
        gone.append(copies.start(back, o_back))
        down[...] = dot(hid, wdown[...]).astype(BF)
        gone.append(copies.start(down, o_down))
    nz, _, wide = u.shape
    piece = ma.shape[1] // nz
    step = hidden.shape[2] // nz
    for z in range(nz):
        at = slice(z * piece, (z + 1) * piece)
        both = dot(ma[:, at], g_gu[0], LEFT_T) + dot(mb[:, at], g_gu[1], LEFT_T)
        u[z, :piece, :] = both.astype(BF)
        at = slice(z * step, (z + 1) * step)
        both = (dot(hidden[0, :, at], ea[...], LEFT_T) + dot(hidden[1, :, at], eb[...], LEFT_T)).astype(BF)
        u[z, piece : piece + step, :] = both[:, :wide]
        rest = both.shape[1] - wide
        u[z, piece + step :, :rest] = both[: step // 2, wide:]
        u[z, piece + step :, rest:] = both[step // 2 :, wide:]
        gone.append(copies.start(u.at[z], o_u.at[z]))
    for c in gone:
        c.wait()


def unpack_down_kernel(u, out):
    step, wide = out.shape[0], u.shape[1]
    rest = out.shape[1] - wide
    out[:, :wide] = u[:step, :].astype(F32)
    out[: step // 2, wide:] = u[step:, :rest].astype(F32)
    out[step // 2 :, wide:] = u[step:, rest:].astype(F32)


def sums_kernel(a, b, c, d, ab, cd):
    ab[...] = a[...] + b[...]
    cd[...] = c[...] + d[...]


def last_sum_kernel(a, b, c, qkv, out):
    total = (a[...].astype(F32) + b[...].astype(F32) + c[...].astype(F32)).astype(BF)
    blocks, rows, width = qkv.shape
    for j in range(blocks):
        qkv[j] = total[j * rows : (j + 1) * rows]
    low = out.shape[0]
    for k in range(out.shape[1] // width):
        at = blocks * rows + k * low
        out[:, k * width : (k + 1) * width] = total[at : at + low]


def norm_kernel(source, a, b, residual, xhat, inverse):
    r = source[...].astype(F32) + a[...].astype(F32) + b[...].astype(F32)
    inv = lax.rsqrt(jnp.mean(r * r, axis=-1, keepdims=True) + epsilon)
    residual[...] = r
    inverse[...] = inv
    xhat[...] = (r * inv).astype(BF)


def norm_back(g_res, source, inverse, a, b):
    scaled = a[...].astype(F32) + b[...].astype(F32)
    inv = inverse[...]
    unit = source[...].astype(F32) * inv
    back = inv * (scaled - unit * jnp.mean(scaled * unit, axis=-1, keepdims=True))
    return g_res[...].astype(F32) + back


def norm_back_kernel(g_res, source, inverse, a, b, out, low):
    g = norm_back(g_res, source, inverse, a, b)
    out[...] = g
    low[...] = g.astype(BF)


def norm_back_low_kernel(g_res, source, inverse, a, b, low):
    low[...] = norm_back(g_res, source, inverse, a, b).astype(BF)


def rotary_constants(total):
    frequency = rope_base ** (-2.0 * np.arange(HD // 2, dtype=np.float32) / HD).astype(np.float32)
    angles = np.arange(total, dtype=np.float32)[:, None] * frequency[None, :].astype(np.float32)
    c, s = np.cos(angles), np.sin(angles)
    flat, signed = np.concatenate([c, c], 1), np.concatenate([-s, s], 1)
    cosines = np.concatenate([flat] * (GROUP + 1) + [np.ones_like(flat)], 1)
    sines = np.concatenate([signed] * (GROUP + 1) + [np.zeros_like(flat)], 1)
    return jnp.asarray(cosines, F32), jnp.asarray(sines, F32)


def paired(*items):
    return sum(jnp.sum(w.astype(F32) * g, axis=1) for w, g in items)


def on_line(
    hidden_in, lengths, span_order, attn_gain, w_query, w_key, w_value, w_out,
    mlp_gain, w_gate, w_up, w_down, out_grad,
):
    lay = Line()
    _, slots, width = hidden_in.shape
    rows, nz = w_query.shape[0], lay.nz
    tokens, length, own = 16 * slots, 4 * slots, 2 * slots
    go = lengths[0] > 0
    meta = jnp.stack([k.astype(jnp.int32) for k in (*lay.order, lay.c & 1, lay.c)])
    gain, gain_m = attn_gain[None, :], mlp_gain[None, :]
    cos_table, sin_table = rotary_constants(length)

    def halves(x):
        return x.reshape(2, x.shape[0] // 2, width)

    wide = w_gate.shape[1] * 2 // KV
    cut = wide // 2
    tables = [pltpu.VMEM((length, WIDE), F32)] * 2

    def flat(x):
        return x.reshape(-1, width)

    d1 = send(w_down, lay.pair)
    d2 = send(w_down, lay.inner)
    q0 = lay.exchange(
        kernel_call(pack_attention_kernel, shaped(KV, rows, WIDE))((), w_query, w_key, w_value, gain)
    )
    theirs = send(lengths, lay.xflip)
    o0 = send(w_out, lay.place)
    gu_s = kernel_call(pack_mlp_kernel, shaped(KV, rows, wide))((), w_gate, w_up, gain_m)
    xhat, inverse, g_low = kernel_call(
        prepare_kernel, (shaped(own, width), shaped(own, 1, dtype=F32), shaped(own, width))
    )((meta, lengths, span_order), hidden_in.reshape(own, width), out_grad.reshape(own, width))
    q0, d1, d2, theirs, gu_s, xhat, g_low = fence(q0, d1, d2, theirs, gu_s, xhat, g_low)
    d3 = send(d2, lay.outward)
    d4 = send(d1, lay.inner)
    x1 = send(xhat, lay.first)
    attn_piece = jnp.concatenate([q0.reshape(KV * rows, WIDE), stacked_columns(o0, WIDE)], axis=0)
    d3, d4, x1, attn_piece = fence(d3, d4, x1, attn_piece)
    attn_full = lay.spread(attn_piece)

    def gather(xhat, x1, g_low, gu_s):
        gu0 = lay.exchange(gu_s)
        x01 = jnp.stack([xhat, x1])
        x2 = send(x01, lay.second)
        x2, gu0, x01, g_low = fence(x2, gu0, x01, g_low)
        x0123 = jnp.stack([x01, x2])
        x3 = send(x0123, lay.core)
        e1 = send(g_low, lay.first)
        x3, x0123, e1 = fence(x3, x0123, e1)
        e01 = jnp.stack([g_low, e1])
        return x0123, x3, gu0, e01

    xa, xb, gu0, e01 = unit_of_work(go, gather, xhat, x1, g_low, gu_s)
    attn_full, gu0 = fence(attn_full, gu0)
    wgu = lay.spread(gu0.reshape(KV * rows, wide))
    attn_full = attn_full.reshape(nz, -1, WIDE)
    seq_len = jnp.concatenate([lengths, theirs])

    def forward(meta, seq_len, span_order, xa, xb, attn_full, cos_table, sin_table, hidden_in, e01, d4):
        e2 = send(e01, lay.second)
        wqkv, qkv, att = kernel_call(
            attention_kernel,
            (shaped(width, WIDE), shaped(4, length, WIDE), shaped(2, tokens // 2, QW)),
            scratch=[pltpu.VMEM((length, width), BF)] + tables,
        )((meta, seq_len, span_order), flat(xa), flat(xb), attn_full, cos_table, sin_table)
        wqkv, qkv, att, e2 = fence(wqkv, qkv, att, e2)
        wout, mine, other = kernel_call(
            project_kernel, (shaped(QW, width), shaped(tokens // 2, width), shaped(tokens // 2, width))
        )((), att, attn_full)
        got = send(other, lay.core)
        r = halves(plus(mine, got))
        e0123 = jnp.stack([e01, e2])
        r, e0123 = fence(r, e0123)
        got = send(r[1], lay.second)
        e3 = send(e0123, lay.core)
        got, e3, r = fence(got, e3, r)
        r = halves(plus(r[0], got))
        got = send(r[1], lay.first)
        residual, xm0, inverse_m = kernel_call(
            norm_kernel, (shaped(own, width, dtype=F32), shaped(own, width), shaped(own, 1, dtype=F32))
        )((), hidden_in.reshape(own, width), r[0], got)
        m01 = jnp.stack([xm0, send(xm0, lay.first)])
        m01, d4 = fence(m01, d4)
        m2 = send(m01, lay.second)
        d5 = send(d4, lay.outward)
        m2, d5 = fence(m2, d5)
        ma = jnp.stack([m01, m2])
        mb = send(ma, lay.core)
        return wqkv, qkv, att, wout, residual, inverse_m, flat(ma), flat(mb), flat(e0123), flat(e3), d5

    wqkv, qkv, att, wout, residual, inverse_m, ma, mb, ea, eb, d5 = unit_of_work(
        go, forward, meta, seq_len, span_order, xa, xb, attn_full, cos_table, sin_table, hidden_in, e01, d4
    )
    half_rows = shaped(tokens // 2, width)
    low = w_down.shape[0]
    piece = KV * rows + low * width // wide
    outs = (half_rows, half_rows, half_rows, half_rows, shaped(nz, piece, wide))
    ins = (ma, mb, ea, eb, wgu, w_down, d1, d2, d3, d4, d5)
    down_mine, down_other, mine, other, u_mlp = moving_call(
        mlp_kernel,
        outs,
        scratch=vmem(*ins, *outs)
        + [pltpu.VMEM((2, tokens // 2, cut), BF), pltpu.VMEM((2, tokens // 2, wide), BF), pltpu.VMEM((cut, width), BF)],
        copies=len(ins) + 4 + nz,
    )((meta,), *ins)
    v_mlp = lay.gather_sum(u_mlp.reshape(nz * piece, wide))
    both = KV * rows + QW // nz * width // WIDE

    def backward(
        meta, seq_len, lengths, span_order, mine, other, down_mine, down_other, g_low, residual, inverse_m, att, wqkv, wout, qkv,
        xa, xb, cos_table, sin_table,
    ):
        got = send(other, lay.core)
        got, mine = fence(got, mine.astype(F32))
        r = halves((mine + got.astype(F32)).astype(BF))
        r = halves(plus(r[0], send(r[1], lay.second)))
        got = send(r[1], lay.first)
        got_down = send(down_other, lay.core)
        g_res2, h0 = kernel_call(
            norm_back_kernel, (shaped(own, width, dtype=F32), shaped(own, width))
        )((), g_low, residual, inverse_m, r[0], got)
        ga, gb = lay.plane_tokens(h0)
        d = halves(plus(down_mine, got_down))
        ga, gb, d = fence(ga, gb, d)
        got_down = send(d[1], lay.second)
        outs = [half_rows, half_rows] + [shaped(both, WIDE)] * nz
        ins = (ga, gb, att, wout, wqkv, qkv, flat(xa), flat(xb))
        mine, other, u0, u1, u2, u3 = moving_call(
            attention_back_kernel,
            outs,
            scratch=vmem(*ins, *outs)
            + [pltpu.VMEM((2, tokens // 2, WIDE), BF), pltpu.VMEM((length, width), BF)]
            + tables
            + [pltpu.VMEM((QW, width), BF)],
            copies=len(ins) + len(outs) + 16,
        )((meta, seq_len, span_order), *ins, cos_table, sin_table)
        got_down, mine, other, u0, u1, u2, u3 = fence(got_down, mine, other, u0, u1, u2, u3)
        d = halves(plus(d[0], got_down))
        return g_res2, mine, other, d[0], d[1], u3, u2, u1, u0

    g_res2, mine, other, da, db, u3, u2, u1, u0 = unit_of_work(
        go, backward, meta, seq_len, lengths, span_order, mine, other, down_mine, down_other, g_low, residual, inverse_m, att, wqkv,
        wout, qkv, xa, xb, cos_table, sin_table,
    )
    got = send(other, lay.core)
    got, mine = fence(got, mine)
    c5 = send(u3, lay.inward)
    r = halves(plus(mine, got))
    got = send(r[1], lay.second)
    v_gu = v_mlp[: KV * rows]
    c5, r, got, v_gu = fence(c5, r, got, v_gu)
    c4 = send(plus(u3, c5), lay.inner)
    c3 = send(u2, lay.inward)
    r = halves(plus(r[0], got))
    got = send(r[1], lay.first)
    got_down = send(db, lay.first)
    c4, c3, r, got, got_down = fence(c4, c3, r, got, got_down)
    c1, c2 = kernel_call(sums_kernel, (shaped(both, WIDE), shaped(both, WIDE)))((), u1, c4, u2, c3)
    c1 = send(c1, lay.pair)
    c2 = send(c2, lay.inner)
    v_gu = lay.exchange(v_gu.reshape(KV, rows, wide))
    grad_down = kernel_call(unpack_down_kernel, shaped(low, width, dtype=F32))((), v_mlp[KV * rows :])
    block_out = kernel_call(finish_kernel, shaped(own, width))(
        (meta, lengths, span_order), residual, da, got_down
    )
    grad_in = kernel_call(norm_back_low_kernel, shaped(own, width))(
        (), g_res2, hidden_in.reshape(own, width), inverse, r[0], got
    )
    c1, c2, v_gu, grad_down, block_out, grad_in = fence(c1, c2, v_gu, grad_down, block_out, grad_in)
    c0 = u0
    v_qkv, v_out = kernel_call(last_sum_kernel, (shaped(KV, rows, WIDE), shaped(*w_out.shape)))((), c0, c1, c2)
    v_qkv = lay.exchange(v_qkv)
    grad_out = send(v_out, lay.back)
    grad_gate, grad_up, total_m = kernel_call(
        unpack_mlp_kernel, (shaped(*w_gate.shape, dtype=F32), shaped(*w_up.shape, dtype=F32), shaped(1, rows, dtype=F32))
    )((), v_gu, w_gate, w_up, gain_m)
    grad_out, v_qkv, grad_gate, grad_up, total_m = fence(grad_out.astype(F32), v_qkv, grad_gate, grad_up, total_m)
    grad_query, grad_key, grad_value, total = kernel_call(
        unpack_attention_kernel,
        tuple(shaped(*w.shape, dtype=F32) for w in (w_query, w_key, w_value)) + (shaped(1, rows, dtype=F32),),
    )((), v_qkv, w_query, w_key, w_value, gain)
    return (
        block_out.reshape(hidden_in.shape), grad_in.reshape(hidden_in.shape), total[0], grad_query, grad_key, grad_value,
        grad_out, total_m[0], grad_gate, grad_up, grad_down,
    )


def anywhere(
    hidden_in, lengths, span_order, attn_gain, w_query, w_key, w_value, w_out,
    mlp_gain, w_gate, w_up, w_down, out_grad,
):
    lay = Layout()
    micro, slots, width = hidden_in.shape
    rows, nz = w_query.shape[0], lay.nz
    gain = attn_gain.astype(F32)[:, None]
    gain_m = mlp_gain.astype(F32)[:, None]
    pos = jnp.concatenate([positions_of(span_order, k, slots) for k in range(lay.ctx)])
    usable = (positions_of(span_order, lay.c, slots)[None, :] < lengths[:, None]).astype(F32)[..., None]
    cosines, sines = rope_tables(pos)
    length = slots * lay.ctx

    def tokens(x):
        return lax.all_gather(x, "ctx", axis=1, tiled=True).reshape(micro * length, width)

    def own(x):
        x = x.astype(BF).reshape(micro, length, width)
        return lax.psum_scatter(x, "ctx", scatter_dimension=1, tiled=True).astype(F32)

    spread, collect = lay.spread, lay.gather_sum
    wqkv = spread(lay.exchange(pack_attention(w_query, w_key, w_value, gain)).reshape(KV * rows, -1))
    wgu = spread(lay.exchange(pack_mlp(w_gate, w_up, gain_m, nz)).reshape(KV * rows, -1))
    wout = spread(send(w_out, lay.place))
    wdown = spread(w_down)
    source = hidden_in.astype(F32)
    unit, inverse = unit_rows(source)
    xs = tokens(unit.astype(BF))
    g_res = out_grad.astype(F32) * usable
    g_mlp = tokens(g_res.astype(BF))
    pre = mm(xs, wqkv).reshape(micro, length, -1)
    attended, kept = attend(pre, pos, lengths, cosines, sines)
    att = attended.reshape(micro * length, QW)
    residual = source + own(mm(att, wout))
    unit_m, inverse_m = unit_rows(residual)
    xm = tokens(unit_m.astype(BF))
    gate_up = mm(xm, wgu)
    hidden = swiglu(gate_up)
    block_out = (usable * (residual + own(mm(hidden, wdown)))).astype(BF)
    grad_down = collect(mm_lt(hidden, g_mlp)).astype(F32)
    g_gu = swiglu_back(gate_up, mm_rt(g_mlp, wdown))
    v_gu = lay.exchange(collect(mm_lt(xm, g_gu)).reshape(KV, rows, -1))
    u_gate, u_up = unpack_mlp(v_gu, nz)
    g_res2 = g_res + unit_back(own(mm_rt(g_gu, wgu)), unit_m, inverse_m)
    g_branch = tokens(g_res2.astype(BF))
    grad_out = send(collect(mm_lt(att, g_branch)), lay.back).astype(F32)
    g_att = mm_rt(g_branch, wout).astype(BF).reshape(micro, length, QW)
    g_pre = attend_back(g_att, kept, cosines, sines).reshape(micro * length, -1)
    v_qkv = lay.exchange(collect(mm_lt(xs, g_pre)).reshape(KV, rows, -1))
    u_q, u_k, u_v = unpack_attention(v_qkv)
    grad_in = (g_res2 + unit_back(own(mm_rt(g_pre, wqkv)), unit, inverse)).astype(BF)
    return (
        block_out, grad_in, paired((w_query, u_q), (w_key, u_k), (w_value, u_v)),
        u_q * gain, u_k * gain, u_v * gain, grad_out,
        paired((w_gate, u_gate), (w_up, u_up)), u_gate * gain_m, u_up * gain_m, grad_down,
    )


def solution(mesh):
    rows = P(AXES, None)
    tokens = P("fsdp", "ctx", None)
    line = mesh.shape["ctx"] == 4 and mesh.shape["fsdp"] == 8
    return jax.shard_map(
        on_line if line else anywhere,
        mesh=mesh,
        in_specs=(tokens, P("fsdp"), P(), P(AXES), rows, rows, rows, rows, P(AXES), rows, rows, rows, tokens),
        out_specs=(tokens, tokens, P(AXES), rows, rows, rows, rows, P(AXES), rows, rows, rows),
        check_vma=False,
    )
```

profile of v0, /device:TPU:1, one launch (start us, length us, event | category | flops | bytes accessed | tf_op | source)
XLA Modules:
  0.0 345.4 jit_solution(8052395537203514805)
XLA Ops:
  7.2 2.2 collective-permute-start.20
  10.1 2.0 shard_map.230
  12.0 4.7 %all-to-all-start.1 = ((bf16[8,48,384]{2,1,0:T(8,128)(2,1)}), bf16[8,48,384]{2,1,0:T(8,128)(2,1)S(1)}, u32[]{:S(2)}, u32[]{:S(2)}) async-start(bf16[8,48,384]{2,1,0:T(8,128)(2,1)} %shard_map.230), calls=%async_computation.1 | async-start | bytes 589824 | tf_op jit(solution)/shard_map/all_to_all | solution.py:73
  16.7 5.9 %collective-permute-start.26 = (bf16[48,1536]{1,0:T(8,128)(2,1)}, bf16[48,1536]{1,0:T(8,128)(2,1)}, u32[]{:S(2)}, u32[]{:S(2)}) collective-permute-start(bf16[48,1536]{1,0:T(8,128)(2,1)} %param.28), channel_id=1, source_target_pairs={{0,0},{1,8},{2,16},{3,24},{4,1},{5,9},{6,17},{7,25},{8,2},{9,10},{... | collective-permute-start | bytes 442376 | tf_op jit(solution)/shard_map/ppermute | solution.py:41
  24.0 1.5 shard_map.231
  25.6 1.9 shard_map.232
  28.9 1.4 collective-permute-start.24
  33.4 6.4 %collective-permute-done.23.h3 = bf16[128,1536]{1,0:T(8,128)(2,1)S(1)} collective-permute-done((bf16[128,1536]{1,0:T(8,128)(2,1)S(1)}, bf16[128,1536]{1,0:T(8,128)(2,1)S(1)}, u32[]{:S(2)}, u32[]{:S(2)}) %collective-permute-start.23) | collective-permute-done | bytes 393248 | tf_op jit(solution)/shard_map/ppermute | solution.py:41
  40.6 30.4 %conditional.3 = (bf16[2,2,128,1536]{3,2,1,0:T(8,128)(2,1)}, bf16[2,2,128,1536]{3,2,1,0:T(8,128)(2,1)}, bf16[8,48,1024]{2,1,0:T(8,128)(2,1)S(1)}, bf16[2,128,1536]{2,1,0:T(8,128)(2,1)S(1)}) conditional(s32[]{:T(128)} %bitcast.34, () %tuple.52, (bf16[128,1536]{1,0:T(8,128)(2,1)}, bf16[128,1536]{1,0:T(8,128)(2,1)}, bf16[8,48,1024]{2,1,0:T(8,128)(2,1)S(1)}, ...), branch_computations={%region_0.1_spmd, %region_1.2_spmd} | conditional | flops 1572864 | bytes 18874520 | solution.py:48
  41.9 20.1 %all_to_all.19 = bf16[8,48,1024]{2,1,0:T(8,128)(2,1)S(1)} all-to-all(bf16[8,48,1024]{2,1,0:T(8,128)(2,1)S(1)} %get-tuple-element.69), channel_id=1, replica_groups={{0,1,2,3,4,5,6,7},{8,9,10,11,12,13,14,15},{16,17,18,19,20,21,22,23},{24..., dimensions={0} | all-to-all | bytes 1572864 | tf_op jit(solution)/shard_map/cond/branch_1_fun/all_to_all | solution.py:73
  62.0 1.3 pad_maximum_fusion
  64.1 6.9 %collective-permute-done.2 = bf16[128,1536]{1,0:T(8,128)(2,1)S(1)} collective-permute-done((bf16[128,1536]{1,0:T(8,128)(2,1)S(1)}, bf16[128,1536]{1,0:T(8,128)(2,1)S(1)}, u32[]{:S(2)}, u32[]{:S(2)}) %collective-permute-start.2) | collective-permute-done | bytes 393248 | tf_op jit(solution)/shard_map/cond/branch_1_fun/ppermute | solution.py:41
  71.1 10.4 %all-gather.3.cloned.1.call-done = bf16[2304,384]{1,0:T(8,128)(2,1)} async-done(((bf16[576,384]{1,0:T(8,128)(2,1)}), bf16[2304,384]{1,0:T(8,128)(2,1)}) %all-gather.3.cloned.1.call-update) | async-done | bytes 1769488 | tf_op jit(solution)/shard_map/all_gather | solution.py:83
  81.7 76.3 %conditional.4 = (bf16[1536,384]{1,0:T(8,128)(2,1)}, bf16[4,256,384]{2,1,0:T(8,128)(2,1)S(1)}, bf16[2,512,192]{2,1,0:T(8,128)(2,1)S(1)}, bf16[192,1536]{1,0:T(8,...) conditional(s32[]{:T(128)} %bitcast.34, () %tuple.51, ...), branch_computations={%region_2.3_spmd, %region_3.4_spmd} | conditional | flops 3145728 | bytes 69206608 | solution.py:48
  82.9 8.2 %branch_1_fun.5 = (bf16[1536,384]{1,0:T(8,128)(2,1)}, bf16[4,256,384]{2,1,0:T(8,128)(2,1)S(1)}, bf16[2,512,192]{2,1,0:T(8,128)(2,1)S(1)}) custom-call(s32[6]{0:T(128)S(1)} %get-tuple-element.78.meta, s32[4]{0:T(128)S(1)} %get-tuple-element.79.lens, s32[8]{0:T(128)S(1)} %get-tuple-element.80.spans, bf16[512,1536]{1,0:T(8,128)(2,1)} %bitcast.6.xa, ...), custom_call_target="tpu_custom_call" | custom-call | tf_op jit(solution)/shard_map/cond/branch_1_fun/pallas_call | solution.py:306
  91.1 1.7 collective-permute-done.3
  92.8 2.7 branch_1_fun.6
  95.5 1.5 collective-permute-start.4
  97.1 1.3 pad_maximum_fusion.3
  98.4 1.9 collective-permute-done.4
  102.5 10.1 %collective-permute-done.5 = bf16[256,1536]{1,0:T(8,128)(2,1)S(1)} collective-permute-done((bf16[256,1536]{1,0:T(8,128)(2,1)S(1)}, bf16[256,1536]{1,0:T(8,128)(2,1)S(1)}, u32[]{:S(2)}, u32[]{:S(2)}) %collective-permute-start.5) | collective-permute-done | bytes 786464 | tf_op jit(solution)/shard_map/cond/branch_1_fun/ppermute | solution.py:41
  114.6 5.8 %collective-permute-done.7.b = bf16[128,1536]{1,0:T(8,128)(2,1)S(1)} collective-permute-done((bf16[128,1536]{1,0:T(8,128)(2,1)S(1)}, bf16[128,1536]{1,0:T(8,128)(2,1)S(1)}, u32[]{:S(2)}, u32[]{:S(2)}) %collective-permute-start.7) | collective-permute-done | bytes 393248 | tf_op jit(solution)/shard_map/cond/branch_1_fun/ppermute | solution.py:41
  121.2 2.1 branch_1_fun.7
  124.5 6.0 %collective-permute-done.8 = bf16[128,1536]{1,0:T(8,128)(2,1)S(1)} collective-permute-done((bf16[128,1536]{1,0:T(8,128)(2,1)}, bf16[128,1536]{1,0:T(8,128)(2,1)S(1)}, u32[]{:S(2)}, u32[]{:S(2)}) %collective-permute-start.8) | collective-permute-done | bytes 393248 | tf_op jit(solution)/shard_map/cond/branch_1_fun/ppermute | solution.py:41
  134.2 17.7 %collective-permute-done.10 = bf16[128,1536]{1,0:T(8,128)(2,1)} collective-permute-done((bf16[128,1536]{1,0:T(8,128)(2,1)}, bf16[128,1536]{1,0:T(8,128)(2,1)}, u32[]{:S(2)}, u32[]{:S(2)}) %collective-permute-start.10) | collective-permute-done | bytes 393248 | tf_op jit(solution)/shard_map/cond/branch_1_fun/ppermute | solution.py:41
  154.3 3.4 collective-permute-done.11
  157.9 29.1 %shard_map.233 = (bf16[512,1536]{1,0:T(8,128)(2,1)}, bf16[512,1536]{1,0:T(8,128)(2,1)}, bf16[512,1536]{1,0:T(8,128)(2,1)}, bf16[512,1536]{1,0:T(8,128)(2,1)}, bf16[4,576,1024]{2,1,0:T(8,128)(2,1)}) custom-call(s32[6]{0:T(128)S(1)} %stack.99.meta, bf16[512,1536]{1,0:T(8,128)(2,1)} %get-tuple-element.255.h_ma, bf16[512,1536]{1,0:T(8,128)(2,1)} %get-tuple-element.256.h_mb, ...), custom_call_target="tpu_custom_call" | custom-call | tf_op jit(solution)/shard_map/pallas_call | solution.py:322
  187.1 71.1 %conditional.5 = (f32[128,1536]{1,0:T(8,128)S(1)}, bf16[512,1536]{1,0:T(8,128)(2,1)S(1)}, bf16[512,1536]{1,0:T(8,128)(2,1)S(1)}, bf16[128,1536]{1,0:T(8,128)(2,1...) conditional(s32[]{:T(128)} %bitcast.34, () %tuple.50, ...), branch_computations={%region_4.5_spmd, %region_5.6_spmd} | conditional | flops 5898240 | bytes 107741904 | solution.py:48
  187.6 1.8 convert_element_type.14
  189.4 1.4 collective-permute-done.12
  192.6 10.1 %collective-permute-done.13 = bf16[256,1536]{1,0:T(8,128)(2,1)S(1)} collective-permute-done((bf16[256,1536]{1,0:T(8,128)(2,1)S(1)}, bf16[256,1536]{1,0:T(8,128)(2,1)S(1)}, u32[]{:S(2)}, u32[]{:S(2)}) %collective-permute-start.13) | collective-permute-done | bytes 786464 | tf_op jit(solution)/shard_map/cond/branch_1_fun/ppermute | solution.py:41
  204.8 5.8 %collective-permute-done.14.b = bf16[128,1536]{1,0:T(8,128)(2,1)S(1)} collective-permute-done((bf16[128,1536]{1,0:T(8,128)(2,1)S(1)}, bf16[128,1536]{1,0:T(8,128)(2,1)S(1)}, u32[]{:S(2)}, u32[]{:S(2)}) %collective-permute-start.14) | collective-permute-done | bytes 393248 | tf_op jit(solution)/shard_map/cond/branch_1_fun/ppermute | solution.py:41
  211.3 2.2 branch_1_fun.8
  214.7 6.0 %collective-permute-done.15 = bf16[128,1536]{1,0:T(8,128)(2,1)S(1)} collective-permute-done((bf16[128,1536]{1,0:T(8,128)(2,1)}, bf16[128,1536]{1,0:T(8,128)(2,1)S(1)}, u32[]{:S(2)}, u32[]{:S(2)}) %collective-permute-start.15) | collective-permute-done | bytes 393248 | tf_op jit(solution)/shard_map/cond/branch_1_fun/ppermute | solution.py:41
  223.1 2.9 collective-permute-start.18
  226.0 7.1 %collective-permute-done.16 = bf16[2,128,1536]{2,1,0:T(8,128)(2,1)S(1)} collective-permute-done((bf16[2,128,1536]{2,1,0:T(8,128)(2,1)S(1)}, bf16[2,128,1536]{2,1,0:T(8,128)(2,1)S(1)}, u32[]{:S(2)}, u32[]{:S(2)}) %collective-permute-start.16) | collective-permute-done | bytes 786464 | tf_op jit(solution)/shard_map/cond/branch_1_fun/ppermute | solution.py:41
  233.3 3.4 collective-permute-start.17
  237.2 2.6 collective-permute-done.17
  241.5 14.4 %branch_1_fun.9 = (bf16[512,1536]{1,0:T(8,128)(2,1)S(1)}, bf16[512,1536]{1,0:T(8,128)(2,1)}, bf16[576,384]{1,0:T(8,128)(2,1)}, bf16[576,384]{1,0:T(8,128)(2,1)},...) custom-call(s32[6]{0:T(128)S(1)} %get-tuple-element.123.meta, s32[4]{0:T(128)S(1)} %get-tuple-element.124.lens, ...), custom_call_target="tpu_custom_call" | custom-call | tf_op jit(solution)/shard_map/cond/branch_1_fun/pallas_call | solution.py:322
  255.9 1.3 bitcast_add_fusion.1
  258.7 3.0 collective-permute-done.28
  265.5 2.1 collective-permute-start.27
  267.5 2.1 collective-permute-start.31
  270.8 1.5 reduce-scatter.2.cloned.1.call-done
  272.4 2.1 slice.103
  274.4 4.1 %collective-permute-done.27 = bf16[576,384]{1,0:T(8,128)(2,1)} collective-permute-done((bf16[576,384]{1,0:T(8,128)(2,1)S(1)}, bf16[576,384]{1,0:T(8,128)(2,1)}, u32[]{:S(2)}, u32[]{:S(2)}) %collective-permute-start.27) | collective-permute-done | bytes 442400 | tf_op jit(solution)/shard_map/ppermute | solution.py:41
  278.5 1.9 add.31
  280.4 1.4 collective-permute-start.30
  283.8 1.7 collective-permute-start.32
  285.6 6.0 %all-to-all-start.2 = ((bf16[8,48,1024]{2,1,0:T(8,128)(2,1)}), bf16[8,48,1024]{2,1,0:T(8,128)(2,1)S(1)}, u32[]{:S(2)}, u32[]{:S(2)}) async-start(bf16[8,48,1024]{2,1,0:T(8,128)(2,1)} %bitcast.51), calls=%async_computation.3 | async-start | bytes 1572864 | tf_op jit(solution)/shard_map/all_to_all | solution.py:73
  291.5 1.8 slice.105.u
  293.3 2.0 shard_map.235
  295.3 2.3 shard_map.234
  297.6 4.2 %collective-permute-start.34 = (bf16[576,384]{1,0:T(8,128)(2,1)}, bf16[576,384]{1,0:T(8,128)(2,1)}, u32[]{:S(2)}, u32[]{:S(2)}) collective-permute-start(bf16[576,384]{1,0:T(8,128)(2,1)} %get-tuple-element.286), channel_id=1, source_target_pairs={{0,8},{1,9},{2,10},{3,11},{4,12},{5,13},{6,14},{7,15},{8,0},{9,1},... | collective-permute-start | bytes 1327112 | tf_op jit(solution)/shard_map/ppermute | solution.py:41
  301.8 1.4 collective-permute-start.35
  303.2 1.9 shard_map.236
  305.9 2.2 shard_map.237
  308.1 4.4 %collective-permute-done.34.b = bf16[576,384]{1,0:T(8,128)(2,1)} collective-permute-done((bf16[576,384]{1,0:T(8,128)(2,1)}, bf16[576,384]{1,0:T(8,128)(2,1)}, u32[]{:S(2)}, u32[]{:S(2)}) %collective-permute-start.34) | collective-permute-done | bytes 442400 | tf_op jit(solution)/shard_map/ppermute | solution.py:41
  312.5 2.0 shard_map.238
  314.5 4.6 %all-to-all-start.3 = ((bf16[8,48,384]{2,1,0:T(8,128)(2,1)}), bf16[8,48,384]{2,1,0:T(8,128)(2,1)S(1)}, u32[]{:S(2)}, u32[]{:S(2)}) async-start(bf16[8,48,384]{2,1,0:T(8,128)(2,1)} %get-tuple-element.301), calls=%async_computation.4 | async-start | bytes 589824 | tf_op jit(solution)/shard_map/all_to_all | solution.py:73
  319.1 3.5 %collective-permute-start.36 = (bf16[48,1536]{1,0:T(8,128)(2,1)}, bf16[48,1536]{1,0:T(8,128)(2,1)S(1)}, u32[]{:S(2)}, u32[]{:S(2)}) collective-permute-start(bf16[48,1536]{1,0:T(8,128)(2,1)} %get-tuple-element.300), channel_id=1, source_target_pairs={{0,0},{8,1},{16,2},{24,3},{1,4},{9,5},{17,6},{25,7},{2,8},{10,9},{... | collective-permute-start | bytes 442376 | tf_op jit(solution)/shard_map/ppermute | solution.py:41
  322.6 2.8 shard_map.239
  325.4 9.7 %collective-permute-done.36 = bf16[48,1536]{1,0:T(8,128)(2,1)S(1)} collective-permute-done((bf16[48,1536]{1,0:T(8,128)(2,1)}, bf16[48,1536]{1,0:T(8,128)(2,1)S(1)}, u32[]{:S(2)}, u32[]{:S(2)}) %collective-permute-start.36) | collective-permute-done | bytes 147488 | tf_op jit(solution)/shard_map/ppermute | solution.py:41
  336.6 2.1 shard_map.240
  (154 shorter events, 44.1 us)
Async XLA Ops:
  7.2 18.4 %copy-start.6 = (bf16[2,64,1536]{2,1,0:T(8,128)(2,1)S(1)}, bf16[2,64,1536]{2,1,0:T(8,128)(2,1)}, u32[]{:S(2)}) copy-start(bf16[2,64,1536]{2,1,0:T(8,128)(2,1)} %param.21) | copy-start | bytes 1179652
  7.2 18.4 %copy-start.33 = (s32[8]{0:T(128)S(1)}, s32[8]{0:T(128)}, u32[]{:S(2)}) copy-start(s32[8]{0:T(128)} %spans.3) | copy-start | bytes 100
  7.2 20.3 %collective-permute-start.20 = (bf16[128,1536]{1,0:T(8,128)(2,1)}, bf16[128,1536]{1,0:T(8,128)(2,1)S(1)}, u32[]{:S(2)}, u32[]{:S(2)}) collective-permute-start(bf16[128,1536]{1,0:T(8,128)(2,1)} %h0.1), channel_id=1, source_target_pairs={{0,8},{1,9},{2,10},{3,11},{4,12},{5,13},{6,14},{7,15},{8,0},{9,1},... | collective-permute-start | bytes 1179656 | tf_op jit(solution)/shard_map/ppermute | solution.py:41
  9.4 18.2 %collective-permute-start.21 = (bf16[128,1536]{1,0:T(8,128)(2,1)}, bf16[128,1536]{1,0:T(8,128)(2,1)S(1)}, u32[]{:S(2)}, u32[]{:S(2)}) collective-permute-start(bf16[128,1536]{1,0:T(8,128)(2,1)} %h0.1), channel_id=1, source_target_pairs={{8,16},{9,17},{10,18},{11,19},{12,20},{13,21},{14,22},{15,23},{16,... | collective-permute-start | bytes 1179656 | tf_op jit(solution)/shard_map/ppermute | solution.py:41
  12.0 15.5 %all-to-all-start.1 = ((bf16[8,48,384]{2,1,0:T(8,128)(2,1)}), bf16[8,48,384]{2,1,0:T(8,128)(2,1)S(1)}, u32[]{:S(2)}, u32[]{:S(2)}) async-start(bf16[8,48,384]{2,1,0:T(8,128)(2,1)} %shard_map.230), calls=%async_computation.1 | async-start | bytes 589824 | tf_op jit(solution)/shard_map/all_to_all | solution.py:73
  16.7 64.8 %all-gather.3.cloned.1.call-start = ((), (), s32[]{:S(2)}) async-start(), calls=%async_computation.5 | async-start | bytes 2211840 | tf_op jit(solution)/shard_map/all_gather | solution.py:83
  16.7 13.6 %collective-permute-start.26 = (bf16[48,1536]{1,0:T(8,128)(2,1)}, bf16[48,1536]{1,0:T(8,128)(2,1)}, u32[]{:S(2)}, u32[]{:S(2)}) collective-permute-start(bf16[48,1536]{1,0:T(8,128)(2,1)} %param.28), channel_id=1, source_target_pairs={{0,0},{1,8},{2,16},{3,24},{4,1},{5,9},{6,17},{7,25},{8,2},{9,10},{... | collective-permute-start | bytes 442376 | tf_op jit(solution)/shard_map/ppermute | solution.py:41
  22.7 4.9 %collective-permute-start.22 = (s32[2]{0:T(128)}, s32[2]{0:T(128)S(1)}, u32[]{:S(2)}, u32[]{:S(2)}) collective-permute-start(s32[2]{0:T(128)} %lens.3), channel_id=1, source_target_pairs={{0,4},{1,5},{2,6},{3,7},{4,0},{5,1},{6,2},{7,3},{8,12},{9,13},{10,... | collective-permute-start | bytes 32 | tf_op jit(solution)/shard_map/ppermute | solution.py:41
  24.0 16.0 %copy-start.34 = (s32[2]{0:T(128)S(1)}, s32[2]{0:T(128)}, u32[]{:S(2)}) copy-start(s32[2]{0:T(128)} %lens.3) | copy-start | bytes 28
  27.5 12.5 %copy-start.23 = (bf16[128,1536]{1,0:T(8,128)(2,1)}, bf16[128,1536]{1,0:T(8,128)(2,1)S(1)}, u32[]{:S(2)}) copy-start(bf16[128,1536]{1,0:T(8,128)(2,1)S(1)} %get-tuple-element.246) | copy-start | bytes 1179652
  27.5 12.5 %copy-start.28 = (bf16[128,1536]{1,0:T(8,128)(2,1)}, bf16[128,1536]{1,0:T(8,128)(2,1)S(1)}, u32[]{:S(2)}) copy-start(bf16[128,1536]{1,0:T(8,128)(2,1)S(1)} %collective-permute-done.20.h1) | copy-start | bytes 1179652
  27.6 12.5 %copy-start.29 = (bf16[128,1536]{1,0:T(8,128)(2,1)}, bf16[128,1536]{1,0:T(8,128)(2,1)S(1)}, u32[]{:S(2)}) copy-start(bf16[128,1536]{1,0:T(8,128)(2,1)S(1)} %collective-permute-done.21.h2) | copy-start | bytes 1179652
  27.6 12.3 %collective-permute-start.23 = (bf16[128,1536]{1,0:T(8,128)(2,1)S(1)}, bf16[128,1536]{1,0:T(8,128)(2,1)S(1)}, u32[]{:S(2)}, u32[]{:S(2)}) collective-permute-start(bf16[128,1536]{1,0:T(8,128)(2,1)S(1)} %collective-permute-done.21.h2), channel_id=1, source_target_pairs={{8,0},{9,1},{10,2},{11,3},{12,4},{13,5},{14,6},{15,7},{16,24},{17,... | collective-permute-start | bytes 1179656 | tf_op jit(solution)/shard_map/ppermute | solution.py:41
  28.9 11.0 %collective-permute-start.24 = (bf16[128,1536]{1,0:T(8,128)(2,1)S(1)}, bf16[128,1536]{1,0:T(8,128)(2,1)}, u32[]{:S(2)}, u32[]{:S(2)}) collective-permute-start(bf16[128,1536]{1,0:T(8,128)(2,1)S(1)} %collective-permute-done.20.h1), channel_id=1, source_target_pairs={{8,16},{9,17},{10,18},{11,19},{12,20},{13,21},{14,22},{15,23},{16,... | collective-permute-start | bytes 1179656 | tf_op jit(solution)/shard_map/ppermute | solution.py:41
  30.3 9.6 %collective-permute-start.25 = (bf16[128,1536]{1,0:T(8,128)(2,1)}, bf16[128,1536]{1,0:T(8,128)(2,1)}, u32[]{:S(2)}, u32[]{:S(2)}) collective-permute-start(bf16[128,1536]{1,0:T(8,128)(2,1)} %get-tuple-element.240), channel_id=1, source_target_pairs={{0,4},{1,3},{2,6},{3,1},{4,0},{5,7},{6,2},{7,5},{8,12},{9,11},{10,... | collective-permute-start | bytes 1179656 | tf_op jit(solution)/shard_map/ppermute | solution.py:41
  33.4 6.5 %copy-start.26 = (bf16[576,384]{1,0:T(8,128)(2,1)}, bf16[576,384]{1,0:T(8,128)(2,1)S(1)}, u32[]{:S(2)}) copy-start(bf16[576,384]{1,0:T(8,128)(2,1)S(1)} %slice_dynamic-update-slice_fusion) | copy-start | bytes 1327108
  39.9 118.0 %all-gather.5.cloned.1.call-start = ((), (), s32[]{:S(2)}) async-start(), calls=%async_computation.6 | async-start | bytes 3932160 | tf_op jit(solution)/shard_map/all_gather | solution.py:83
  41.8 20.1 %collective-permute-start = (bf16[2,128,1536]{2,1,0:T(8,128)(2,1)S(1)}, bf16[2,128,1536]{2,1,0:T(8,128)(2,1)S(1)}, u32[]{:S(2)}, u32[]{:S(2)}) collective-permute-start(bf16[2,128,1536]{2,1,0:T(8,128)(2,1)S(1)} %pad_maximum_fusion.1), channel_id=1, source_target_pairs={{0,2},{1,5},{2,0},{3,7},{4,6},{5,1},{6,4},{7,3},{8,10},{9,13},{10,... | collective-permute-start | bytes 2359304 | tf_op jit(solution)/shard_map/cond/branch_1_fun/ppermute | solution.py:41
  63.3 7.7 %collective-permute-start.1 = (bf16[2,2,128,1536]{3,2,1,0:T(8,128)(2,1)}, bf16[2,2,128,1536]{3,2,1,0:T(8,128)(2,1)}, u32[]{:S(2)}, u32[]{:S(2)}) collective-permute-start(bf16[2,2,128,1536]{3,2,1,0:T(8,128)(2,1)} %pad_maximum_fusion), channel_id=1, source_target_pairs={{0,1},{1,0},{2,3},{3,2},{4,5},{5,4},{6,7},{7,6},{8,9},{9,8},{10,11... | collective-permute-start | bytes 4718600 | tf_op jit(solution)/shard_map/cond/branch_1_fun/ppermute | solution.py:41
  63.9 7.0 %collective-permute-start.2 = (bf16[128,1536]{1,0:T(8,128)(2,1)S(1)}, bf16[128,1536]{1,0:T(8,128)(2,1)S(1)}, u32[]{:S(2)}, u32[]{:S(2)}) collective-permute-start(bf16[128,1536]{1,0:T(8,128)(2,1)S(1)} %get-tuple-element.73), channel_id=1, source_target_pairs={{0,4},{1,3},{2,6},{3,1},{4,0},{5,7},{6,2},{7,5},{8,12},{9,11},{10,... | collective-permute-start | bytes 1179656 | tf_op jit(solution)/shard_map/cond/branch_1_fun/ppermute | solution.py:41
  71.1 10.5 %copy-start.8 = (bf16[8,48,1024]{2,1,0:T(8,128)(2,1)}, bf16[8,48,1024]{2,1,0:T(8,128)(2,1)S(1)}, u32[]{:S(2)}) copy-start(bf16[8,48,1024]{2,1,0:T(8,128)(2,1)S(1)} %get-tuple-element.259) | copy-start | bytes 2359300
  81.5 190.8 %reduce-scatter.2.cloned.1.call-start = ((), (), s32[]{:S(2)}) async-start(), calls=%async_computation.7 | async-start | bytes 5898240 | tf_op jit(solution)/shard_map/reduce_scatter | solution.py:89
  81.7 11.2 %collective-permute-start.3 = (bf16[2,128,1536]{2,1,0:T(8,128)(2,1)S(1)}, bf16[2,128,1536]{2,1,0:T(8,128)(2,1)S(1)}, u32[]{:S(2)}, u32[]{:S(2)}) collective-permute-start(bf16[2,128,1536]{2,1,0:T(8,128)(2,1)S(1)} %get-tuple-element.89), channel_id=1, source_target_pairs={{0,2},{1,5},{2,0},{3,7},{4,6},{5,1},{6,4},{7,3},{8,10},{9,13},{10,... | collective-permute-start | bytes 2359304 | tf_op jit(solution)/shard_map/cond/branch_1_fun/ppermute | solution.py:41
  82.9 9.9 %copy-start = (bf16[2304,384]{1,0:T(8,128)(2,1)S(1)}, bf16[2304,384]{1,0:T(8,128)(2,1)}, u32[]{:S(2)}) copy-start(bf16[2304,384]{1,0:T(8,128)(2,1)} %get-tuple-element.83) | copy-start | bytes 5308420 | tf_op jit(solution)/shard_map/cond
  91.1 7.3 %copy-start.4 = (bf16[2,512,192]{2,1,0:T(8,128)(2,1)}, bf16[2,512,192]{2,1,0:T(8,128)(2,1)S(1)}, u32[]{:S(2)}) copy-start(bf16[2,512,192]{2,1,0:T(8,128)(2,1)S(1)} %get-tuple-element.345.att) | copy-start | bytes 1179652 | tf_op jit(solution)/shard_map/cond
  95.5 4.8 %collective-permute-start.4 = (bf16[512,1536]{1,0:T(8,128)(2,1)}, bf16[512,1536]{1,0:T(8,128)(2,1)S(1)}, u32[]{:S(2)}, u32[]{:S(2)}) collective-permute-start(bf16[512,1536]{1,0:T(8,128)(2,1)} %get-tuple-element.96), channel_id=1, source_target_pairs={{0,1},{1,0},{2,3},{3,2},{4,5},{5,4},{6,7},{7,6},{8,9},{9,8},{10,11... | collective-permute-start | bytes 4718600 | tf_op jit(solution)/shard_map/cond/branch_1_fun/ppermute | solution.py:41
  100.7 11.8 %collective-permute-start.6 = (bf16[2,2,128,1536]{3,2,1,0:T(8,128)(2,1)}, bf16[2,2,128,1536]{3,2,1,0:T(8,128)(2,1)}, u32[]{:S(2)}, u32[]{:S(2)}) collective-permute-start(bf16[2,2,128,1536]{3,2,1,0:T(8,128)(2,1)} %pad_maximum_fusion.3), channel_id=1, source_target_pairs={{0,1},{1,0},{2,3},{3,2},{4,5},{5,4},{6,7},{7,6},{8,9},{9,8},{10,11... | collective-permute-start | bytes 4718600 | tf_op jit(solution)/shard_map/cond/branch_1_fun/ppermute | solution.py:41
  101.2 11.3 %collective-permute-start.5 = (bf16[256,1536]{1,0:T(8,128)(2,1)S(1)}, bf16[256,1536]{1,0:T(8,128)(2,1)S(1)}, u32[]{:S(2)}, u32[]{:S(2)}) collective-permute-start(bf16[256,1536]{1,0:T(8,128)(2,1)S(1)} %slice_bitcast_fusion), channel_id=1, source_target_pairs={{0,2},{1,5},{2,0},{3,7},{4,6},{5,1},{6,4},{7,3},{8,10},{9,13},{10,... | collective-permute-start | bytes 2359304 | tf_op jit(solution)/shard_map/cond/branch_1_fun/ppermute | solution.py:41
  113.4 7.0 %collective-permute-start.7 = (bf16[128,1536]{1,0:T(8,128)(2,1)S(1)}, bf16[128,1536]{1,0:T(8,128)(2,1)S(1)}, u32[]{:S(2)}, u32[]{:S(2)}) collective-permute-start(bf16[128,1536]{1,0:T(8,128)(2,1)S(1)} %get-tuple-element.316), channel_id=1, source_target_pairs={{0,4},{1,3},{2,6},{3,1},{4,0},{5,7},{6,2},{7,5},{8,12},{9,11},{10,... | collective-permute-start | bytes 1179656 | tf_op jit(solution)/shard_map/cond/branch_1_fun/ppermute | solution.py:41
  123.3 7.2 %collective-permute-start.8 = (bf16[128,1536]{1,0:T(8,128)(2,1)}, bf16[128,1536]{1,0:T(8,128)(2,1)S(1)}, u32[]{:S(2)}, u32[]{:S(2)}) collective-permute-start(bf16[128,1536]{1,0:T(8,128)(2,1)} %get-tuple-element.104), channel_id=1, source_target_pairs={{0,4},{1,3},{2,6},{3,1},{4,0},{5,7},{6,2},{7,5},{8,12},{9,11},{10,... | collective-permute-start | bytes 1179656 | tf_op jit(solution)/shard_map/cond/branch_1_fun/ppermute | solution.py:41
  131.7 20.2 %collective-permute-start.9 = (bf16[2,128,1536]{2,1,0:T(8,128)(2,1)S(1)}, bf16[2,128,1536]{2,1,0:T(8,128)(2,1)S(1)}, u32[]{:S(2)}, u32[]{:S(2)}) collective-permute-start(bf16[2,128,1536]{2,1,0:T(8,128)(2,1)S(1)} %pad_maximum_fusion.5), channel_id=1, source_target_pairs={{0,2},{1,5},{2,0},{3,7},{4,6},{5,1},{6,4},{7,3},{8,10},{9,13},{10,... | collective-permute-start | bytes 2359304 | tf_op jit(solution)/shard_map/cond/branch_1_fun/ppermute | solution.py:41
  132.9 19.0 %collective-permute-start.10 = (bf16[128,1536]{1,0:T(8,128)(2,1)}, bf16[128,1536]{1,0:T(8,128)(2,1)}, u32[]{:S(2)}, u32[]{:S(2)}) collective-permute-start(bf16[128,1536]{1,0:T(8,128)(2,1)} %get-tuple-element.107), channel_id=1, source_target_pairs={{8,0},{9,1},{10,2},{11,3},{12,4},{13,5},{14,6},{15,7},{16,24},{17,... | collective-permute-start | bytes 1179656 | tf_op jit(solution)/shard_map/cond/branch_1_fun/ppermute | solution.py:41
  151.9 5.8 %copy-start.5 = (bf16[2,512,192]{2,1,0:T(8,128)(2,1)S(1)}, bf16[2,512,192]{2,1,0:T(8,128)(2,1)}, u32[]{:S(2)}) copy-start(bf16[2,512,192]{2,1,0:T(8,128)(2,1)} %copy-done.4) | copy-start | bytes 1179652 | tf_op jit(solution)/shard_map/cond
  153.2 4.5 %collective-permute-start.11 = (bf16[2,2,128,1536]{3,2,1,0:T(8,128)(2,1)}, bf16[2,2,128,1536]{3,2,1,0:T(8,128)(2,1)}, u32[]{:S(2)}, u32[]{:S(2)}) collective-permute-start(bf16[2,2,128,1536]{3,2,1,0:T(8,128)(2,1)} %pad_maximum_fusion.4), channel_id=1, source_target_pairs={{0,1},{1,0},{2,3},{3,2},{4,5},{5,4},{6,7},{7,6},{8,9},{9,8},{10,11... | collective-permute-start | bytes 4718600 | tf_op jit(solution)/shard_map/cond/branch_1_fun/ppermute | solution.py:41
  187.1 3.7 %collective-permute-start.12 = (bf16[512,1536]{1,0:T(8,128)(2,1)}, bf16[512,1536]{1,0:T(8,128)(2,1)S(1)}, u32[]{:S(2)}, u32[]{:S(2)}) collective-permute-start(bf16[512,1536]{1,0:T(8,128)(2,1)} %get-tuple-element.114), channel_id=1, source_target_pairs={{0,1},{1,0},{2,3},{3,2},{4,5},{5,4},{6,7},{7,6},{8,9},{9,8},{10,11... | collective-permute-start | bytes 4718600 | tf_op jit(solution)/shard_map/cond/branch_1_fun/ppermute | solution.py:41
  191.4 20.0 %copy-start.24 = (bf16[128,1536]{1,0:T(8,128)(2,1)S(1)}, bf16[128,1536]{1,0:T(8,128)(2,1)}, u32[]{:S(2)}) copy-start(bf16[128,1536]{1,0:T(8,128)(2,1)} %get-tuple-element.111.g_res) | copy-start | bytes 1179652 | tf_op jit(solution)/shard_map/cond
  191.4 11.3 %collective-permute-start.13 = (bf16[256,1536]{1,0:T(8,128)(2,1)S(1)}, bf16[256,1536]{1,0:T(8,128)(2,1)S(1)}, u32[]{:S(2)}, u32[]{:S(2)}) collective-permute-start(bf16[256,1536]{1,0:T(8,128)(2,1)S(1)} %slice.93), channel_id=1, source_target_pairs={{0,2},{1,5},{2,0},{3,7},{4,6},{5,1},{6,4},{7,3},{8,10},{9,13},{10,... | collective-permute-start | bytes 2359304 | tf_op jit(solution)/shard_map/cond/branch_1_fun/ppermute | solution.py:41
  203.6 7.0 %collective-permute-start.14 = (bf16[128,1536]{1,0:T(8,128)(2,1)S(1)}, bf16[128,1536]{1,0:T(8,128)(2,1)S(1)}, u32[]{:S(2)}, u32[]{:S(2)}) collective-permute-start(bf16[128,1536]{1,0:T(8,128)(2,1)S(1)} %get-tuple-element.322), channel_id=1, source_target_pairs={{0,4},{1,3},{2,6},{3,1},{4,0},{5,7},{6,2},{7,5},{8,12},{9,11},{10,... | collective-permute-start | bytes 1179656 | tf_op jit(solution)/shard_map/cond/branch_1_fun/ppermute | solution.py:41
  213.5 9.6 %copy-start.35 = (bf16[512,1536]{1,0:T(8,128)(2,1)S(1)}, bf16[512,1536]{1,0:T(8,128)(2,1)}, u32[]{:S(2)}) copy-start(bf16[512,1536]{1,0:T(8,128)(2,1)} %get-tuple-element.121) | copy-start | bytes 4718596 | tf_op jit(solution)/shard_map/cond
  213.5 7.2 %collective-permute-start.15 = (bf16[128,1536]{1,0:T(8,128)(2,1)}, bf16[128,1536]{1,0:T(8,128)(2,1)S(1)}, u32[]{:S(2)}, u32[]{:S(2)}) collective-permute-start(bf16[128,1536]{1,0:T(8,128)(2,1)} %get-tuple-element.119), channel_id=1, source_target_pairs={{0,4},{1,3},{2,6},{3,1},{4,0},{5,7},{6,2},{7,5},{8,12},{9,11},{10,... | collective-permute-start | bytes 1179656 | tf_op jit(solution)/shard_map/cond/branch_1_fun/ppermute | solution.py:41
  221.9 11.3 %collective-permute-start.16 = (bf16[2,128,1536]{2,1,0:T(8,128)(2,1)S(1)}, bf16[2,128,1536]{2,1,0:T(8,128)(2,1)S(1)}, u32[]{:S(2)}, u32[]{:S(2)}) collective-permute-start(bf16[2,128,1536]{2,1,0:T(8,128)(2,1)S(1)} %get-tuple-element.321), channel_id=1, source_target_pairs={{0,2},{1,5},{2,0},{3,7},{4,6},{5,1},{6,4},{7,3},{8,10},{9,13},{10,... | collective-permute-start | bytes 2359304 | tf_op jit(solution)/shard_map/cond/branch_1_fun/ppermute | solution.py:41
  223.1 13.6 %collective-permute-start.18 = (bf16[512,1536]{1,0:T(8,128)(2,1)S(1)}, bf16[512,1536]{1,0:T(8,128)(2,1)S(1)}, u32[]{:S(2)}, u32[]{:S(2)}) collective-permute-start(bf16[512,1536]{1,0:T(8,128)(2,1)S(1)} %copy-done.35), channel_id=1, source_target_pairs={{0,1},{1,0},{2,3},{3,2},{4,5},{5,4},{6,7},{7,6},{8,9},{9,8},{10,11... | collective-permute-start | bytes 4718600 | tf_op jit(solution)/shard_map/cond/branch_1_fun/ppermute | solution.py:41
  233.3 6.5 %collective-permute-start.17 = (bf16[2,2,128,1536]{3,2,1,0:T(8,128)(2,1)S(1)}, bf16[2,2,128,1536]{3,2,1,0:T(8,128)(2,1)S(1)}, u32[]{:S(2)}, u32[]{:S(2)}) collective-permute-start(bf16[2,2,128,1536]{3,2,1,0:T(8,128)(2,1)S(1)} %pad_maximum_fusion.6), channel_id=1, source_target_pairs={{0,1},{1,0},{2,3},{3,2},{4,5},{5,4},{6,7},{7,6},{8,9},{9,8},{10,11... | collective-permute-start | bytes 4718600 | tf_op jit(solution)/shard_map/cond/branch_1_fun/ppermute | solution.py:41
  237.2 4.0 %copy-start.12 = (bf16[4,256,384]{2,1,0:T(8,128)(2,1)S(1)}, bf16[4,256,384]{2,1,0:T(8,128)(2,1)}, u32[]{:S(2)}) copy-start(bf16[4,256,384]{2,1,0:T(8,128)(2,1)} %copy-done.11) | copy-start | bytes 2359300 | tf_op jit(solution)/shard_map/cond
  239.9 16.0 %collective-permute-start.19 = (bf16[256,1536]{1,0:T(8,128)(2,1)S(1)}, bf16[256,1536]{1,0:T(8,128)(2,1)}, u32[]{:S(2)}, u32[]{:S(2)}) collective-permute-start(bf16[256,1536]{1,0:T(8,128)(2,1)S(1)} %slice_bitcast_fusion.1), channel_id=1, source_target_pairs={{0,2},{1,5},{2,0},{3,7},{4,6},{5,1},{6,4},{7,3},{8,10},{9,13},{10,... | collective-permute-start | bytes 2359304 | tf_op jit(solution)/shard_map/cond/branch_1_fun/ppermute | solution.py:41
  258.3 3.9 %copy-start.9 = (f32[128,1536]{1,0:T(8,128)}, f32[128,1536]{1,0:T(8,128)S(1)}, u32[]{:S(2)}) copy-start(f32[128,1536]{1,0:T(8,128)S(1)} %get-tuple-element.291.g_res) | copy-start | bytes 2359300
  258.3 3.5 %collective-permute-start.28 = (bf16[512,1536]{1,0:T(8,128)(2,1)S(1)}, bf16[512,1536]{1,0:T(8,128)(2,1)S(1)}, u32[]{:S(2)}, u32[]{:S(2)}) collective-permute-start(bf16[512,1536]{1,0:T(8,128)(2,1)S(1)} %get-tuple-element.274), channel_id=1, source_target_pairs={{0,1},{1,0},{2,3},{3,2},{4,5},{5,4},{6,7},{7,6},{8,9},{9,8},{10,11... | collective-permute-start | bytes 4718600 | tf_op jit(solution)/shard_map/ppermute | solution.py:41
  264.3 17.6 %copy-start.2 = (bf16[512,1536]{1,0:T(8,128)(2,1)S(1)}, bf16[512,1536]{1,0:T(8,128)(2,1)}, u32[]{:S(2)}) copy-start(bf16[512,1536]{1,0:T(8,128)(2,1)} %copy-done.1) | copy-start | bytes 4718596
  264.3 14.2 %collective-permute-start.29 = (bf16[256,1536]{1,0:T(8,128)(2,1)}, bf16[256,1536]{1,0:T(8,128)(2,1)}, u32[]{:S(2)}, u32[]{:S(2)}) collective-permute-start(bf16[256,1536]{1,0:T(8,128)(2,1)} %slice.102), channel_id=1, source_target_pairs={{0,2},{1,5},{2,0},{3,7},{4,6},{5,1},{6,4},{7,3},{8,10},{9,13},{10,... | collective-permute-start | bytes 2359304 | tf_op jit(solution)/shard_map/ppermute | solution.py:41
  265.5 13.1 %collective-permute-start.27 = (bf16[576,384]{1,0:T(8,128)(2,1)S(1)}, bf16[576,384]{1,0:T(8,128)(2,1)}, u32[]{:S(2)}, u32[]{:S(2)}) collective-permute-start(bf16[576,384]{1,0:T(8,128)(2,1)S(1)} %copy-done.14), channel_id=1, source_target_pairs={{0,8},{1,9},{2,10},{3,11},{4,12},{5,13},{6,14},{7,15},{24,16},{25,... | collective-permute-start | bytes 1327112 | tf_op jit(solution)/shard_map/ppermute | solution.py:41
  267.5 27.8 %collective-permute-start.31 = (bf16[576,384]{1,0:T(8,128)(2,1)}, bf16[576,384]{1,0:T(8,128)(2,1)}, u32[]{:S(2)}, u32[]{:S(2)}) collective-permute-start(bf16[576,384]{1,0:T(8,128)(2,1)} %get-tuple-element.280.c), channel_id=1, source_target_pairs={{0,8},{1,9},{2,10},{3,11},{4,12},{5,13},{6,14},{7,15},{24,16},{25,... | collective-permute-start | bytes 1327112 | tf_op jit(solution)/shard_map/ppermute | solution.py:41
  269.6 25.6 %collective-permute-start.33 = (bf16[128,1536]{1,0:T(8,128)(2,1)}, bf16[128,1536]{1,0:T(8,128)(2,1)}, u32[]{:S(2)}, u32[]{:S(2)}) collective-permute-start(bf16[128,1536]{1,0:T(8,128)(2,1)} %get-tuple-element.283), channel_id=1, source_target_pairs={{0,4},{1,3},{2,6},{3,1},{4,0},{5,7},{6,2},{7,5},{8,12},{9,11},{10,... | collective-permute-start | bytes 1179656 | tf_op jit(solution)/shard_map/ppermute | solution.py:41
  280.4 14.9 %collective-permute-start.30 = (bf16[576,384]{1,0:T(8,128)(2,1)}, bf16[576,384]{1,0:T(8,128)(2,1)}, u32[]{:S(2)}, u32[]{:S(2)}) collective-permute-start(bf16[576,384]{1,0:T(8,128)(2,1)} %add.31), channel_id=1, source_target_pairs={{8,16},{9,17},{10,18},{11,19},{12,20},{13,21},{14,22},{15,23},{16,... | collective-permute-start | bytes 1327112 | tf_op jit(solution)/shard_map/ppermute | solution.py:41
  283.8 11.5 %collective-permute-start.32 = (bf16[128,1536]{1,0:T(8,128)(2,1)}, bf16[128,1536]{1,0:T(8,128)(2,1)}, u32[]{:S(2)}, u32[]{:S(2)}) collective-permute-start(bf16[128,1536]{1,0:T(8,128)(2,1)} %slice.104), channel_id=1, source_target_pairs={{0,4},{1,3},{2,6},{3,1},{4,0},{5,7},{6,2},{7,5},{8,12},{9,11},{10,... | collective-permute-start | bytes 1179656 | tf_op jit(solution)/shard_map/ppermute | solution.py:41
  285.6 9.8 %copy-start.13 = (bf16[576,384]{1,0:T(8,128)(2,1)S(1)}, bf16[576,384]{1,0:T(8,128)(2,1)}, u32[]{:S(2)}) copy-start(bf16[576,384]{1,0:T(8,128)(2,1)} %get-tuple-element.272.a) | copy-start | bytes 1327108
  285.6 22.6 %all-to-all-start.2 = ((bf16[8,48,1024]{2,1,0:T(8,128)(2,1)}), bf16[8,48,1024]{2,1,0:T(8,128)(2,1)S(1)}, u32[]{:S(2)}, u32[]{:S(2)}) async-start(bf16[8,48,1024]{2,1,0:T(8,128)(2,1)} %bitcast.51), calls=%async_computation.3 | async-start | bytes 1572864 | tf_op jit(solution)/shard_map/all_to_all | solution.py:73
  293.3 9.9 %copy-start.22 = (bf16[128,1536]{1,0:T(8,128)(2,1)S(1)}, bf16[128,1536]{1,0:T(8,128)(2,1)}, u32[]{:S(2)}) copy-start(bf16[128,1536]{1,0:T(8,128)(2,1)} %copy-done.21) | copy-start | bytes 1179652
  297.6 8.3 %copy-start.10 = (f32[128,1536]{1,0:T(8,128)S(1)}, f32[128,1536]{1,0:T(8,128)}, u32[]{:S(2)}) copy-start(f32[128,1536]{1,0:T(8,128)} %copy-done.9) | copy-start | bytes 2359300
  297.6 14.9 %collective-permute-start.34 = (bf16[576,384]{1,0:T(8,128)(2,1)}, bf16[576,384]{1,0:T(8,128)(2,1)}, u32[]{:S(2)}, u32[]{:S(2)}) collective-permute-start(bf16[576,384]{1,0:T(8,128)(2,1)} %get-tuple-element.286), channel_id=1, source_target_pairs={{0,8},{1,9},{2,10},{3,11},{4,12},{5,13},{6,14},{7,15},{8,0},{9,1},... | collective-permute-start | bytes 1327112 | tf_op jit(solution)/shard_map/ppermute | solution.py:41
  301.8 10.7 %collective-permute-start.35 = (bf16[576,384]{1,0:T(8,128)(2,1)}, bf16[576,384]{1,0:T(8,128)(2,1)}, u32[]{:S(2)}, u32[]{:S(2)}) collective-permute-start(bf16[576,384]{1,0:T(8,128)(2,1)} %get-tuple-element.287), channel_id=1, source_target_pairs={{8,16},{9,17},{10,18},{11,19},{12,20},{13,21},{14,22},{15,23},{16,... | collective-permute-start | bytes 1327112 | tf_op jit(solution)/shard_map/ppermute | solution.py:41
  305.1 7.4 %copy-start.15 = (bf16[576,384]{1,0:T(8,128)(2,1)S(1)}, bf16[576,384]{1,0:T(8,128)(2,1)}, u32[]{:S(2)}) copy-start(bf16[576,384]{1,0:T(8,128)(2,1)} %get-tuple-element.297.a) | copy-start | bytes 1327108
  308.1 14.5 %copy-start.7 = (bf16[8,48,1024]{2,1,0:T(8,128)(2,1)}, bf16[8,48,1024]{2,1,0:T(8,128)(2,1)S(1)}, u32[]{:S(2)}) copy-start(bf16[8,48,1024]{2,1,0:T(8,128)(2,1)S(1)} %all-to-all-done.2.u) | copy-start | bytes 2359300
  314.5 21.3 %all-to-all-start.3 = ((bf16[8,48,384]{2,1,0:T(8,128)(2,1)}), bf16[8,48,384]{2,1,0:T(8,128)(2,1)S(1)}, u32[]{:S(2)}, u32[]{:S(2)}) async-start(bf16[8,48,384]{2,1,0:T(8,128)(2,1)} %get-tuple-element.301), calls=%async_computation.4 | async-start | bytes 589824 | tf_op jit(solution)/shard_map/all_to_all | solution.py:73
  319.1 16.0 %collective-permute-start.36 = (bf16[48,1536]{1,0:T(8,128)(2,1)}, bf16[48,1536]{1,0:T(8,128)(2,1)S(1)}, u32[]{:S(2)}, u32[]{:S(2)}) collective-permute-start(bf16[48,1536]{1,0:T(8,128)(2,1)} %get-tuple-element.300), channel_id=1, source_target_pairs={{0,0},{8,1},{16,2},{24,3},{1,4},{9,5},{17,6},{25,7},{2,8},{10,9},{... | collective-permute-start | bytes 442376 | tf_op jit(solution)/shard_map/ppermute | solution.py:41
  (15 other events, 29.6 us)
Sparse Core Ops, SparseCore 0:
  40.1 41.4 all-gather.2
  83.6 62.3 all-gather.4
  187.2 85.0 reduce-scatter.1
where the time goes:
time: 351 us; the launch traced here: 345 us
  waiting for transfers between devices  126 us (36%)
  Pallas kernels  79.5 us (23%)
  starting transfers between devices  71.7 us (20%)
  blocking collectives  20.1 us (6%)
  local copies, waits for them, and re-layouts  16.5 us (5%)
  other arithmetic  16.3 us (5%)
  between operations  14.3 us (4%)
    ppermute x37, waiting for transfers between devices, send(): return lax.ppermute(x, AXES, pairs)  114 us
    ppermute x37, starting transfers between devices, send(): return lax.ppermute(x, AXES, pairs)  56.4 us
    pallas_call x2, Pallas kernels, call(): pl.pallas_call(body, out_shape=outs, in_specs=[SMEM] * len(scalars) + [pl...  43.6 us
    pallas_call x14, Pallas kernels, call(): pl.pallas_call(body, out_shape=outs, in_specs=[SMEM] * len(scalars) + [VM...  35.9 us
    all_to_all x1, blocking collectives, exchange(): lax.all_to_all(x, AXES, split_axis=0, concat_axis=0, tiled=True, axis_ind...  20.1 us
    all_to_all x3, starting transfers between devices, exchange(): lax.all_to_all(x, AXES, split_axis=0, concat_axis=0, tiled=True, axis_ind...  15.2 us
    all_gather x2, waiting for transfers between devices, spread(): lax.all_gather(x, AXES, axis=0, tiled=True, axis_index_groups=self.lines())  10.5 us
  transfers between devices with their start and end apart: 43, of which 21 were waited for; matrix products, arithmetic and copies ran while one was open for 8% of the time, Pallas kernels for 13%

commit v1 on v0

--- a/solution.py
+++ b/solution.py
@@ -640,61 +640,81 @@
     meta,
     h_ma, h_mb, h_ea, h_eb, h_wgu, h0, h1, h2, h3, h4, h5,
     o_down_mine, o_down_theirs, o_mine, o_theirs, o_u,
-    ma, mb, ea, eb, wgu, d0, d1, d2, d3, d4, d5, down_mine, down_theirs, mine, theirs, u, hidden, g_gu, wdown, sems,
+    x, g, back, down, wgu, d0, d1, d2, d3, d4, d5, u, hidden, g_gu, wdown, sems,
 ):
     copies = Copies(sems)
-    came = [copies.start(h_wgu, wgu), copies.start(h_mb, mb)]
+    came = [copies.start(h_wgu, wgu), copies.start(h_mb, x.at[1])]
     pieces = (d0, d1, d2, d3, d4, d5)
-    downs = [copies.start(h, d) for h, d in zip((h0, h1, h2, h3, h4, h5), pieces)]
-    came_eb = copies.start(h_eb, eb)
-    came_ma = copies.start(h_ma, ma)
-    came_ea = copies.start(h_ea, ea)
-    gone = []
+    came += [copies.start(h, d) for h, d in zip((h0, h1, h2, h3, h4, h5), pieces)]
+    came += [copies.start(h_eb, g.at[1])]
+    later = [copies.start(h_ma, x.at[0]), copies.start(h_ea, g.at[0])]
     half = wgu.shape[1] // 2
     for c in came:
         c.wait()
-    for part, x, g, down, back, o_down, o_back in (
-        (1, mb, eb, down_theirs, theirs, o_down_theirs, o_theirs),
-        (0, ma, ea, down_mine, mine, o_down_mine, o_mine),
-    ):
-        if part == 0:
-            came_ma.wait()
-        gate_up = dot(x[...], wgu[...])
+    assemble(meta, pieces, wdown)
+    out_copies = [
+        pltpu.make_async_copy(v, o, sems.at[copies.used + k])
+        for k, (v, o) in enumerate(
+            ((back.at[1], o_theirs), (down.at[1], o_down_theirs), (back.at[0], o_mine), (down.at[0], o_down_mine))
+        )
+    ]
+    copies.used += 4
+
+    def one(i, carry):
+        part = 1 - i
+
+        @pl.when(i == 1)
+        def _():
+            for c in later:
+                c.wait()
+
+        gate_up = dot(x[part], wgu[...])
         gate, up = gate_up[:, :half], gate_up[:, half:]
         sig = 1.0 / (1.0 + jnp.exp(-gate))
         act = gate * sig
-        hid = (act * up).astype(BF)
-        hidden[part] = hid
-        if part == 1:
-            for c in downs:
-                c.wait()
-            assemble(meta, pieces, wdown)
-            came_eb.wait()
-        else:
-            came_ea.wait()
-        g_hidden = dot(g[...], wdown[...], RIGHT_T)
+        hidden[part] = (act * up).astype(BF)
+        g_hidden = dot(g[part], wdown[...], RIGHT_T)
         g_gu[part, :, :half] = (g_hidden * up * sig * (1.0 + gate * (1.0 - sig))).astype(BF)
         g_gu[part, :, half:] = (g_hidden * act).astype(BF)
-        back[...] = dot(g_gu[part], wgu[...], RIGHT_T).astype(BF)
-        gone.append(copies.start(back, o_back))
-        down[...] = dot(hid, wdown[...]).astype(BF)
-        gone.append(copies.start(down, o_down))
+        back[part] = dot(g_gu[part], wgu[...], RIGHT_T).astype(BF)
+        down[part] = dot(hidden[part], wdown[...]).astype(BF)
+
+        @pl.when(i == 0)
+        def _():
+            out_copies[0].start()
+            out_copies[1].start()
+
+        @pl.when(i == 1)
+        def _():
+            out_copies[2].start()
+            out_copies[3].start()
+
+        return carry
+
+    lax.fori_loop(0, 2, one, 0)
     nz, _, wide = u.shape
-    piece = ma.shape[1] // nz
+    piece = x.shape[2] // nz
     step = hidden.shape[2] // nz
-    for z in range(nz):
-        at = slice(z * piece, (z + 1) * piece)
-        both = dot(ma[:, at], g_gu[0], LEFT_T) + dot(mb[:, at], g_gu[1], LEFT_T)
+    base = copies.used
+
+    def grads(z, carry):
+        at = pl.ds(pl.multiple_of(z * piece, piece), piece)
+        both = dot(x[0, :, at], g_gu[0], LEFT_T) + dot(x[1, :, at], g_gu[1], LEFT_T)
         u[z, :piece, :] = both.astype(BF)
-        at = slice(z * step, (z + 1) * step)
-        both = (dot(hidden[0, :, at], ea[...], LEFT_T) + dot(hidden[1, :, at], eb[...], LEFT_T)).astype(BF)
+        at = pl.ds(pl.multiple_of(z * step, step), step)
+        both = (dot(hidden[0, :, at], g[0], LEFT_T) + dot(hidden[1, :, at], g[1], LEFT_T)).astype(BF)
         u[z, piece : piece + step, :] = both[:, :wide]
         rest = both.shape[1] - wide
         u[z, piece + step :, :rest] = both[: step // 2, wide:]
         u[z, piece + step :, rest:] = both[step // 2 :, wide:]
-        gone.append(copies.start(u.at[z], o_u.at[z]))
-    for c in gone:
+        pltpu.make_async_copy(u.at[z], o_u.at[z], sems.at[base + z]).start()
+        return carry
+
+    lax.fori_loop(0, nz, grads, 0)
+    for c in out_copies:
         c.wait()
+    for z in range(nz):
+        pltpu.make_async_copy(u.at[z], o_u.at[z], sems.at[base + z]).wait()
 
 
 def unpack_down_kernel(u, out):
@@ -864,7 +884,8 @@
     down_mine, down_other, mine, other, u_mlp = moving_call(
         mlp_kernel,
         outs,
-        scratch=vmem(*ins, *outs)
+        scratch=[pltpu.VMEM((2, tokens // 2, width), BF)] * 4
+        + vmem(*ins[4:], outs[4])
         + [pltpu.VMEM((2, tokens // 2, cut), BF), pltpu.VMEM((2, tokens // 2, wide), BF), pltpu.VMEM((cut, width), BF)],
         copies=len(ins) + 4 + nz,
     )((meta,), *ins)
@@ -934,12 +955,18 @@
     c1, c2, v_gu, grad_down, block_out, grad_in = fence(c1, c2, v_gu, grad_down, block_out, grad_in)
     c0 = u0
     v_qkv, v_out = kernel_call(last_sum_kernel, (shaped(KV, rows, WIDE), shaped(*w_out.shape)))((), c0, c1, c2)
-    v_qkv = lay.exchange(v_qkv)
     grad_out = send(v_out, lay.back)
-    grad_gate, grad_up, total_m = kernel_call(
-        unpack_mlp_kernel, (shaped(*w_gate.shape, dtype=F32), shaped(*w_up.shape, dtype=F32), shaped(1, rows, dtype=F32))
-    )((), v_gu, w_gate, w_up, gain_m)
-    grad_out, v_qkv, grad_gate, grad_up, total_m = fence(grad_out.astype(F32), v_qkv, grad_gate, grad_up, total_m)
+
+    def share(v_qkv, v_gu, w_gate, w_up, gain_m):
+        v_qkv = lay.exchange(v_qkv)
+        grad_gate, grad_up, total_m = kernel_call(
+            unpack_mlp_kernel,
+            (shaped(*w_gate.shape, dtype=F32), shaped(*w_up.shape, dtype=F32), shaped(1, rows, dtype=F32)),
+        )((), v_gu, w_gate, w_up, gain_m)
+        return v_qkv, grad_gate, grad_up, total_m
+
+    v_qkv, grad_gate, grad_up, total_m = unit_of_work(go, share, v_qkv, v_gu, w_gate, w_up, gain_m)
+    grad_out = grad_out.astype(F32)
     grad_query, grad_key, grad_value, total = kernel_call(
         unpack_attention_kernel,
         tuple(shaped(*w.shape, dtype=F32) for w in (w_query, w_key, w_value)) + (shaped(1, rows, dtype=F32),),

time: 351 us -> 335 us (0.954)
  Pallas kernels: 79.5 us -> 70.8 us
  waiting for transfers between devices: 126 us -> 122 us
    ppermute x37, waiting for transfers between devices: 114 us -> 104 us  [send(): return lax.ppermute(x, AXES, pairs)]
    pallas_call x2, Pallas kernels: 43.6 us -> 36.2 us  [call(): pl.pallas_call(body, out_shape=outs, in_specs=[SMEM] * len(scalars) + [pl...]
    all_to_all x3, waiting for transfers between devices: 0.01 us -> 4.71 us  [exchange(): lax.all_to_all(x, AXES, split_axis=0, concat_axis=0, tiled=True, axis_ind...]
  transfers between devices with their start and end apart: 43 -> 43, of which waited for: 21 -> 21; matrix products, arithmetic and copies ran while one was open for 8% -> 8% of each run, Pallas kernels for 13% -> 14%
where the time goes in v1:
time: 335 us; the launch traced here: 332 us
  waiting for transfers between devices  122 us (36%)
  starting transfers between devices  73.5 us (22%)
  Pallas kernels  70.8 us (21%)
  blocking collectives  20.1 us (6%)
  other arithmetic  16.3 us (5%)
  local copies, waits for them, and re-layouts  15.8 us (5%)
  between operations  14.1 us (4%)
    ppermute x37, waiting for transfers between devices, send(): return lax.ppermute(x, AXES, pairs)  104 us
    ppermute x37, starting transfers between devices, send(): return lax.ppermute(x, AXES, pairs)  57 us
    pallas_call x2, Pallas kernels, call(): pl.pallas_call(body, out_shape=outs, in_specs=[SMEM] * len(scalars) + [pl...  36.2 us
    pallas_call x14, Pallas kernels, call(): pl.pallas_call(body, out_shape=outs, in_specs=[SMEM] * len(scalars) + [VM...  34.7 us
    all_to_all x1, blocking collectives, exchange(): lax.all_to_all(x, AXES, split_axis=0, concat_axis=0, tiled=True, axis_ind...  20.1 us
    all_to_all x3, starting transfers between devices, exchange(): lax.all_to_all(x, AXES, split_axis=0, concat_axis=0, tiled=True, axis_ind...  16.4 us
    all_gather x2, waiting for transfers between devices, spread(): lax.all_gather(x, AXES, axis=0, tiled=True, axis_index_groups=self.lines())  10.4 us
  transfers between devices with their start and end apart: 43, of which 21 were waited for; matrix products, arithmetic and copies ran while one was open for 8% of the time, Pallas kernels for 14%

profile of v1, /device:TPU:1, one launch (start us, length us, event | category | flops | bytes accessed | tf_op | source)
XLA Modules:
  0.0 332.3 jit_solution(10754220954806115716)
XLA Ops:
  7.2 2.2 collective-permute-start.20
  10.1 2.0 shard_map.230
  12.0 4.7 %all-to-all-start.2 = ((bf16[8,48,384]{2,1,0:T(8,128)(2,1)}), bf16[8,48,384]{2,1,0:T(8,128)(2,1)S(1)}, u32[]{:S(2)}, u32[]{:S(2)}) async-start(bf16[8,48,384]{2,1,0:T(8,128)(2,1)} %shard_map.230), calls=%async_computation.2 | async-start | bytes 589824 | tf_op jit(solution)/shard_map/all_to_all | solution.py:73
  16.7 5.9 %collective-permute-start.26 = (bf16[48,1536]{1,0:T(8,128)(2,1)}, bf16[48,1536]{1,0:T(8,128)(2,1)}, u32[]{:S(2)}, u32[]{:S(2)}) collective-permute-start(bf16[48,1536]{1,0:T(8,128)(2,1)} %param.30), channel_id=1, source_target_pairs={{0,0},{1,8},{2,16},{3,24},{4,1},{5,9},{6,17},{7,25},{8,2},{9,10},{... | collective-permute-start | bytes 442376 | tf_op jit(solution)/shard_map/ppermute | solution.py:41
  24.0 1.5 shard_map.231
  25.6 1.9 shard_map.232
  28.9 1.4 collective-permute-start.24
  33.4 6.4 %collective-permute-done.23.h3 = bf16[128,1536]{1,0:T(8,128)(2,1)S(1)} collective-permute-done((bf16[128,1536]{1,0:T(8,128)(2,1)S(1)}, bf16[128,1536]{1,0:T(8,128)(2,1)S(1)}, u32[]{:S(2)}, u32[]{:S(2)}) %collective-permute-start.23) | collective-permute-done | bytes 393248 | tf_op jit(solution)/shard_map/ppermute | solution.py:41
  40.6 30.4 %conditional.4 = (bf16[2,2,128,1536]{3,2,1,0:T(8,128)(2,1)}, bf16[2,2,128,1536]{3,2,1,0:T(8,128)(2,1)}, bf16[8,48,1024]{2,1,0:T(8,128)(2,1)S(1)}, bf16[2,128,1536]{2,1,0:T(8,128)(2,1)S(1)}) conditional(s32[]{:T(128)} %bitcast.35, () %tuple.61, (bf16[128,1536]{1,0:T(8,128)(2,1)}, bf16[128,1536]{1,0:T(8,128)(2,1)}, bf16[8,48,1024]{2,1,0:T(8,128)(2,1)S(1)}, ...), branch_computations={%region_0.1_spmd, %region_1.2_spmd} | conditional | flops 1572864 | bytes 18874520 | solution.py:48
  41.9 20.1 %all_to_all.18 = bf16[8,48,1024]{2,1,0:T(8,128)(2,1)S(1)} all-to-all(bf16[8,48,1024]{2,1,0:T(8,128)(2,1)S(1)} %get-tuple-element.80), channel_id=1, replica_groups={{0,1,2,3,4,5,6,7},{8,9,10,11,12,13,14,15},{16,17,18,19,20,21,22,23},{24..., dimensions={0} | all-to-all | bytes 1572864 | tf_op jit(solution)/shard_map/cond/branch_1_fun/all_to_all | solution.py:73
  62.0 1.3 pad_maximum_fusion
  64.1 6.9 %collective-permute-done.2 = bf16[128,1536]{1,0:T(8,128)(2,1)S(1)} collective-permute-done((bf16[128,1536]{1,0:T(8,128)(2,1)S(1)}, bf16[128,1536]{1,0:T(8,128)(2,1)S(1)}, u32[]{:S(2)}, u32[]{:S(2)}) %collective-permute-start.2) | collective-permute-done | bytes 393248 | tf_op jit(solution)/shard_map/cond/branch_1_fun/ppermute | solution.py:41
  71.1 10.4 %all-gather.3.cloned.1.call-done = bf16[2304,384]{1,0:T(8,128)(2,1)} async-done(((bf16[576,384]{1,0:T(8,128)(2,1)}), bf16[2304,384]{1,0:T(8,128)(2,1)}) %all-gather.3.cloned.1.call-update) | async-done | bytes 1769488 | tf_op jit(solution)/shard_map/all_gather | solution.py:83
  81.7 76.0 %conditional.5 = (bf16[1536,384]{1,0:T(8,128)(2,1)}, bf16[4,256,384]{2,1,0:T(8,128)(2,1)S(1)}, bf16[2,512,192]{2,1,0:T(8,128)(2,1)S(1)}, bf16[192,1536]{1,0:T(8,...) conditional(s32[]{:T(128)} %bitcast.35, () %tuple.60, ...), branch_computations={%region_2.3_spmd, %region_3.4_spmd} | conditional | flops 3145728 | bytes 69206608 | solution.py:48
  82.9 8.2 %branch_1_fun.6 = (bf16[1536,384]{1,0:T(8,128)(2,1)}, bf16[4,256,384]{2,1,0:T(8,128)(2,1)S(1)}, bf16[2,512,192]{2,1,0:T(8,128)(2,1)S(1)}) custom-call(s32[6]{0:T(128)S(1)} %get-tuple-element.89.meta, s32[4]{0:T(128)S(1)} %get-tuple-element.90.lens, s32[8]{0:T(128)S(1)} %get-tuple-element.91.spans, bf16[512,1536]{1,0:T(8,128)(2,1)} %bitcast.6.xa, ...), custom_call_target="tpu_custom_call" | custom-call | tf_op jit(solution)/shard_map/cond/branch_1_fun/pallas_call | solution.py:306
  91.1 1.7 collective-permute-done.3
  92.8 2.7 branch_1_fun.7
  95.5 1.5 collective-permute-start.4
  98.4 1.9 collective-permute-done.4
  102.5 10.1 %collective-permute-done.5 = bf16[256,1536]{1,0:T(8,128)(2,1)S(1)} collective-permute-done((bf16[256,1536]{1,0:T(8,128)(2,1)S(1)}, bf16[256,1536]{1,0:T(8,128)(2,1)S(1)}, u32[]{:S(2)}, u32[]{:S(2)}) %collective-permute-start.5) | collective-permute-done | bytes 786464 | tf_op jit(solution)/shard_map/cond/branch_1_fun/ppermute | solution.py:41
  114.6 5.8 %collective-permute-done.7.b = bf16[128,1536]{1,0:T(8,128)(2,1)S(1)} collective-permute-done((bf16[128,1536]{1,0:T(8,128)(2,1)S(1)}, bf16[128,1536]{1,0:T(8,128)(2,1)S(1)}, u32[]{:S(2)}, u32[]{:S(2)}) %collective-permute-start.7) | collective-permute-done | bytes 393248 | tf_op jit(solution)/shard_map/cond/branch_1_fun/ppermute | solution.py:41
  121.2 2.1 branch_1_fun.8
  124.5 6.0 %collective-permute-done.8 = bf16[128,1536]{1,0:T(8,128)(2,1)S(1)} collective-permute-done((bf16[128,1536]{1,0:T(8,128)(2,1)}, bf16[128,1536]{1,0:T(8,128)(2,1)S(1)}, u32[]{:S(2)}, u32[]{:S(2)}) %collective-permute-start.8) | collective-permute-done | bytes 393248 | tf_op jit(solution)/shard_map/cond/branch_1_fun/ppermute | solution.py:41
  134.2 17.7 %collective-permute-done.10 = bf16[128,1536]{1,0:T(8,128)(2,1)} collective-permute-done((bf16[128,1536]{1,0:T(8,128)(2,1)}, bf16[128,1536]{1,0:T(8,128)(2,1)}, u32[]{:S(2)}, u32[]{:S(2)}) %collective-permute-start.10) | collective-permute-done | bytes 393248 | tf_op jit(solution)/shard_map/cond/branch_1_fun/ppermute | solution.py:41
  154.3 3.4 %collective-permute-done.11 = bf16[2,2,128,1536]{3,2,1,0:T(8,128)(2,1)} collective-permute-done((bf16[2,2,128,1536]{3,2,1,0:T(8,128)(2,1)}, bf16[2,2,128,1536]{3,2,1,0:T(8,128)(2,1)}, u32[]{:S(2)}, u32[]{:S(2)}) %collective-permute-start.11) | collective-permute-done | bytes 1572896 | tf_op jit(solution)/shard_map/cond/branch_1_fun/ppermute | solution.py:41
  157.7 21.7 %shard_map.233 = (bf16[512,1536]{1,0:T(8,128)(2,1)}, bf16[512,1536]{1,0:T(8,128)(2,1)}, bf16[512,1536]{1,0:T(8,128)(2,1)}, bf16[512,1536]{1,0:T(8,128)(2,1)}, bf16[4,576,1024]{2,1,0:T(8,128)(2,1)}) custom-call(s32[6]{0:T(128)S(1)} %stack.99.meta, bf16[512,1536]{1,0:T(8,128)(2,1)} %get-tuple-element.270.h_ma, bf16[512,1536]{1,0:T(8,128)(2,1)} %get-tuple-element.271.h_mb, ...), custom_call_target="tpu_custom_call" | custom-call | tf_op jit(solution)/shard_map/pallas_call | solution.py:322
  179.4 70.9 %conditional.6 = (f32[128,1536]{1,0:T(8,128)S(1)}, bf16[512,1536]{1,0:T(8,128)(2,1)S(1)}, bf16[512,1536]{1,0:T(8,128)(2,1)S(1)}, bf16[128,1536]{1,0:T(8,128)(2,1...) conditional(s32[]{:T(128)} %bitcast.35, () %tuple.59, ...), branch_computations={%region_4.5_spmd, %region_5.6_spmd} | conditional | flops 5898240 | bytes 107741904 | solution.py:48
  179.9 1.8 convert_element_type.4
  181.7 1.4 collective-permute-done.12
  185.0 10.1 %collective-permute-done.13 = bf16[256,1536]{1,0:T(8,128)(2,1)S(1)} collective-permute-done((bf16[256,1536]{1,0:T(8,128)(2,1)S(1)}, bf16[256,1536]{1,0:T(8,128)(2,1)S(1)}, u32[]{:S(2)}, u32[]{:S(2)}) %collective-permute-start.13) | collective-permute-done | bytes 786464 | tf_op jit(solution)/shard_map/cond/branch_1_fun/ppermute | solution.py:41
  197.1 5.8 %collective-permute-done.14.b = bf16[128,1536]{1,0:T(8,128)(2,1)S(1)} collective-permute-done((bf16[128,1536]{1,0:T(8,128)(2,1)S(1)}, bf16[128,1536]{1,0:T(8,128)(2,1)S(1)}, u32[]{:S(2)}, u32[]{:S(2)}) %collective-permute-start.14) | collective-permute-done | bytes 393248 | tf_op jit(solution)/shard_map/cond/branch_1_fun/ppermute | solution.py:41
  203.7 2.2 branch_1_fun.9
  207.0 6.0 %collective-permute-done.15 = bf16[128,1536]{1,0:T(8,128)(2,1)S(1)} collective-permute-done((bf16[128,1536]{1,0:T(8,128)(2,1)}, bf16[128,1536]{1,0:T(8,128)(2,1)S(1)}, u32[]{:S(2)}, u32[]{:S(2)}) %collective-permute-start.15) | collective-permute-done | bytes 393248 | tf_op jit(solution)/shard_map/cond/branch_1_fun/ppermute | solution.py:41
  215.4 2.9 collective-permute-start.18
  218.4 7.1 %collective-permute-done.16 = bf16[2,128,1536]{2,1,0:T(8,128)(2,1)S(1)} collective-permute-done((bf16[2,128,1536]{2,1,0:T(8,128)(2,1)S(1)}, bf16[2,128,1536]{2,1,0:T(8,128)(2,1)S(1)}, u32[]{:S(2)}, u32[]{:S(2)}) %collective-permute-start.16) | collective-permute-done | bytes 786464 | tf_op jit(solution)/shard_map/cond/branch_1_fun/ppermute | solution.py:41
  225.7 3.4 %collective-permute-start.17 = (bf16[2,2,128,1536]{3,2,1,0:T(8,128)(2,1)S(1)}, bf16[2,2,128,1536]{3,2,1,0:T(8,128)(2,1)S(1)}, u32[]{:S(2)}, u32[]{:S(2)}) collective-permute-start(bf16[2,2,128,1536]{3,2,1,0:T(8,128)(2,1)S(1)} %pad_maximum_fusion.6), channel_id=1, source_target_pairs={{0,1},{1,0},{2,3},{3,2},{4,5},{5,4},{6,7},{7,6},{8,9},{9,8},{10,11... | collective-permute-start | bytes 4718600 | tf_op jit(solution)/shard_map/cond/branch_1_fun/ppermute | solution.py:41
  229.5 2.6 collective-permute-done.17
  233.8 14.4 %branch_1_fun.10 = (bf16[512,1536]{1,0:T(8,128)(2,1)S(1)}, bf16[512,1536]{1,0:T(8,128)(2,1)}, bf16[576,384]{1,0:T(8,128)(2,1)}, bf16[576,384]{1,0:T(8,128)(2,1)}...) custom-call(s32[6]{0:T(128)S(1)} %get-tuple-element.134.meta, s32[4]{0:T(128)S(1)} %get-tuple-element.135.lens, ...), custom_call_target="tpu_custom_call" | custom-call | tf_op jit(solution)/shard_map/cond/branch_1_fun/pallas_call | solution.py:322
  248.2 1.3 bitcast_add_fusion.1
  250.8 3.0 collective-permute-done.28
  257.5 2.1 collective-permute-start.27
  259.6 2.1 collective-permute-start.31
  262.9 2.0 reduce-scatter.2.cloned.1.call-done
  264.9 2.1 slice.103
  267.0 3.8 %collective-permute-done.27 = bf16[576,384]{1,0:T(8,128)(2,1)} collective-permute-done((bf16[576,384]{1,0:T(8,128)(2,1)S(1)}, bf16[576,384]{1,0:T(8,128)(2,1)}, u32[]{:S(2)}, u32[]{:S(2)}) %collective-permute-start.27) | collective-permute-done | bytes 442400 | tf_op jit(solution)/shard_map/ppermute | solution.py:41
  270.9 1.9 add.31
  272.7 1.4 collective-permute-start.30
  276.2 1.7 collective-permute-start.32
  277.9 5.7 %all-to-all-start.3 = ((bf16[8,48,1024]{2,1,0:T(8,128)(2,1)}), bf16[8,48,1024]{2,1,0:T(8,128)(2,1)S(1)}, u32[]{:S(2)}, u32[]{:S(2)}) async-start(bf16[8,48,1024]{2,1,0:T(8,128)(2,1)} %bitcast.52), calls=%async_computation.4 | async-start | bytes 1572864 | tf_op jit(solution)/shard_map/all_to_all | solution.py:73
  283.6 1.8 slice.105.u
  285.4 2.0 shard_map.235
  287.4 2.3 shard_map.234
  289.7 4.4 %collective-permute-start.34 = (bf16[576,384]{1,0:T(8,128)(2,1)}, bf16[576,384]{1,0:T(8,128)(2,1)}, u32[]{:S(2)}, u32[]{:S(2)}) collective-permute-start(bf16[576,384]{1,0:T(8,128)(2,1)} %get-tuple-element.301), channel_id=1, source_target_pairs={{0,8},{1,9},{2,10},{3,11},{4,12},{5,13},{6,14},{7,15},{8,0},{9,1},... | collective-permute-start | bytes 1327112 | tf_op jit(solution)/shard_map/ppermute | solution.py:41
  294.1 1.4 collective-permute-start.35
  295.5 1.9 shard_map.236
  298.3 2.3 shard_map.237
  300.6 4.3 %collective-permute-done.34.b = bf16[576,384]{1,0:T(8,128)(2,1)} collective-permute-done((bf16[576,384]{1,0:T(8,128)(2,1)}, bf16[576,384]{1,0:T(8,128)(2,1)}, u32[]{:S(2)}, u32[]{:S(2)}) %collective-permute-start.34) | collective-permute-done | bytes 442400 | tf_op jit(solution)/shard_map/ppermute | solution.py:41
  304.8 2.0 shard_map.238
  306.9 3.9 %collective-permute-start.36 = (bf16[48,1536]{1,0:T(8,128)(2,1)}, bf16[48,1536]{1,0:T(8,128)(2,1)S(1)}, u32[]{:S(2)}, u32[]{:S(2)}) collective-permute-start(bf16[48,1536]{1,0:T(8,128)(2,1)} %get-tuple-element.322), channel_id=1, source_target_pairs={{0,0},{8,1},{16,2},{24,3},{1,4},{9,5},{17,6},{25,7},{2,8},{10,9},{... | collective-permute-start | bytes 442376 | tf_op jit(solution)/shard_map/ppermute | solution.py:41
  310.8 12.2 %conditional.7 = (bf16[8,48,384]{2,1,0:T(8,128)(2,1)}, f32[48,4096]{1,0:T(8,128)}, f32[48,4096]{1,0:T(8,128)}, f32[48]{0:T(128)}) conditional(s32[]{:T(128)} %bitcast.35, () %tuple.72, (bf16[8,48,384]{2,1,0:T(8,128)(2,1)}, bf16[8,48,1024]{2,1,0:T(8,128)(2,1)S(1)}, bf16[48,4096]{1,0:T(8,128)(2,1)S(1)}, bf16[48,4096]{1,0:T(8,128)(2,1)S(1)}, ...), branch_computations={%region_7.8_spmd, %region_8.9_spmd} | conditional | bytes 1868014 | solution.py:48
  310.8 6.1 %all-to-all-start = ((bf16[8,48,384]{2,1,0:T(8,128)(2,1)}), bf16[8,48,384]{2,1,0:T(8,128)(2,1)}, u32[]{:S(2)}, u32[]{:S(2)}) async-start(bf16[8,48,384]{2,1,0:T(8,128)(2,1)} %get-tuple-element.160), calls=%async_computation | async-start | bytes 589824 | tf_op jit(solution)/shard_map/cond/branch_1_fun/all_to_all | solution.py:73
  316.8 1.4 branch_1_fun.11
  318.3 4.7 %all-to-all-done = bf16[8,48,384]{2,1,0:T(8,128)(2,1)} async-done(((bf16[8,48,384]{2,1,0:T(8,128)(2,1)}), bf16[8,48,384]{2,1,0:T(8,128)(2,1)}, u32[]{:S(2)}, u32[]{:S(2)}) %all-to-all-start) | async-done | bytes 294944 | tf_op jit(solution)/shard_map/cond/branch_1_fun/all_to_all | solution.py:73
  323.0 2.1 shard_map.239
  (157 shorter events, 44.6 us)
Async XLA Ops:
  7.2 18.4 %copy-start.6 = (bf16[2,64,1536]{2,1,0:T(8,128)(2,1)S(1)}, bf16[2,64,1536]{2,1,0:T(8,128)(2,1)}, u32[]{:S(2)}) copy-start(bf16[2,64,1536]{2,1,0:T(8,128)(2,1)} %param.23) | copy-start | bytes 1179652
  7.2 18.4 %copy-start.33 = (s32[8]{0:T(128)S(1)}, s32[8]{0:T(128)}, u32[]{:S(2)}) copy-start(s32[8]{0:T(128)} %spans.3) | copy-start | bytes 100
  7.2 20.3 %collective-permute-start.20 = (bf16[128,1536]{1,0:T(8,128)(2,1)}, bf16[128,1536]{1,0:T(8,128)(2,1)S(1)}, u32[]{:S(2)}, u32[]{:S(2)}) collective-permute-start(bf16[128,1536]{1,0:T(8,128)(2,1)} %h0.1), channel_id=1, source_target_pairs={{0,8},{1,9},{2,10},{3,11},{4,12},{5,13},{6,14},{7,15},{8,0},{9,1},... | collective-permute-start | bytes 1179656 | tf_op jit(solution)/shard_map/ppermute | solution.py:41
  9.4 18.2 %collective-permute-start.21 = (bf16[128,1536]{1,0:T(8,128)(2,1)}, bf16[128,1536]{1,0:T(8,128)(2,1)S(1)}, u32[]{:S(2)}, u32[]{:S(2)}) collective-permute-start(bf16[128,1536]{1,0:T(8,128)(2,1)} %h0.1), channel_id=1, source_target_pairs={{8,16},{9,17},{10,18},{11,19},{12,20},{13,21},{14,22},{15,23},{16,... | collective-permute-start | bytes 1179656 | tf_op jit(solution)/shard_map/ppermute | solution.py:41
  12.0 15.5 %all-to-all-start.2 = ((bf16[8,48,384]{2,1,0:T(8,128)(2,1)}), bf16[8,48,384]{2,1,0:T(8,128)(2,1)S(1)}, u32[]{:S(2)}, u32[]{:S(2)}) async-start(bf16[8,48,384]{2,1,0:T(8,128)(2,1)} %shard_map.230), calls=%async_computation.2 | async-start | bytes 589824 | tf_op jit(solution)/shard_map/all_to_all | solution.py:73
  16.7 64.8 %all-gather.3.cloned.1.call-start = ((), (), s32[]{:S(2)}) async-start(), calls=%async_computation.5 | async-start | bytes 2211840 | tf_op jit(solution)/shard_map/all_gather | solution.py:83
  16.7 13.6 %collective-permute-start.26 = (bf16[48,1536]{1,0:T(8,128)(2,1)}, bf16[48,1536]{1,0:T(8,128)(2,1)}, u32[]{:S(2)}, u32[]{:S(2)}) collective-permute-start(bf16[48,1536]{1,0:T(8,128)(2,1)} %param.30), channel_id=1, source_target_pairs={{0,0},{1,8},{2,16},{3,24},{4,1},{5,9},{6,17},{7,25},{8,2},{9,10},{... | collective-permute-start | bytes 442376 | tf_op jit(solution)/shard_map/ppermute | solution.py:41
  22.7 4.9 %collective-permute-start.22 = (s32[2]{0:T(128)}, s32[2]{0:T(128)S(1)}, u32[]{:S(2)}, u32[]{:S(2)}) collective-permute-start(s32[2]{0:T(128)} %lens.3), channel_id=1, source_target_pairs={{0,4},{1,5},{2,6},{3,7},{4,0},{5,1},{6,2},{7,3},{8,12},{9,13},{10,... | collective-permute-start | bytes 32 | tf_op jit(solution)/shard_map/ppermute | solution.py:41
  24.0 16.0 %copy-start.35 = (s32[2]{0:T(128)S(1)}, s32[2]{0:T(128)}, u32[]{:S(2)}) copy-start(s32[2]{0:T(128)} %lens.3) | copy-start | bytes 28
  27.5 12.5 %copy-start.24 = (bf16[128,1536]{1,0:T(8,128)(2,1)}, bf16[128,1536]{1,0:T(8,128)(2,1)S(1)}, u32[]{:S(2)}) copy-start(bf16[128,1536]{1,0:T(8,128)(2,1)S(1)} %get-tuple-element.261) | copy-start | bytes 1179652
  27.5 12.5 %copy-start.28 = (bf16[128,1536]{1,0:T(8,128)(2,1)}, bf16[128,1536]{1,0:T(8,128)(2,1)S(1)}, u32[]{:S(2)}) copy-start(bf16[128,1536]{1,0:T(8,128)(2,1)S(1)} %collective-permute-done.20.h1) | copy-start | bytes 1179652
  27.6 12.5 %copy-start.29 = (bf16[128,1536]{1,0:T(8,128)(2,1)}, bf16[128,1536]{1,0:T(8,128)(2,1)S(1)}, u32[]{:S(2)}) copy-start(bf16[128,1536]{1,0:T(8,128)(2,1)S(1)} %collective-permute-done.21.h2) | copy-start | bytes 1179652
  27.6 12.3 %collective-permute-start.23 = (bf16[128,1536]{1,0:T(8,128)(2,1)S(1)}, bf16[128,1536]{1,0:T(8,128)(2,1)S(1)}, u32[]{:S(2)}, u32[]{:S(2)}) collective-permute-start(bf16[128,1536]{1,0:T(8,128)(2,1)S(1)} %collective-permute-done.21.h2), channel_id=1, source_target_pairs={{8,0},{9,1},{10,2},{11,3},{12,4},{13,5},{14,6},{15,7},{16,24},{17,... | collective-permute-start | bytes 1179656 | tf_op jit(solution)/shard_map/ppermute | solution.py:41
  28.9 11.0 %collective-permute-start.24 = (bf16[128,1536]{1,0:T(8,128)(2,1)S(1)}, bf16[128,1536]{1,0:T(8,128)(2,1)}, u32[]{:S(2)}, u32[]{:S(2)}) collective-permute-start(bf16[128,1536]{1,0:T(8,128)(2,1)S(1)} %collective-permute-done.20.h1), channel_id=1, source_target_pairs={{8,16},{9,17},{10,18},{11,19},{12,20},{13,21},{14,22},{15,23},{16,... | collective-permute-start | bytes 1179656 | tf_op jit(solution)/shard_map/ppermute | solution.py:41
  30.3 9.6 %collective-permute-start.25 = (bf16[128,1536]{1,0:T(8,128)(2,1)}, bf16[128,1536]{1,0:T(8,128)(2,1)}, u32[]{:S(2)}, u32[]{:S(2)}) collective-permute-start(bf16[128,1536]{1,0:T(8,128)(2,1)} %get-tuple-element.255), channel_id=1, source_target_pairs={{0,4},{1,3},{2,6},{3,1},{4,0},{5,7},{6,2},{7,5},{8,12},{9,11},{10,... | collective-permute-start | bytes 1179656 | tf_op jit(solution)/shard_map/ppermute | solution.py:41
  33.4 6.5 %copy-start.27 = (bf16[576,384]{1,0:T(8,128)(2,1)}, bf16[576,384]{1,0:T(8,128)(2,1)S(1)}, u32[]{:S(2)}) copy-start(bf16[576,384]{1,0:T(8,128)(2,1)S(1)} %slice_dynamic-update-slice_fusion) | copy-start | bytes 1327108
  39.9 117.7 %all-gather.5.cloned.1.call-start = ((), (), s32[]{:S(2)}) async-start(), calls=%async_computation.6 | async-start | bytes 3932160 | tf_op jit(solution)/shard_map/all_gather | solution.py:83
  41.8 20.1 %collective-permute-start = (bf16[2,128,1536]{2,1,0:T(8,128)(2,1)S(1)}, bf16[2,128,1536]{2,1,0:T(8,128)(2,1)S(1)}, u32[]{:S(2)}, u32[]{:S(2)}) collective-permute-start(bf16[2,128,1536]{2,1,0:T(8,128)(2,1)S(1)} %pad_maximum_fusion.1), channel_id=1, source_target_pairs={{0,2},{1,5},{2,0},{3,7},{4,6},{5,1},{6,4},{7,3},{8,10},{9,13},{10,... | collective-permute-start | bytes 2359304 | tf_op jit(solution)/shard_map/cond/branch_1_fun/ppermute | solution.py:41
  63.3 7.7 %collective-permute-start.1 = (bf16[2,2,128,1536]{3,2,1,0:T(8,128)(2,1)}, bf16[2,2,128,1536]{3,2,1,0:T(8,128)(2,1)}, u32[]{:S(2)}, u32[]{:S(2)}) collective-permute-start(bf16[2,2,128,1536]{3,2,1,0:T(8,128)(2,1)} %pad_maximum_fusion), channel_id=1, source_target_pairs={{0,1},{1,0},{2,3},{3,2},{4,5},{5,4},{6,7},{7,6},{8,9},{9,8},{10,11... | collective-permute-start | bytes 4718600 | tf_op jit(solution)/shard_map/cond/branch_1_fun/ppermute | solution.py:41
  63.9 7.0 %collective-permute-start.2 = (bf16[128,1536]{1,0:T(8,128)(2,1)S(1)}, bf16[128,1536]{1,0:T(8,128)(2,1)S(1)}, u32[]{:S(2)}, u32[]{:S(2)}) collective-permute-start(bf16[128,1536]{1,0:T(8,128)(2,1)S(1)} %get-tuple-element.84), channel_id=1, source_target_pairs={{0,4},{1,3},{2,6},{3,1},{4,0},{5,7},{6,2},{7,5},{8,12},{9,11},{10,... | collective-permute-start | bytes 1179656 | tf_op jit(solution)/shard_map/cond/branch_1_fun/ppermute | solution.py:41
  71.1 10.4 %copy-start.7 = (bf16[8,48,1024]{2,1,0:T(8,128)(2,1)}, bf16[8,48,1024]{2,1,0:T(8,128)(2,1)S(1)}, u32[]{:S(2)}) copy-start(bf16[8,48,1024]{2,1,0:T(8,128)(2,1)S(1)} %get-tuple-element.274) | copy-start | bytes 2359300
  81.5 183.4 %reduce-scatter.2.cloned.1.call-start = ((), (), s32[]{:S(2)}) async-start(), calls=%async_computation.7 | async-start | bytes 5898240 | tf_op jit(solution)/shard_map/reduce_scatter | solution.py:89
  81.7 11.2 %collective-permute-start.3 = (bf16[2,128,1536]{2,1,0:T(8,128)(2,1)S(1)}, bf16[2,128,1536]{2,1,0:T(8,128)(2,1)S(1)}, u32[]{:S(2)}, u32[]{:S(2)}) collective-permute-start(bf16[2,128,1536]{2,1,0:T(8,128)(2,1)S(1)} %get-tuple-element.100), channel_id=1, source_target_pairs={{0,2},{1,5},{2,0},{3,7},{4,6},{5,1},{6,4},{7,3},{8,10},{9,13},{10,... | collective-permute-start | bytes 2359304 | tf_op jit(solution)/shard_map/cond/branch_1_fun/ppermute | solution.py:41
  82.9 9.9 %copy-start = (bf16[2304,384]{1,0:T(8,128)(2,1)S(1)}, bf16[2304,384]{1,0:T(8,128)(2,1)}, u32[]{:S(2)}) copy-start(bf16[2304,384]{1,0:T(8,128)(2,1)} %get-tuple-element.94) | copy-start | bytes 5308420 | tf_op jit(solution)/shard_map/cond
  91.1 7.3 %copy-start.4 = (bf16[2,512,192]{2,1,0:T(8,128)(2,1)}, bf16[2,512,192]{2,1,0:T(8,128)(2,1)S(1)}, u32[]{:S(2)}) copy-start(bf16[2,512,192]{2,1,0:T(8,128)(2,1)S(1)} %get-tuple-element.356.att) | copy-start | bytes 1179652 | tf_op jit(solution)/shard_map/cond
  95.5 4.8 %collective-permute-start.4 = (bf16[512,1536]{1,0:T(8,128)(2,1)}, bf16[512,1536]{1,0:T(8,128)(2,1)S(1)}, u32[]{:S(2)}, u32[]{:S(2)}) collective-permute-start(bf16[512,1536]{1,0:T(8,128)(2,1)} %get-tuple-element.107), channel_id=1, source_target_pairs={{0,1},{1,0},{2,3},{3,2},{4,5},{5,4},{6,7},{7,6},{8,9},{9,8},{10,11... | collective-permute-start | bytes 4718600 | tf_op jit(solution)/shard_map/cond/branch_1_fun/ppermute | solution.py:41
  100.7 11.8 %collective-permute-start.6 = (bf16[2,2,128,1536]{3,2,1,0:T(8,128)(2,1)}, bf16[2,2,128,1536]{3,2,1,0:T(8,128)(2,1)}, u32[]{:S(2)}, u32[]{:S(2)}) collective-permute-start(bf16[2,2,128,1536]{3,2,1,0:T(8,128)(2,1)} %pad_maximum_fusion.3), channel_id=1, source_target_pairs={{0,1},{1,0},{2,3},{3,2},{4,5},{5,4},{6,7},{7,6},{8,9},{9,8},{10,11... | collective-permute-start | bytes 4718600 | tf_op jit(solution)/shard_map/cond/branch_1_fun/ppermute | solution.py:41
  101.2 11.3 %collective-permute-start.5 = (bf16[256,1536]{1,0:T(8,128)(2,1)S(1)}, bf16[256,1536]{1,0:T(8,128)(2,1)S(1)}, u32[]{:S(2)}, u32[]{:S(2)}) collective-permute-start(bf16[256,1536]{1,0:T(8,128)(2,1)S(1)} %slice_bitcast_fusion), channel_id=1, source_target_pairs={{0,2},{1,5},{2,0},{3,7},{4,6},{5,1},{6,4},{7,3},{8,10},{9,13},{10,... | collective-permute-start | bytes 2359304 | tf_op jit(solution)/shard_map/cond/branch_1_fun/ppermute | solution.py:41
  113.4 7.0 %collective-permute-start.7 = (bf16[128,1536]{1,0:T(8,128)(2,1)S(1)}, bf16[128,1536]{1,0:T(8,128)(2,1)S(1)}, u32[]{:S(2)}, u32[]{:S(2)}) collective-permute-start(bf16[128,1536]{1,0:T(8,128)(2,1)S(1)} %get-tuple-element.327), channel_id=1, source_target_pairs={{0,4},{1,3},{2,6},{3,1},{4,0},{5,7},{6,2},{7,5},{8,12},{9,11},{10,... | collective-permute-start | bytes 1179656 | tf_op jit(solution)/shard_map/cond/branch_1_fun/ppermute | solution.py:41
  123.3 7.2 %collective-permute-start.8 = (bf16[128,1536]{1,0:T(8,128)(2,1)}, bf16[128,1536]{1,0:T(8,128)(2,1)S(1)}, u32[]{:S(2)}, u32[]{:S(2)}) collective-permute-start(bf16[128,1536]{1,0:T(8,128)(2,1)} %get-tuple-element.115), channel_id=1, source_target_pairs={{0,4},{1,3},{2,6},{3,1},{4,0},{5,7},{6,2},{7,5},{8,12},{9,11},{10,... | collective-permute-start | bytes 1179656 | tf_op jit(solution)/shard_map/cond/branch_1_fun/ppermute | solution.py:41
  131.6 20.3 %collective-permute-start.9 = (bf16[2,128,1536]{2,1,0:T(8,128)(2,1)S(1)}, bf16[2,128,1536]{2,1,0:T(8,128)(2,1)S(1)}, u32[]{:S(2)}, u32[]{:S(2)}) collective-permute-start(bf16[2,128,1536]{2,1,0:T(8,128)(2,1)S(1)} %pad_maximum_fusion.5), channel_id=1, source_target_pairs={{0,2},{1,5},{2,0},{3,7},{4,6},{5,1},{6,4},{7,3},{8,10},{9,13},{10,... | collective-permute-start | bytes 2359304 | tf_op jit(solution)/shard_map/cond/branch_1_fun/ppermute | solution.py:41
  132.9 19.0 %collective-permute-start.10 = (bf16[128,1536]{1,0:T(8,128)(2,1)}, bf16[128,1536]{1,0:T(8,128)(2,1)}, u32[]{:S(2)}, u32[]{:S(2)}) collective-permute-start(bf16[128,1536]{1,0:T(8,128)(2,1)} %get-tuple-element.118), channel_id=1, source_target_pairs={{8,0},{9,1},{10,2},{11,3},{12,4},{13,5},{14,6},{15,7},{16,24},{17,... | collective-permute-start | bytes 1179656 | tf_op jit(solution)/shard_map/cond/branch_1_fun/ppermute | solution.py:41
  151.9 5.8 %copy-start.5 = (bf16[2,512,192]{2,1,0:T(8,128)(2,1)S(1)}, bf16[2,512,192]{2,1,0:T(8,128)(2,1)}, u32[]{:S(2)}) copy-start(bf16[2,512,192]{2,1,0:T(8,128)(2,1)} %copy-done.4) | copy-start | bytes 1179652 | tf_op jit(solution)/shard_map/cond
  153.2 4.5 %collective-permute-start.11 = (bf16[2,2,128,1536]{3,2,1,0:T(8,128)(2,1)}, bf16[2,2,128,1536]{3,2,1,0:T(8,128)(2,1)}, u32[]{:S(2)}, u32[]{:S(2)}) collective-permute-start(bf16[2,2,128,1536]{3,2,1,0:T(8,128)(2,1)} %pad_maximum_fusion.4), channel_id=1, source_target_pairs={{0,1},{1,0},{2,3},{3,2},{4,5},{5,4},{6,7},{7,6},{8,9},{9,8},{10,11... | collective-permute-start | bytes 4718600 | tf_op jit(solution)/shard_map/cond/branch_1_fun/ppermute | solution.py:41
  179.5 3.7 %collective-permute-start.12 = (bf16[512,1536]{1,0:T(8,128)(2,1)}, bf16[512,1536]{1,0:T(8,128)(2,1)S(1)}, u32[]{:S(2)}, u32[]{:S(2)}) collective-permute-start(bf16[512,1536]{1,0:T(8,128)(2,1)} %get-tuple-element.125), channel_id=1, source_target_pairs={{0,1},{1,0},{2,3},{3,2},{4,5},{5,4},{6,7},{7,6},{8,9},{9,8},{10,11... | collective-permute-start | bytes 4718600 | tf_op jit(solution)/shard_map/cond/branch_1_fun/ppermute | solution.py:41
  183.7 20.0 %copy-start.25 = (bf16[128,1536]{1,0:T(8,128)(2,1)S(1)}, bf16[128,1536]{1,0:T(8,128)(2,1)}, u32[]{:S(2)}) copy-start(bf16[128,1536]{1,0:T(8,128)(2,1)} %get-tuple-element.122.g_res) | copy-start | bytes 1179652 | tf_op jit(solution)/shard_map/cond
  183.7 11.3 %collective-permute-start.13 = (bf16[256,1536]{1,0:T(8,128)(2,1)S(1)}, bf16[256,1536]{1,0:T(8,128)(2,1)S(1)}, u32[]{:S(2)}, u32[]{:S(2)}) collective-permute-start(bf16[256,1536]{1,0:T(8,128)(2,1)S(1)} %slice.93), channel_id=1, source_target_pairs={{0,2},{1,5},{2,0},{3,7},{4,6},{5,1},{6,4},{7,3},{8,10},{9,13},{10,... | collective-permute-start | bytes 2359304 | tf_op jit(solution)/shard_map/cond/branch_1_fun/ppermute | solution.py:41
  195.9 7.0 %collective-permute-start.14 = (bf16[128,1536]{1,0:T(8,128)(2,1)S(1)}, bf16[128,1536]{1,0:T(8,128)(2,1)S(1)}, u32[]{:S(2)}, u32[]{:S(2)}) collective-permute-start(bf16[128,1536]{1,0:T(8,128)(2,1)S(1)} %get-tuple-element.333), channel_id=1, source_target_pairs={{0,4},{1,3},{2,6},{3,1},{4,0},{5,7},{6,2},{7,5},{8,12},{9,11},{10,... | collective-permute-start | bytes 1179656 | tf_op jit(solution)/shard_map/cond/branch_1_fun/ppermute | solution.py:41
  205.8 9.6 %copy-start.36 = (bf16[512,1536]{1,0:T(8,128)(2,1)S(1)}, bf16[512,1536]{1,0:T(8,128)(2,1)}, u32[]{:S(2)}) copy-start(bf16[512,1536]{1,0:T(8,128)(2,1)} %get-tuple-element.132) | copy-start | bytes 4718596 | tf_op jit(solution)/shard_map/cond
  205.9 7.2 %collective-permute-start.15 = (bf16[128,1536]{1,0:T(8,128)(2,1)}, bf16[128,1536]{1,0:T(8,128)(2,1)S(1)}, u32[]{:S(2)}, u32[]{:S(2)}) collective-permute-start(bf16[128,1536]{1,0:T(8,128)(2,1)} %get-tuple-element.130), channel_id=1, source_target_pairs={{0,4},{1,3},{2,6},{3,1},{4,0},{5,7},{6,2},{7,5},{8,12},{9,11},{10,... | collective-permute-start | bytes 1179656 | tf_op jit(solution)/shard_map/cond/branch_1_fun/ppermute | solution.py:41
  214.2 11.3 %collective-permute-start.16 = (bf16[2,128,1536]{2,1,0:T(8,128)(2,1)S(1)}, bf16[2,128,1536]{2,1,0:T(8,128)(2,1)S(1)}, u32[]{:S(2)}, u32[]{:S(2)}) collective-permute-start(bf16[2,128,1536]{2,1,0:T(8,128)(2,1)S(1)} %get-tuple-element.332), channel_id=1, source_target_pairs={{0,2},{1,5},{2,0},{3,7},{4,6},{5,1},{6,4},{7,3},{8,10},{9,13},{10,... | collective-permute-start | bytes 2359304 | tf_op jit(solution)/shard_map/cond/branch_1_fun/ppermute | solution.py:41
  215.4 13.7 %collective-permute-start.18 = (bf16[512,1536]{1,0:T(8,128)(2,1)S(1)}, bf16[512,1536]{1,0:T(8,128)(2,1)S(1)}, u32[]{:S(2)}, u32[]{:S(2)}) collective-permute-start(bf16[512,1536]{1,0:T(8,128)(2,1)S(1)} %copy-done.36), channel_id=1, source_target_pairs={{0,1},{1,0},{2,3},{3,2},{4,5},{5,4},{6,7},{7,6},{8,9},{9,8},{10,11... | collective-permute-start | bytes 4718600 | tf_op jit(solution)/shard_map/cond/branch_1_fun/ppermute | solution.py:41
  225.7 6.5 %collective-permute-start.17 = (bf16[2,2,128,1536]{3,2,1,0:T(8,128)(2,1)S(1)}, bf16[2,2,128,1536]{3,2,1,0:T(8,128)(2,1)S(1)}, u32[]{:S(2)}, u32[]{:S(2)}) collective-permute-start(bf16[2,2,128,1536]{3,2,1,0:T(8,128)(2,1)S(1)} %pad_maximum_fusion.6), channel_id=1, source_target_pairs={{0,1},{1,0},{2,3},{3,2},{4,5},{5,4},{6,7},{7,6},{8,9},{9,8},{10,11... | collective-permute-start | bytes 4718600 | tf_op jit(solution)/shard_map/cond/branch_1_fun/ppermute | solution.py:41
  232.2 16.0 %collective-permute-start.19 = (bf16[256,1536]{1,0:T(8,128)(2,1)S(1)}, bf16[256,1536]{1,0:T(8,128)(2,1)}, u32[]{:S(2)}, u32[]{:S(2)}) collective-permute-start(bf16[256,1536]{1,0:T(8,128)(2,1)S(1)} %slice_bitcast_fusion.1), channel_id=1, source_target_pairs={{0,2},{1,5},{2,0},{3,7},{4,6},{5,1},{6,4},{7,3},{8,10},{9,13},{10,... | collective-permute-start | bytes 2359304 | tf_op jit(solution)/shard_map/cond/branch_1_fun/ppermute | solution.py:41
  250.4 3.5 %collective-permute-start.28 = (bf16[512,1536]{1,0:T(8,128)(2,1)S(1)}, bf16[512,1536]{1,0:T(8,128)(2,1)S(1)}, u32[]{:S(2)}, u32[]{:S(2)}) collective-permute-start(bf16[512,1536]{1,0:T(8,128)(2,1)S(1)} %get-tuple-element.289), channel_id=1, source_target_pairs={{0,1},{1,0},{2,3},{3,2},{4,5},{5,4},{6,7},{7,6},{8,9},{9,8},{10,11... | collective-permute-start | bytes 4718600 | tf_op jit(solution)/shard_map/ppermute | solution.py:41
  256.3 17.8 %copy-start.2 = (bf16[512,1536]{1,0:T(8,128)(2,1)S(1)}, bf16[512,1536]{1,0:T(8,128)(2,1)}, u32[]{:S(2)}) copy-start(bf16[512,1536]{1,0:T(8,128)(2,1)} %copy-done.1) | copy-start | bytes 4718596
  256.3 14.5 %collective-permute-start.29 = (bf16[256,1536]{1,0:T(8,128)(2,1)}, bf16[256,1536]{1,0:T(8,128)(2,1)}, u32[]{:S(2)}, u32[]{:S(2)}) collective-permute-start(bf16[256,1536]{1,0:T(8,128)(2,1)} %slice.102), channel_id=1, source_target_pairs={{0,2},{1,5},{2,0},{3,7},{4,6},{5,1},{6,4},{7,3},{8,10},{9,13},{10,... | collective-permute-start | bytes 2359304 | tf_op jit(solution)/shard_map/ppermute | solution.py:41
  257.5 13.3 %collective-permute-start.27 = (bf16[576,384]{1,0:T(8,128)(2,1)S(1)}, bf16[576,384]{1,0:T(8,128)(2,1)}, u32[]{:S(2)}, u32[]{:S(2)}) collective-permute-start(bf16[576,384]{1,0:T(8,128)(2,1)S(1)} %copy-done.13), channel_id=1, source_target_pairs={{0,8},{1,9},{2,10},{3,11},{4,12},{5,13},{6,14},{7,15},{24,16},{25,... | collective-permute-start | bytes 1327112 | tf_op jit(solution)/shard_map/ppermute | solution.py:41
  259.6 27.8 %collective-permute-start.31 = (bf16[576,384]{1,0:T(8,128)(2,1)}, bf16[576,384]{1,0:T(8,128)(2,1)}, u32[]{:S(2)}, u32[]{:S(2)}) collective-permute-start(bf16[576,384]{1,0:T(8,128)(2,1)} %get-tuple-element.295.c), channel_id=1, source_target_pairs={{0,8},{1,9},{2,10},{3,11},{4,12},{5,13},{6,14},{7,15},{24,16},{25,... | collective-permute-start | bytes 1327112 | tf_op jit(solution)/shard_map/ppermute | solution.py:41
  261.7 25.6 %collective-permute-start.33 = (bf16[128,1536]{1,0:T(8,128)(2,1)}, bf16[128,1536]{1,0:T(8,128)(2,1)}, u32[]{:S(2)}, u32[]{:S(2)}) collective-permute-start(bf16[128,1536]{1,0:T(8,128)(2,1)} %get-tuple-element.298), channel_id=1, source_target_pairs={{0,4},{1,3},{2,6},{3,1},{4,0},{5,7},{6,2},{7,5},{8,12},{9,11},{10,... | collective-permute-start | bytes 1179656 | tf_op jit(solution)/shard_map/ppermute | solution.py:41
  272.7 14.6 %collective-permute-start.30 = (bf16[576,384]{1,0:T(8,128)(2,1)}, bf16[576,384]{1,0:T(8,128)(2,1)}, u32[]{:S(2)}, u32[]{:S(2)}) collective-permute-start(bf16[576,384]{1,0:T(8,128)(2,1)} %add.31), channel_id=1, source_target_pairs={{8,16},{9,17},{10,18},{11,19},{12,20},{13,21},{14,22},{15,23},{16,... | collective-permute-start | bytes 1327112 | tf_op jit(solution)/shard_map/ppermute | solution.py:41
  276.2 11.2 %collective-permute-start.32 = (bf16[128,1536]{1,0:T(8,128)(2,1)}, bf16[128,1536]{1,0:T(8,128)(2,1)}, u32[]{:S(2)}, u32[]{:S(2)}) collective-permute-start(bf16[128,1536]{1,0:T(8,128)(2,1)} %slice.104), channel_id=1, source_target_pairs={{0,4},{1,3},{2,6},{3,1},{4,0},{5,7},{6,2},{7,5},{8,12},{9,11},{10,... | collective-permute-start | bytes 1179656 | tf_op jit(solution)/shard_map/ppermute | solution.py:41
  277.9 9.5 %copy-start.12 = (bf16[576,384]{1,0:T(8,128)(2,1)S(1)}, bf16[576,384]{1,0:T(8,128)(2,1)}, u32[]{:S(2)}) copy-start(bf16[576,384]{1,0:T(8,128)(2,1)} %get-tuple-element.287.a) | copy-start | bytes 1327108
  277.9 22.7 %all-to-all-start.3 = ((bf16[8,48,1024]{2,1,0:T(8,128)(2,1)}), bf16[8,48,1024]{2,1,0:T(8,128)(2,1)S(1)}, u32[]{:S(2)}, u32[]{:S(2)}) async-start(bf16[8,48,1024]{2,1,0:T(8,128)(2,1)} %bitcast.52), calls=%async_computation.4 | async-start | bytes 1572864 | tf_op jit(solution)/shard_map/all_to_all | solution.py:73
  285.4 10.2 %copy-start.23 = (bf16[128,1536]{1,0:T(8,128)(2,1)S(1)}, bf16[128,1536]{1,0:T(8,128)(2,1)}, u32[]{:S(2)}) copy-start(bf16[128,1536]{1,0:T(8,128)(2,1)} %copy-done.22) | copy-start | bytes 1179652
  289.7 8.6 %copy-start.9 = (f32[128,1536]{1,0:T(8,128)S(1)}, f32[128,1536]{1,0:T(8,128)}, u32[]{:S(2)}) copy-start(f32[128,1536]{1,0:T(8,128)} %copy-done.8) | copy-start | bytes 2359300
  289.7 15.2 %collective-permute-start.34 = (bf16[576,384]{1,0:T(8,128)(2,1)}, bf16[576,384]{1,0:T(8,128)(2,1)}, u32[]{:S(2)}, u32[]{:S(2)}) collective-permute-start(bf16[576,384]{1,0:T(8,128)(2,1)} %get-tuple-element.301), channel_id=1, source_target_pairs={{0,8},{1,9},{2,10},{3,11},{4,12},{5,13},{6,14},{7,15},{8,0},{9,1},... | collective-permute-start | bytes 1327112 | tf_op jit(solution)/shard_map/ppermute | solution.py:41
  294.1 10.7 %collective-permute-start.35 = (bf16[576,384]{1,0:T(8,128)(2,1)}, bf16[576,384]{1,0:T(8,128)(2,1)}, u32[]{:S(2)}, u32[]{:S(2)}) collective-permute-start(bf16[576,384]{1,0:T(8,128)(2,1)} %get-tuple-element.302), channel_id=1, source_target_pairs={{8,16},{9,17},{10,18},{11,19},{12,20},{13,21},{14,22},{15,23},{16,... | collective-permute-start | bytes 1327112 | tf_op jit(solution)/shard_map/ppermute | solution.py:41
  297.5 7.4 %copy-start.14 = (bf16[576,384]{1,0:T(8,128)(2,1)S(1)}, bf16[576,384]{1,0:T(8,128)(2,1)}, u32[]{:S(2)}) copy-start(bf16[576,384]{1,0:T(8,128)(2,1)} %get-tuple-element.312.a) | copy-start | bytes 1327108
  298.3 12.5 %copy-start.20 = (bf16[48,4096]{1,0:T(8,128)(2,1)S(1)}, bf16[48,4096]{1,0:T(8,128)(2,1)}, u32[]{:S(2)}) copy-start(bf16[48,4096]{1,0:T(8,128)(2,1)} %wg.1) | copy-start | bytes 1179652
  298.3 12.5 %copy-start.21 = (bf16[48,4096]{1,0:T(8,128)(2,1)S(1)}, bf16[48,4096]{1,0:T(8,128)(2,1)}, u32[]{:S(2)}) copy-start(bf16[48,4096]{1,0:T(8,128)(2,1)} %wu.1) | copy-start | bytes 1179652
  298.3 12.5 %copy-start.34 = (bf16[48]{0:T(256)(128)(2,1)S(1)}, bf16[48]{0:T(256)(128)(2,1)}, u32[]{:S(2)}) copy-start(bf16[48]{0:T(256)(128)(2,1)} %param.31) | copy-start | bytes 292
  306.9 18.2 %collective-permute-start.36 = (bf16[48,1536]{1,0:T(8,128)(2,1)}, bf16[48,1536]{1,0:T(8,128)(2,1)S(1)}, u32[]{:S(2)}, u32[]{:S(2)}) collective-permute-start(bf16[48,1536]{1,0:T(8,128)(2,1)} %get-tuple-element.322), channel_id=1, source_target_pairs={{0,0},{8,1},{16,2},{24,3},{1,4},{9,5},{17,6},{25,7},{2,8},{10,9},{... | collective-permute-start | bytes 442376 | tf_op jit(solution)/shard_map/ppermute | solution.py:41
  310.8 12.2 %all-to-all-start = ((bf16[8,48,384]{2,1,0:T(8,128)(2,1)}), bf16[8,48,384]{2,1,0:T(8,128)(2,1)}, u32[]{:S(2)}, u32[]{:S(2)}) async-start(bf16[8,48,384]{2,1,0:T(8,128)(2,1)} %get-tuple-element.160), calls=%async_computation | async-start | bytes 589824 | tf_op jit(solution)/shard_map/cond/branch_1_fun/all_to_all | solution.py:73
  (16 other events, 36.6 us)
Sparse Core Ops, SparseCore 0:
  40.1 41.4 all-gather.2
  83.6 62.3 all-gather.4
  179.6 85.3 reduce-scatter.1

commit v2 on v1

--- a/solution.py
+++ b/solution.py
@@ -838,20 +838,21 @@
     xa, xb, gu0, e01 = unit_of_work(go, gather, xhat, x1, g_low, gu_s)
     attn_full, gu0 = fence(attn_full, gu0)
     wgu = lay.spread(gu0.reshape(KV * rows, wide))
+    d5 = send(d4, lay.outward)
     attn_full = attn_full.reshape(nz, -1, WIDE)
     seq_len = jnp.concatenate([lengths, theirs])
 
-    def forward(meta, seq_len, span_order, xa, xb, attn_full, cos_table, sin_table, hidden_in, e01, d4):
+    def forward(meta, seq_len, span_order, xa, xb, attn_full, cos_table, sin_table, hidden_in, e01):
         e2 = send(e01, lay.second)
         wqkv, qkv, att = kernel_call(
             attention_kernel,
             (shaped(width, WIDE), shaped(4, length, WIDE), shaped(2, tokens // 2, QW)),
             scratch=[pltpu.VMEM((length, width), BF)] + tables,
         )((meta, seq_len, span_order), flat(xa), flat(xb), attn_full, cos_table, sin_table)
-        wqkv, qkv, att, e2 = fence(wqkv, qkv, att, e2)
         wout, mine, other = kernel_call(
             project_kernel, (shaped(QW, width), shaped(tokens // 2, width), shaped(tokens // 2, width))
         )((), att, attn_full)
+        wqkv, qkv, att, wout, mine, other, e2 = fence(wqkv, qkv, att, wout, mine, other, e2)
         got = send(other, lay.core)
         r = halves(plus(mine, got))
         e0123 = jnp.stack([e01, e2])
@@ -865,16 +866,13 @@
             norm_kernel, (shaped(own, width, dtype=F32), shaped(own, width), shaped(own, 1, dtype=F32))
         )((), hidden_in.reshape(own, width), r[0], got)
         m01 = jnp.stack([xm0, send(xm0, lay.first)])
-        m01, d4 = fence(m01, d4)
         m2 = send(m01, lay.second)
-        d5 = send(d4, lay.outward)
-        m2, d5 = fence(m2, d5)
         ma = jnp.stack([m01, m2])
         mb = send(ma, lay.core)
-        return wqkv, qkv, att, wout, residual, inverse_m, flat(ma), flat(mb), flat(e0123), flat(e3), d5
-
-    wqkv, qkv, att, wout, residual, inverse_m, ma, mb, ea, eb, d5 = unit_of_work(
-        go, forward, meta, seq_len, span_order, xa, xb, attn_full, cos_table, sin_table, hidden_in, e01, d4
+        return wqkv, qkv, att, wout, residual, inverse_m, flat(ma), flat(mb), flat(e0123), flat(e3)
+
+    wqkv, qkv, att, wout, residual, inverse_m, ma, mb, ea, eb = unit_of_work(
+        go, forward, meta, seq_len, span_order, xa, xb, attn_full, cos_table, sin_table, hidden_in, e01
     )
     half_rows = shaped(tokens // 2, width)
     low = w_down.shape[0]

time: 335 us -> 327 us (0.976)
  waiting for transfers between devices: 122 us -> 113 us
    ppermute x37, waiting for transfers between devices: 104 us -> 97.2 us  [send(): return lax.ppermute(x, AXES, pairs)]
  transfers between devices with their start and end apart: 43 -> 43, of which waited for: 21 -> 19; matrix products, arithmetic and copies ran while one was open for 8% -> 9% of each run, Pallas kernels for 14% -> 14%
where the time goes in v2:
time: 327 us; the launch traced here: 325 us
  waiting for transfers between devices  113 us (35%)
  starting transfers between devices  75.1 us (23%)
  Pallas kernels  70.8 us (22%)
  blocking collectives  20.1 us (6%)
  other arithmetic  16.3 us (5%)
  local copies, waits for them, and re-layouts  15.8 us (5%)
  between operations  14.1 us (4%)
    ppermute x37, waiting for transfers between devices, send(): return lax.ppermute(x, AXES, pairs)  97.2 us
    ppermute x37, starting transfers between devices, send(): return lax.ppermute(x, AXES, pairs)  58.3 us
    pallas_call x2, Pallas kernels, call(): pl.pallas_call(body, out_shape=outs, in_specs=[SMEM] * len(scalars) + [pl...  36.2 us
    pallas_call x14, Pallas kernels, call(): pl.pallas_call(body, out_shape=outs, in_specs=[SMEM] * len(scalars) + [VM...  34.6 us
    all_to_all x1, blocking collectives, exchange(): lax.all_to_all(x, AXES, split_axis=0, concat_axis=0, tiled=True, axis_ind...  20.1 us
    all_to_all x3, starting transfers between devices, exchange(): lax.all_to_all(x, AXES, split_axis=0, concat_axis=0, tiled=True, axis_ind...  16.7 us
    all_gather x2, waiting for transfers between devices, spread(): lax.all_gather(x, AXES, axis=0, tiled=True, axis_index_groups=self.lines())  10.4 us
  transfers between devices with their start and end apart: 43, of which 19 were waited for; matrix products, arithmetic and copies ran while one was open for 9% of the time, Pallas kernels for 14%

profile of v2, /device:TPU:1, one launch (start us, length us, event | category | flops | bytes accessed | tf_op | source)
XLA Modules:
  0.0 325.1 jit_solution(14107880106501513009)
XLA Ops:
  7.2 2.2 collective-permute-start.19
  10.1 2.0 shard_map.230
  12.0 4.7 %all-to-all-start.2 = ((bf16[8,48,384]{2,1,0:T(8,128)(2,1)}), bf16[8,48,384]{2,1,0:T(8,128)(2,1)S(1)}, u32[]{:S(2)}, u32[]{:S(2)}) async-start(bf16[8,48,384]{2,1,0:T(8,128)(2,1)} %shard_map.230), calls=%async_computation.2 | async-start | bytes 589824 | tf_op jit(solution)/shard_map/all_to_all | solution.py:73
  16.7 5.9 %collective-permute-start.25 = (bf16[48,1536]{1,0:T(8,128)(2,1)}, bf16[48,1536]{1,0:T(8,128)(2,1)}, u32[]{:S(2)}, u32[]{:S(2)}) collective-permute-start(bf16[48,1536]{1,0:T(8,128)(2,1)} %param.30), channel_id=1, source_target_pairs={{0,0},{1,8},{2,16},{3,24},{4,1},{5,9},{6,17},{7,25},{8,2},{9,10},{... | collective-permute-start | bytes 442376 | tf_op jit(solution)/shard_map/ppermute | solution.py:41
  22.7 1.3 collective-permute-start.21
  24.0 1.5 shard_map.231
  25.6 1.9 shard_map.232
  27.6 1.3 collective-permute-start.22
  28.9 1.4 collective-permute-start.23
  33.5 6.4 %collective-permute-done.22.h3 = bf16[128,1536]{1,0:T(8,128)(2,1)S(1)} collective-permute-done((bf16[128,1536]{1,0:T(8,128)(2,1)S(1)}, bf16[128,1536]{1,0:T(8,128)(2,1)S(1)}, u32[]{:S(2)}, u32[]{:S(2)}) %collective-permute-start.22) | collective-permute-done | bytes 393248 | tf_op jit(solution)/shard_map/ppermute | solution.py:41
  40.6 30.4 %conditional.4 = (bf16[2,2,128,1536]{3,2,1,0:T(8,128)(2,1)}, bf16[2,2,128,1536]{3,2,1,0:T(8,128)(2,1)}, bf16[8,48,1024]{2,1,0:T(8,128)(2,1)S(1)}, bf16[2,128,1536]{2,1,0:T(8,128)(2,1)S(1)}) conditional(s32[]{:T(128)} %bitcast.35, () %tuple.59, (bf16[128,1536]{1,0:T(8,128)(2,1)}, bf16[128,1536]{1,0:T(8,128)(2,1)}, bf16[8,48,1024]{2,1,0:T(8,128)(2,1)S(1)}, ...), branch_computations={%region_0.1_spmd, %region_1.2_spmd} | conditional | flops 1572864 | bytes 18874520 | solution.py:48
  41.9 20.1 %all_to_all.18 = bf16[8,48,1024]{2,1,0:T(8,128)(2,1)S(1)} all-to-all(bf16[8,48,1024]{2,1,0:T(8,128)(2,1)S(1)} %get-tuple-element.78), channel_id=1, replica_groups={{0,1,2,3,4,5,6,7},{8,9,10,11,12,13,14,15},{16,17,18,19,20,21,22,23},{24..., dimensions={0} | all-to-all | bytes 1572864 | tf_op jit(solution)/shard_map/cond/branch_1_fun/all_to_all | solution.py:73
  62.0 1.3 pad_maximum_fusion
  64.1 6.9 %collective-permute-done.2 = bf16[128,1536]{1,0:T(8,128)(2,1)S(1)} collective-permute-done((bf16[128,1536]{1,0:T(8,128)(2,1)S(1)}, bf16[128,1536]{1,0:T(8,128)(2,1)S(1)}, u32[]{:S(2)}, u32[]{:S(2)}) %collective-permute-start.2) | collective-permute-done | bytes 393248 | tf_op jit(solution)/shard_map/cond/branch_1_fun/ppermute | solution.py:41
  71.1 10.4 %all-gather.3.cloned.1.call-done = bf16[2304,384]{1,0:T(8,128)(2,1)} async-done(((bf16[576,384]{1,0:T(8,128)(2,1)}), bf16[2304,384]{1,0:T(8,128)(2,1)}) %all-gather.3.cloned.1.call-update) | async-done | bytes 1769488 | tf_op jit(solution)/shard_map/all_gather | solution.py:83
  83.0 66.8 %conditional.5 = (bf16[1536,384]{1,0:T(8,128)(2,1)}, bf16[4,256,384]{2,1,0:T(8,128)(2,1)S(1)}, bf16[2,512,192]{2,1,0:T(8,128)(2,1)S(1)}, bf16[192,1536]{1,0:T(8,...) conditional(s32[]{:T(128)} %bitcast.35, () %tuple.58, ...), branch_computations={%region_2.3_spmd, %region_3.4_spmd} | conditional | flops 3145728 | bytes 68420128 | solution.py:48
  84.2 8.2 %branch_1_fun.6 = (bf16[1536,384]{1,0:T(8,128)(2,1)}, bf16[4,256,384]{2,1,0:T(8,128)(2,1)S(1)}, bf16[2,512,192]{2,1,0:T(8,128)(2,1)S(1)}) custom-call(s32[6]{0:T(128)S(1)} %get-tuple-element.87.meta, s32[4]{0:T(128)S(1)} %get-tuple-element.88.lens, s32[8]{0:T(128)S(1)} %get-tuple-element.89.spans, bf16[512,1536]{1,0:T(8,128)(2,1)} %bitcast.6.xa, ...), custom_call_target="tpu_custom_call" | custom-call | tf_op jit(solution)/shard_map/cond/branch_1_fun/pallas_call | solution.py:306
  92.4 2.7 branch_1_fun.7
  96.1 1.3 pad_maximum_fusion.3
  97.4 1.9 collective-permute-done.4
  101.5 10.1 %collective-permute-done.5 = bf16[256,1536]{1,0:T(8,128)(2,1)S(1)} collective-permute-done((bf16[256,1536]{1,0:T(8,128)(2,1)S(1)}, bf16[256,1536]{1,0:T(8,128)(2,1)S(1)}, u32[]{:S(2)}, u32[]{:S(2)}) %collective-permute-start.5) | collective-permute-done | bytes 786464 | tf_op jit(solution)/shard_map/cond/branch_1_fun/ppermute | solution.py:41
  113.2 6.3 %collective-permute-done.7.b = bf16[128,1536]{1,0:T(8,128)(2,1)S(1)} collective-permute-done((bf16[128,1536]{1,0:T(8,128)(2,1)S(1)}, bf16[128,1536]{1,0:T(8,128)(2,1)S(1)}, u32[]{:S(2)}, u32[]{:S(2)}) %collective-permute-start.7) | collective-permute-done | bytes 393248 | tf_op jit(solution)/shard_map/cond/branch_1_fun/ppermute | solution.py:41
  120.2 2.1 branch_1_fun.8
  123.1 6.5 %collective-permute-done.8 = bf16[128,1536]{1,0:T(8,128)(2,1)S(1)} collective-permute-done((bf16[128,1536]{1,0:T(8,128)(2,1)}, bf16[128,1536]{1,0:T(8,128)(2,1)S(1)}, u32[]{:S(2)}, u32[]{:S(2)}) %collective-permute-start.8) | collective-permute-done | bytes 393248 | tf_op jit(solution)/shard_map/cond/branch_1_fun/ppermute | solution.py:41
  131.9 10.1 %collective-permute-done.9 = bf16[2,128,1536]{2,1,0:T(8,128)(2,1)S(1)} collective-permute-done((bf16[2,128,1536]{2,1,0:T(8,128)(2,1)S(1)}, bf16[2,128,1536]{2,1,0:T(8,128)(2,1)S(1)}, u32[]{:S(2)}, u32[]{:S(2)}) %collective-permute-start.9) | collective-permute-done | bytes 786464 | tf_op jit(solution)/shard_map/cond/branch_1_fun/ppermute | solution.py:41
  143.3 3.1 collective-permute-start.10
  146.4 3.4 %collective-permute-done.10 = bf16[2,2,128,1536]{3,2,1,0:T(8,128)(2,1)} collective-permute-done((bf16[2,2,128,1536]{3,2,1,0:T(8,128)(2,1)}, bf16[2,2,128,1536]{3,2,1,0:T(8,128)(2,1)}, u32[]{:S(2)}, u32[]{:S(2)}) %collective-permute-start.10) | collective-permute-done | bytes 1572896 | tf_op jit(solution)/shard_map/cond/branch_1_fun/ppermute | solution.py:41
  149.8 21.8 %shard_map.233 = (bf16[512,1536]{1,0:T(8,128)(2,1)}, bf16[512,1536]{1,0:T(8,128)(2,1)}, bf16[512,1536]{1,0:T(8,128)(2,1)}, bf16[512,1536]{1,0:T(8,128)(2,1)}, bf16[4,576,1024]{2,1,0:T(8,128)(2,1)}) custom-call(s32[6]{0:T(128)S(1)} %stack.99.meta, bf16[512,1536]{1,0:T(8,128)(2,1)} %get-tuple-element.264.h_ma, bf16[512,1536]{1,0:T(8,128)(2,1)} %get-tuple-element.265.h_mb, ...), custom_call_target="tpu_custom_call" | custom-call | tf_op jit(solution)/shard_map/pallas_call | solution.py:322
  171.6 71.0 %conditional.6 = (f32[128,1536]{1,0:T(8,128)S(1)}, bf16[512,1536]{1,0:T(8,128)(2,1)S(1)}, bf16[512,1536]{1,0:T(8,128)(2,1)S(1)}, bf16[128,1536]{1,0:T(8,128)(2,1...) conditional(s32[]{:T(128)} %bitcast.35, () %tuple.57, ...), branch_computations={%region_4.5_spmd, %region_5.6_spmd} | conditional | flops 5898240 | bytes 107741904 | solution.py:48
  172.1 1.8 convert_element_type.4
  173.9 1.4 collective-permute-done.11
  177.1 10.1 %collective-permute-done.12 = bf16[256,1536]{1,0:T(8,128)(2,1)S(1)} collective-permute-done((bf16[256,1536]{1,0:T(8,128)(2,1)S(1)}, bf16[256,1536]{1,0:T(8,128)(2,1)S(1)}, u32[]{:S(2)}, u32[]{:S(2)}) %collective-permute-start.12) | collective-permute-done | bytes 786464 | tf_op jit(solution)/shard_map/cond/branch_1_fun/ppermute | solution.py:41
  188.8 6.3 %collective-permute-done.13.b = bf16[128,1536]{1,0:T(8,128)(2,1)S(1)} collective-permute-done((bf16[128,1536]{1,0:T(8,128)(2,1)S(1)}, bf16[128,1536]{1,0:T(8,128)(2,1)S(1)}, u32[]{:S(2)}, u32[]{:S(2)}) %collective-permute-start.13) | collective-permute-done | bytes 393248 | tf_op jit(solution)/shard_map/cond/branch_1_fun/ppermute | solution.py:41
  195.8 2.2 branch_1_fun.9
  198.7 6.5 %collective-permute-done.14 = bf16[128,1536]{1,0:T(8,128)(2,1)S(1)} collective-permute-done((bf16[128,1536]{1,0:T(8,128)(2,1)}, bf16[128,1536]{1,0:T(8,128)(2,1)S(1)}, u32[]{:S(2)}, u32[]{:S(2)}) %collective-permute-start.14) | collective-permute-done | bytes 393248 | tf_op jit(solution)/shard_map/cond/branch_1_fun/ppermute | solution.py:41
  207.6 2.4 collective-permute-start.17
  210.1 7.6 %collective-permute-done.15 = bf16[2,128,1536]{2,1,0:T(8,128)(2,1)S(1)} collective-permute-done((bf16[2,128,1536]{2,1,0:T(8,128)(2,1)S(1)}, bf16[2,128,1536]{2,1,0:T(8,128)(2,1)S(1)}, u32[]{:S(2)}, u32[]{:S(2)}) %collective-permute-start.15) | collective-permute-done | bytes 786464 | tf_op jit(solution)/shard_map/cond/branch_1_fun/ppermute | solution.py:41
  217.8 3.4 %collective-permute-start.16 = (bf16[2,2,128,1536]{3,2,1,0:T(8,128)(2,1)S(1)}, bf16[2,2,128,1536]{3,2,1,0:T(8,128)(2,1)S(1)}, u32[]{:S(2)}, u32[]{:S(2)}) collective-permute-start(bf16[2,2,128,1536]{3,2,1,0:T(8,128)(2,1)S(1)} %pad_maximum_fusion.6), channel_id=1, source_target_pairs={{0,1},{1,0},{2,3},{3,2},{4,5},{5,4},{6,7},{7,6},{8,9},{9,8},{10,11... | collective-permute-start | bytes 4718600 | tf_op jit(solution)/shard_map/cond/branch_1_fun/ppermute | solution.py:41
  221.7 2.6 collective-permute-done.16
  226.0 14.4 %branch_1_fun.10 = (bf16[512,1536]{1,0:T(8,128)(2,1)S(1)}, bf16[512,1536]{1,0:T(8,128)(2,1)}, bf16[576,384]{1,0:T(8,128)(2,1)}, bf16[576,384]{1,0:T(8,128)(2,1)}...) custom-call(s32[6]{0:T(128)S(1)} %get-tuple-element.130.meta, s32[4]{0:T(128)S(1)} %get-tuple-element.131.lens, ...), custom_call_target="tpu_custom_call" | custom-call | tf_op jit(solution)/shard_map/cond/branch_1_fun/pallas_call | solution.py:322
  240.4 1.3 bitcast_add_fusion.1
  243.0 3.0 collective-permute-done.28
  249.7 5.9 %collective-permute-start.27 = (bf16[576,384]{1,0:T(8,128)(2,1)S(1)}, bf16[576,384]{1,0:T(8,128)(2,1)}, u32[]{:S(2)}, u32[]{:S(2)}) collective-permute-start(bf16[576,384]{1,0:T(8,128)(2,1)S(1)} %copy-done.13), channel_id=1, source_target_pairs={{0,8},{1,9},{2,10},{3,11},{4,12},{5,13},{6,14},{7,15},{24,16},{25,... | collective-permute-start | bytes 1327112 | tf_op jit(solution)/shard_map/ppermute | solution.py:41
  255.6 2.1 collective-permute-start.31
  258.4 2.1 slice.103
  260.5 3.9 %collective-permute-done.27 = bf16[576,384]{1,0:T(8,128)(2,1)} collective-permute-done((bf16[576,384]{1,0:T(8,128)(2,1)S(1)}, bf16[576,384]{1,0:T(8,128)(2,1)}, u32[]{:S(2)}, u32[]{:S(2)}) %collective-permute-start.27) | collective-permute-done | bytes 442400 | tf_op jit(solution)/shard_map/ppermute | solution.py:41
  264.3 1.9 add.31
  266.2 1.4 collective-permute-start.30
  270.2 5.9 %all-to-all-start.3 = ((bf16[8,48,1024]{2,1,0:T(8,128)(2,1)}), bf16[8,48,1024]{2,1,0:T(8,128)(2,1)S(1)}, u32[]{:S(2)}, u32[]{:S(2)}) async-start(bf16[8,48,1024]{2,1,0:T(8,128)(2,1)} %bitcast.52), calls=%async_computation.4 | async-start | bytes 1572864 | tf_op jit(solution)/shard_map/all_to_all | solution.py:73
  276.1 1.8 slice.105.u
  277.9 2.0 shard_map.235
  279.9 2.3 shard_map.234
  282.2 4.5 %collective-permute-start.34 = (bf16[576,384]{1,0:T(8,128)(2,1)}, bf16[576,384]{1,0:T(8,128)(2,1)}, u32[]{:S(2)}, u32[]{:S(2)}) collective-permute-start(bf16[576,384]{1,0:T(8,128)(2,1)} %get-tuple-element.295), channel_id=1, source_target_pairs={{0,8},{1,9},{2,10},{3,11},{4,12},{5,13},{6,14},{7,15},{8,0},{9,1},... | collective-permute-start | bytes 1327112 | tf_op jit(solution)/shard_map/ppermute | solution.py:41
  286.7 1.4 collective-permute-start.35
  288.1 1.9 shard_map.236
  290.8 2.3 shard_map.237
  293.1 4.3 %collective-permute-done.34.b = bf16[576,384]{1,0:T(8,128)(2,1)} collective-permute-done((bf16[576,384]{1,0:T(8,128)(2,1)}, bf16[576,384]{1,0:T(8,128)(2,1)}, u32[]{:S(2)}, u32[]{:S(2)}) %collective-permute-start.34) | collective-permute-done | bytes 442400 | tf_op jit(solution)/shard_map/ppermute | solution.py:41
  297.4 2.0 shard_map.238
  299.4 3.9 %collective-permute-start.36 = (bf16[48,1536]{1,0:T(8,128)(2,1)}, bf16[48,1536]{1,0:T(8,128)(2,1)S(1)}, u32[]{:S(2)}, u32[]{:S(2)}) collective-permute-start(bf16[48,1536]{1,0:T(8,128)(2,1)} %get-tuple-element.316), channel_id=1, source_target_pairs={{0,0},{8,1},{16,2},{24,3},{1,4},{9,5},{17,6},{25,7},{2,8},{10,9},{... | collective-permute-start | bytes 442376 | tf_op jit(solution)/shard_map/ppermute | solution.py:41
  303.3 12.5 %conditional.7 = (bf16[8,48,384]{2,1,0:T(8,128)(2,1)}, f32[48,4096]{1,0:T(8,128)}, f32[48,4096]{1,0:T(8,128)}, f32[48]{0:T(128)}) conditional(s32[]{:T(128)} %bitcast.35, () %tuple.70, (bf16[8,48,384]{2,1,0:T(8,128)(2,1)}, bf16[8,48,1024]{2,1,0:T(8,128)(2,1)S(1)}, bf16[48,4096]{1,0:T(8,128)(2,1)S(1)}, bf16[48,4096]{1,0:T(8,128)(2,1)S(1)}, ...), branch_computations={%region_7.8_spmd, %region_8.9_spmd} | conditional | bytes 1868014 | solution.py:48
  303.3 6.1 %all-to-all-start = ((bf16[8,48,384]{2,1,0:T(8,128)(2,1)}), bf16[8,48,384]{2,1,0:T(8,128)(2,1)}, u32[]{:S(2)}, u32[]{:S(2)}) async-start(bf16[8,48,384]{2,1,0:T(8,128)(2,1)} %get-tuple-element.156), calls=%async_computation | async-start | bytes 589824 | tf_op jit(solution)/shard_map/cond/branch_1_fun/all_to_all | solution.py:73
  309.4 1.4 branch_1_fun.11
  310.8 4.9 %all-to-all-done = bf16[8,48,384]{2,1,0:T(8,128)(2,1)} async-done(((bf16[8,48,384]{2,1,0:T(8,128)(2,1)}), bf16[8,48,384]{2,1,0:T(8,128)(2,1)}, u32[]{:S(2)}, u32[]{:S(2)}) %all-to-all-start) | async-done | bytes 294944 | tf_op jit(solution)/shard_map/cond/branch_1_fun/all_to_all | solution.py:73
  315.8 2.1 shard_map.239
  (157 shorter events, 38.8 us)
Async XLA Ops:
  7.2 18.4 %copy-start.6 = (bf16[2,64,1536]{2,1,0:T(8,128)(2,1)S(1)}, bf16[2,64,1536]{2,1,0:T(8,128)(2,1)}, u32[]{:S(2)}) copy-start(bf16[2,64,1536]{2,1,0:T(8,128)(2,1)} %param.23) | copy-start | bytes 1179652
  7.2 18.4 %copy-start.33 = (s32[8]{0:T(128)S(1)}, s32[8]{0:T(128)}, u32[]{:S(2)}) copy-start(s32[8]{0:T(128)} %spans.3) | copy-start | bytes 100
  7.2 20.3 %collective-permute-start.19 = (bf16[128,1536]{1,0:T(8,128)(2,1)}, bf16[128,1536]{1,0:T(8,128)(2,1)S(1)}, u32[]{:S(2)}, u32[]{:S(2)}) collective-permute-start(bf16[128,1536]{1,0:T(8,128)(2,1)} %h0.1), channel_id=1, source_target_pairs={{0,8},{1,9},{2,10},{3,11},{4,12},{5,13},{6,14},{7,15},{8,0},{9,1},... | collective-permute-start | bytes 1179656 | tf_op jit(solution)/shard_map/ppermute | solution.py:41
  9.4 18.2 %collective-permute-start.20 = (bf16[128,1536]{1,0:T(8,128)(2,1)}, bf16[128,1536]{1,0:T(8,128)(2,1)S(1)}, u32[]{:S(2)}, u32[]{:S(2)}) collective-permute-start(bf16[128,1536]{1,0:T(8,128)(2,1)} %h0.1), channel_id=1, source_target_pairs={{8,16},{9,17},{10,18},{11,19},{12,20},{13,21},{14,22},{15,23},{16,... | collective-permute-start | bytes 1179656 | tf_op jit(solution)/shard_map/ppermute | solution.py:41
  12.0 15.5 %all-to-all-start.2 = ((bf16[8,48,384]{2,1,0:T(8,128)(2,1)}), bf16[8,48,384]{2,1,0:T(8,128)(2,1)S(1)}, u32[]{:S(2)}, u32[]{:S(2)}) async-start(bf16[8,48,384]{2,1,0:T(8,128)(2,1)} %shard_map.230), calls=%async_computation.2 | async-start | bytes 589824 | tf_op jit(solution)/shard_map/all_to_all | solution.py:73
  16.7 64.8 %all-gather.3.cloned.1.call-start = ((), (), s32[]{:S(2)}) async-start(), calls=%async_computation.5 | async-start | bytes 2211840 | tf_op jit(solution)/shard_map/all_gather | solution.py:83
  16.7 13.7 %collective-permute-start.25 = (bf16[48,1536]{1,0:T(8,128)(2,1)}, bf16[48,1536]{1,0:T(8,128)(2,1)}, u32[]{:S(2)}, u32[]{:S(2)}) collective-permute-start(bf16[48,1536]{1,0:T(8,128)(2,1)} %param.30), channel_id=1, source_target_pairs={{0,0},{1,8},{2,16},{3,24},{4,1},{5,9},{6,17},{7,25},{8,2},{9,10},{... | collective-permute-start | bytes 442376 | tf_op jit(solution)/shard_map/ppermute | solution.py:41
  22.7 4.9 %collective-permute-start.21 = (s32[2]{0:T(128)}, s32[2]{0:T(128)S(1)}, u32[]{:S(2)}, u32[]{:S(2)}) collective-permute-start(s32[2]{0:T(128)} %lens.3), channel_id=1, source_target_pairs={{0,4},{1,5},{2,6},{3,7},{4,0},{5,1},{6,2},{7,3},{8,12},{9,13},{10,... | collective-permute-start | bytes 32 | tf_op jit(solution)/shard_map/ppermute | solution.py:41
  24.0 16.0 %copy-start.35 = (s32[2]{0:T(128)S(1)}, s32[2]{0:T(128)}, u32[]{:S(2)}) copy-start(s32[2]{0:T(128)} %lens.3) | copy-start | bytes 28
  27.5 12.5 %copy-start.24 = (bf16[128,1536]{1,0:T(8,128)(2,1)}, bf16[128,1536]{1,0:T(8,128)(2,1)S(1)}, u32[]{:S(2)}) copy-start(bf16[128,1536]{1,0:T(8,128)(2,1)S(1)} %get-tuple-element.256) | copy-start | bytes 1179652
  27.5 12.5 %copy-start.28 = (bf16[128,1536]{1,0:T(8,128)(2,1)}, bf16[128,1536]{1,0:T(8,128)(2,1)S(1)}, u32[]{:S(2)}) copy-start(bf16[128,1536]{1,0:T(8,128)(2,1)S(1)} %collective-permute-done.19.h1) | copy-start | bytes 1179652
  27.6 12.5 %copy-start.29 = (bf16[128,1536]{1,0:T(8,128)(2,1)}, bf16[128,1536]{1,0:T(8,128)(2,1)S(1)}, u32[]{:S(2)}) copy-start(bf16[128,1536]{1,0:T(8,128)(2,1)S(1)} %collective-permute-done.20.h2) | copy-start | bytes 1179652
  27.6 12.3 %collective-permute-start.22 = (bf16[128,1536]{1,0:T(8,128)(2,1)S(1)}, bf16[128,1536]{1,0:T(8,128)(2,1)S(1)}, u32[]{:S(2)}, u32[]{:S(2)}) collective-permute-start(bf16[128,1536]{1,0:T(8,128)(2,1)S(1)} %collective-permute-done.20.h2), channel_id=1, source_target_pairs={{8,0},{9,1},{10,2},{11,3},{12,4},{13,5},{14,6},{15,7},{16,24},{17,... | collective-permute-start | bytes 1179656 | tf_op jit(solution)/shard_map/ppermute | solution.py:41
  28.9 11.0 %collective-permute-start.23 = (bf16[128,1536]{1,0:T(8,128)(2,1)S(1)}, bf16[128,1536]{1,0:T(8,128)(2,1)}, u32[]{:S(2)}, u32[]{:S(2)}) collective-permute-start(bf16[128,1536]{1,0:T(8,128)(2,1)S(1)} %collective-permute-done.19.h1), channel_id=1, source_target_pairs={{8,16},{9,17},{10,18},{11,19},{12,20},{13,21},{14,22},{15,23},{16,... | collective-permute-start | bytes 1179656 | tf_op jit(solution)/shard_map/ppermute | solution.py:41
  30.3 9.6 %collective-permute-start.24 = (bf16[128,1536]{1,0:T(8,128)(2,1)}, bf16[128,1536]{1,0:T(8,128)(2,1)}, u32[]{:S(2)}, u32[]{:S(2)}) collective-permute-start(bf16[128,1536]{1,0:T(8,128)(2,1)} %get-tuple-element.250), channel_id=1, source_target_pairs={{0,4},{1,3},{2,6},{3,1},{4,0},{5,7},{6,2},{7,5},{8,12},{9,11},{10,... | collective-permute-start | bytes 1179656 | tf_op jit(solution)/shard_map/ppermute | solution.py:41
  33.5 6.4 %copy-start.27 = (bf16[576,384]{1,0:T(8,128)(2,1)}, bf16[576,384]{1,0:T(8,128)(2,1)S(1)}, u32[]{:S(2)}) copy-start(bf16[576,384]{1,0:T(8,128)(2,1)S(1)} %slice_dynamic-update-slice_fusion) | copy-start | bytes 1327108
  39.9 109.9 %all-gather.5.cloned.1.call-start = ((), (), s32[]{:S(2)}) async-start(), calls=%async_computation.6 | async-start | bytes 3932160 | tf_op jit(solution)/shard_map/all_gather | solution.py:83
  41.8 20.1 %collective-permute-start = (bf16[2,128,1536]{2,1,0:T(8,128)(2,1)S(1)}, bf16[2,128,1536]{2,1,0:T(8,128)(2,1)S(1)}, u32[]{:S(2)}, u32[]{:S(2)}) collective-permute-start(bf16[2,128,1536]{2,1,0:T(8,128)(2,1)S(1)} %pad_maximum_fusion.1), channel_id=1, source_target_pairs={{0,2},{1,5},{2,0},{3,7},{4,6},{5,1},{6,4},{7,3},{8,10},{9,13},{10,... | collective-permute-start | bytes 2359304 | tf_op jit(solution)/shard_map/cond/branch_1_fun/ppermute | solution.py:41
  63.3 7.7 %collective-permute-start.1 = (bf16[2,2,128,1536]{3,2,1,0:T(8,128)(2,1)}, bf16[2,2,128,1536]{3,2,1,0:T(8,128)(2,1)}, u32[]{:S(2)}, u32[]{:S(2)}) collective-permute-start(bf16[2,2,128,1536]{3,2,1,0:T(8,128)(2,1)} %pad_maximum_fusion), channel_id=1, source_target_pairs={{0,1},{1,0},{2,3},{3,2},{4,5},{5,4},{6,7},{7,6},{8,9},{9,8},{10,11... | collective-permute-start | bytes 4718600 | tf_op jit(solution)/shard_map/cond/branch_1_fun/ppermute | solution.py:41
  63.9 7.0 %collective-permute-start.2 = (bf16[128,1536]{1,0:T(8,128)(2,1)S(1)}, bf16[128,1536]{1,0:T(8,128)(2,1)S(1)}, u32[]{:S(2)}, u32[]{:S(2)}) collective-permute-start(bf16[128,1536]{1,0:T(8,128)(2,1)S(1)} %get-tuple-element.82), channel_id=1, source_target_pairs={{0,4},{1,3},{2,6},{3,1},{4,0},{5,7},{6,2},{7,5},{8,12},{9,11},{10,... | collective-permute-start | bytes 1179656 | tf_op jit(solution)/shard_map/cond/branch_1_fun/ppermute | solution.py:41
  71.1 10.5 %copy-start.7 = (bf16[8,48,1024]{2,1,0:T(8,128)(2,1)}, bf16[8,48,1024]{2,1,0:T(8,128)(2,1)S(1)}, u32[]{:S(2)}) copy-start(bf16[8,48,1024]{2,1,0:T(8,128)(2,1)S(1)} %get-tuple-element.268) | copy-start | bytes 2359300
  81.5 176.9 %reduce-scatter.2.cloned.1.call-start = ((), (), s32[]{:S(2)}) async-start(), calls=%async_computation.7 | async-start | bytes 5898240 | tf_op jit(solution)/shard_map/reduce_scatter | solution.py:89
  81.6 68.2 %collective-permute-start.26 = (bf16[128,1536]{1,0:T(8,128)(2,1)}, bf16[128,1536]{1,0:T(8,128)(2,1)}, u32[]{:S(2)}, u32[]{:S(2)}) collective-permute-start(bf16[128,1536]{1,0:T(8,128)(2,1)} %collective-permute-done.23.h4), channel_id=1, source_target_pairs={{8,0},{9,1},{10,2},{11,3},{12,4},{13,5},{14,6},{15,7},{16,24},{17,... | collective-permute-start | bytes 1179656 | tf_op jit(solution)/shard_map/ppermute | solution.py:41
  83.0 12.2 %collective-permute-start.3 = (bf16[2,128,1536]{2,1,0:T(8,128)(2,1)S(1)}, bf16[2,128,1536]{2,1,0:T(8,128)(2,1)S(1)}, u32[]{:S(2)}, u32[]{:S(2)}) collective-permute-start(bf16[2,128,1536]{2,1,0:T(8,128)(2,1)S(1)} %get-tuple-element.101), channel_id=1, source_target_pairs={{0,2},{1,5},{2,0},{3,7},{4,6},{5,1},{6,4},{7,3},{8,10},{9,13},{10,... | collective-permute-start | bytes 2359304 | tf_op jit(solution)/shard_map/cond/branch_1_fun/ppermute | solution.py:41
  84.2 8.3 %copy-start = (bf16[2304,384]{1,0:T(8,128)(2,1)S(1)}, bf16[2304,384]{1,0:T(8,128)(2,1)}, u32[]{:S(2)}) copy-start(bf16[2304,384]{1,0:T(8,128)(2,1)} %get-tuple-element.92) | copy-start | bytes 5308420 | tf_op jit(solution)/shard_map/cond
  92.4 5.0 %copy-start.4 = (bf16[2,512,192]{2,1,0:T(8,128)(2,1)}, bf16[2,512,192]{2,1,0:T(8,128)(2,1)S(1)}, u32[]{:S(2)}) copy-start(bf16[2,512,192]{2,1,0:T(8,128)(2,1)S(1)} %get-tuple-element.351.att) | copy-start | bytes 1179652 | tf_op jit(solution)/shard_map/cond
  95.1 4.2 %collective-permute-start.4 = (bf16[512,1536]{1,0:T(8,128)(2,1)}, bf16[512,1536]{1,0:T(8,128)(2,1)S(1)}, u32[]{:S(2)}, u32[]{:S(2)}) collective-permute-start(bf16[512,1536]{1,0:T(8,128)(2,1)} %get-tuple-element.108), channel_id=1, source_target_pairs={{0,1},{1,0},{2,3},{3,2},{4,5},{5,4},{6,7},{7,6},{8,9},{9,8},{10,11... | collective-permute-start | bytes 4718600 | tf_op jit(solution)/shard_map/cond/branch_1_fun/ppermute | solution.py:41
  99.7 11.8 %collective-permute-start.6 = (bf16[2,2,128,1536]{3,2,1,0:T(8,128)(2,1)}, bf16[2,2,128,1536]{3,2,1,0:T(8,128)(2,1)}, u32[]{:S(2)}, u32[]{:S(2)}) collective-permute-start(bf16[2,2,128,1536]{3,2,1,0:T(8,128)(2,1)} %pad_maximum_fusion.3), channel_id=1, source_target_pairs={{0,1},{1,0},{2,3},{3,2},{4,5},{5,4},{6,7},{7,6},{8,9},{9,8},{10,11... | collective-permute-start | bytes 4718600 | tf_op jit(solution)/shard_map/cond/branch_1_fun/ppermute | solution.py:41
  100.2 11.3 %collective-permute-start.5 = (bf16[256,1536]{1,0:T(8,128)(2,1)S(1)}, bf16[256,1536]{1,0:T(8,128)(2,1)S(1)}, u32[]{:S(2)}, u32[]{:S(2)}) collective-permute-start(bf16[256,1536]{1,0:T(8,128)(2,1)S(1)} %slice_bitcast_fusion), channel_id=1, source_target_pairs={{0,2},{1,5},{2,0},{3,7},{4,6},{5,1},{6,4},{7,3},{8,10},{9,13},{10,... | collective-permute-start | bytes 2359304 | tf_op jit(solution)/shard_map/cond/branch_1_fun/ppermute | solution.py:41
  112.4 7.0 %collective-permute-start.7 = (bf16[128,1536]{1,0:T(8,128)(2,1)S(1)}, bf16[128,1536]{1,0:T(8,128)(2,1)S(1)}, u32[]{:S(2)}, u32[]{:S(2)}) collective-permute-start(bf16[128,1536]{1,0:T(8,128)(2,1)S(1)} %get-tuple-element.323), channel_id=1, source_target_pairs={{0,4},{1,3},{2,6},{3,1},{4,0},{5,7},{6,2},{7,5},{8,12},{9,11},{10,... | collective-permute-start | bytes 1179656 | tf_op jit(solution)/shard_map/cond/branch_1_fun/ppermute | solution.py:41
  122.3 7.2 %collective-permute-start.8 = (bf16[128,1536]{1,0:T(8,128)(2,1)}, bf16[128,1536]{1,0:T(8,128)(2,1)S(1)}, u32[]{:S(2)}, u32[]{:S(2)}) collective-permute-start(bf16[128,1536]{1,0:T(8,128)(2,1)} %get-tuple-element.116), channel_id=1, source_target_pairs={{0,4},{1,3},{2,6},{3,1},{4,0},{5,7},{6,2},{7,5},{8,12},{9,11},{10,... | collective-permute-start | bytes 1179656 | tf_op jit(solution)/shard_map/cond/branch_1_fun/ppermute | solution.py:41
  130.7 11.3 %collective-permute-start.9 = (bf16[2,128,1536]{2,1,0:T(8,128)(2,1)S(1)}, bf16[2,128,1536]{2,1,0:T(8,128)(2,1)S(1)}, u32[]{:S(2)}, u32[]{:S(2)}) collective-permute-start(bf16[2,128,1536]{2,1,0:T(8,128)(2,1)S(1)} %get-tuple-element.322), channel_id=1, source_target_pairs={{0,2},{1,5},{2,0},{3,7},{4,6},{5,1},{6,4},{7,3},{8,10},{9,13},{10,... | collective-permute-start | bytes 2359304 | tf_op jit(solution)/shard_map/cond/branch_1_fun/ppermute | solution.py:41
  142.0 7.8 %copy-start.5 = (bf16[2,512,192]{2,1,0:T(8,128)(2,1)S(1)}, bf16[2,512,192]{2,1,0:T(8,128)(2,1)}, u32[]{:S(2)}) copy-start(bf16[2,512,192]{2,1,0:T(8,128)(2,1)} %copy-done.4) | copy-start | bytes 1179652 | tf_op jit(solution)/shard_map/cond
  143.3 6.5 %collective-permute-start.10 = (bf16[2,2,128,1536]{3,2,1,0:T(8,128)(2,1)}, bf16[2,2,128,1536]{3,2,1,0:T(8,128)(2,1)}, u32[]{:S(2)}, u32[]{:S(2)}) collective-permute-start(bf16[2,2,128,1536]{3,2,1,0:T(8,128)(2,1)} %pad_maximum_fusion.4), channel_id=1, source_target_pairs={{0,1},{1,0},{2,3},{3,2},{4,5},{5,4},{6,7},{7,6},{8,9},{9,8},{10,11... | collective-permute-start | bytes 4718600 | tf_op jit(solution)/shard_map/cond/branch_1_fun/ppermute | solution.py:41
  171.6 3.7 %collective-permute-start.11 = (bf16[512,1536]{1,0:T(8,128)(2,1)}, bf16[512,1536]{1,0:T(8,128)(2,1)S(1)}, u32[]{:S(2)}, u32[]{:S(2)}) collective-permute-start(bf16[512,1536]{1,0:T(8,128)(2,1)} %get-tuple-element.121), channel_id=1, source_target_pairs={{0,1},{1,0},{2,3},{3,2},{4,5},{5,4},{6,7},{7,6},{8,9},{9,8},{10,11... | collective-permute-start | bytes 4718600 | tf_op jit(solution)/shard_map/cond/branch_1_fun/ppermute | solution.py:41
  175.9 20.0 %copy-start.25 = (bf16[128,1536]{1,0:T(8,128)(2,1)S(1)}, bf16[128,1536]{1,0:T(8,128)(2,1)}, u32[]{:S(2)}) copy-start(bf16[128,1536]{1,0:T(8,128)(2,1)} %get-tuple-element.118.g_res) | copy-start | bytes 1179652 | tf_op jit(solution)/shard_map/cond
  175.9 11.3 %collective-permute-start.12 = (bf16[256,1536]{1,0:T(8,128)(2,1)S(1)}, bf16[256,1536]{1,0:T(8,128)(2,1)S(1)}, u32[]{:S(2)}, u32[]{:S(2)}) collective-permute-start(bf16[256,1536]{1,0:T(8,128)(2,1)S(1)} %slice.93), channel_id=1, source_target_pairs={{0,2},{1,5},{2,0},{3,7},{4,6},{5,1},{6,4},{7,3},{8,10},{9,13},{10,... | collective-permute-start | bytes 2359304 | tf_op jit(solution)/shard_map/cond/branch_1_fun/ppermute | solution.py:41
  188.1 7.0 %collective-permute-start.13 = (bf16[128,1536]{1,0:T(8,128)(2,1)S(1)}, bf16[128,1536]{1,0:T(8,128)(2,1)S(1)}, u32[]{:S(2)}, u32[]{:S(2)}) collective-permute-start(bf16[128,1536]{1,0:T(8,128)(2,1)S(1)} %get-tuple-element.329), channel_id=1, source_target_pairs={{0,4},{1,3},{2,6},{3,1},{4,0},{5,7},{6,2},{7,5},{8,12},{9,11},{10,... | collective-permute-start | bytes 1179656 | tf_op jit(solution)/shard_map/cond/branch_1_fun/ppermute | solution.py:41
  198.0 9.6 %copy-start.36 = (bf16[512,1536]{1,0:T(8,128)(2,1)S(1)}, bf16[512,1536]{1,0:T(8,128)(2,1)}, u32[]{:S(2)}) copy-start(bf16[512,1536]{1,0:T(8,128)(2,1)} %get-tuple-element.128) | copy-start | bytes 4718596 | tf_op jit(solution)/shard_map/cond
  198.0 7.2 %collective-permute-start.14 = (bf16[128,1536]{1,0:T(8,128)(2,1)}, bf16[128,1536]{1,0:T(8,128)(2,1)S(1)}, u32[]{:S(2)}, u32[]{:S(2)}) collective-permute-start(bf16[128,1536]{1,0:T(8,128)(2,1)} %get-tuple-element.126), channel_id=1, source_target_pairs={{0,4},{1,3},{2,6},{3,1},{4,0},{5,7},{6,2},{7,5},{8,12},{9,11},{10,... | collective-permute-start | bytes 1179656 | tf_op jit(solution)/shard_map/cond/branch_1_fun/ppermute | solution.py:41
  206.4 11.3 %collective-permute-start.15 = (bf16[2,128,1536]{2,1,0:T(8,128)(2,1)S(1)}, bf16[2,128,1536]{2,1,0:T(8,128)(2,1)S(1)}, u32[]{:S(2)}, u32[]{:S(2)}) collective-permute-start(bf16[2,128,1536]{2,1,0:T(8,128)(2,1)S(1)} %get-tuple-element.328), channel_id=1, source_target_pairs={{0,2},{1,5},{2,0},{3,7},{4,6},{5,1},{6,4},{7,3},{8,10},{9,13},{10,... | collective-permute-start | bytes 2359304 | tf_op jit(solution)/shard_map/cond/branch_1_fun/ppermute | solution.py:41
  207.6 13.7 %collective-permute-start.17 = (bf16[512,1536]{1,0:T(8,128)(2,1)S(1)}, bf16[512,1536]{1,0:T(8,128)(2,1)S(1)}, u32[]{:S(2)}, u32[]{:S(2)}) collective-permute-start(bf16[512,1536]{1,0:T(8,128)(2,1)S(1)} %copy-done.36), channel_id=1, source_target_pairs={{0,1},{1,0},{2,3},{3,2},{4,5},{5,4},{6,7},{7,6},{8,9},{9,8},{10,11... | collective-permute-start | bytes 4718600 | tf_op jit(solution)/shard_map/cond/branch_1_fun/ppermute | solution.py:41
  217.8 6.5 %collective-permute-start.16 = (bf16[2,2,128,1536]{3,2,1,0:T(8,128)(2,1)S(1)}, bf16[2,2,128,1536]{3,2,1,0:T(8,128)(2,1)S(1)}, u32[]{:S(2)}, u32[]{:S(2)}) collective-permute-start(bf16[2,2,128,1536]{3,2,1,0:T(8,128)(2,1)S(1)} %pad_maximum_fusion.6), channel_id=1, source_target_pairs={{0,1},{1,0},{2,3},{3,2},{4,5},{5,4},{6,7},{7,6},{8,9},{9,8},{10,11... | collective-permute-start | bytes 4718600 | tf_op jit(solution)/shard_map/cond/branch_1_fun/ppermute | solution.py:41
  224.4 16.0 %collective-permute-start.18 = (bf16[256,1536]{1,0:T(8,128)(2,1)S(1)}, bf16[256,1536]{1,0:T(8,128)(2,1)}, u32[]{:S(2)}, u32[]{:S(2)}) collective-permute-start(bf16[256,1536]{1,0:T(8,128)(2,1)S(1)} %slice_bitcast_fusion.1), channel_id=1, source_target_pairs={{0,2},{1,5},{2,0},{3,7},{4,6},{5,1},{6,4},{7,3},{8,10},{9,13},{10,... | collective-permute-start | bytes 2359304 | tf_op jit(solution)/shard_map/cond/branch_1_fun/ppermute | solution.py:41
  242.5 3.5 %collective-permute-start.28 = (bf16[512,1536]{1,0:T(8,128)(2,1)S(1)}, bf16[512,1536]{1,0:T(8,128)(2,1)S(1)}, u32[]{:S(2)}, u32[]{:S(2)}) collective-permute-start(bf16[512,1536]{1,0:T(8,128)(2,1)S(1)} %get-tuple-element.283), channel_id=1, source_target_pairs={{0,1},{1,0},{2,3},{3,2},{4,5},{5,4},{6,7},{7,6},{8,9},{9,8},{10,11... | collective-permute-start | bytes 4718600 | tf_op jit(solution)/shard_map/ppermute | solution.py:41
  248.5 19.1 %copy-start.2 = (bf16[512,1536]{1,0:T(8,128)(2,1)S(1)}, bf16[512,1536]{1,0:T(8,128)(2,1)}, u32[]{:S(2)}) copy-start(bf16[512,1536]{1,0:T(8,128)(2,1)} %copy-done.1) | copy-start | bytes 4718596
  248.5 15.8 %collective-permute-start.29 = (bf16[256,1536]{1,0:T(8,128)(2,1)}, bf16[256,1536]{1,0:T(8,128)(2,1)}, u32[]{:S(2)}, u32[]{:S(2)}) collective-permute-start(bf16[256,1536]{1,0:T(8,128)(2,1)} %slice.102), channel_id=1, source_target_pairs={{0,2},{1,5},{2,0},{3,7},{4,6},{5,1},{6,4},{7,3},{8,10},{9,13},{10,... | collective-permute-start | bytes 2359304 | tf_op jit(solution)/shard_map/ppermute | solution.py:41
  249.7 14.6 %collective-permute-start.27 = (bf16[576,384]{1,0:T(8,128)(2,1)S(1)}, bf16[576,384]{1,0:T(8,128)(2,1)}, u32[]{:S(2)}, u32[]{:S(2)}) collective-permute-start(bf16[576,384]{1,0:T(8,128)(2,1)S(1)} %copy-done.13), channel_id=1, source_target_pairs={{0,8},{1,9},{2,10},{3,11},{4,12},{5,13},{6,14},{7,15},{24,16},{25,... | collective-permute-start | bytes 1327112 | tf_op jit(solution)/shard_map/ppermute | solution.py:41
  255.6 24.3 %collective-permute-start.31 = (bf16[576,384]{1,0:T(8,128)(2,1)}, bf16[576,384]{1,0:T(8,128)(2,1)}, u32[]{:S(2)}, u32[]{:S(2)}) collective-permute-start(bf16[576,384]{1,0:T(8,128)(2,1)} %get-tuple-element.289.c), channel_id=1, source_target_pairs={{0,8},{1,9},{2,10},{3,11},{4,12},{5,13},{6,14},{7,15},{24,16},{25,... | collective-permute-start | bytes 1327112 | tf_op jit(solution)/shard_map/ppermute | solution.py:41
  257.7 22.2 %collective-permute-start.33 = (bf16[128,1536]{1,0:T(8,128)(2,1)}, bf16[128,1536]{1,0:T(8,128)(2,1)}, u32[]{:S(2)}, u32[]{:S(2)}) collective-permute-start(bf16[128,1536]{1,0:T(8,128)(2,1)} %get-tuple-element.292), channel_id=1, source_target_pairs={{0,4},{1,3},{2,6},{3,1},{4,0},{5,7},{6,2},{7,5},{8,12},{9,11},{10,... | collective-permute-start | bytes 1179656 | tf_op jit(solution)/shard_map/ppermute | solution.py:41
  266.2 13.7 %collective-permute-start.30 = (bf16[576,384]{1,0:T(8,128)(2,1)}, bf16[576,384]{1,0:T(8,128)(2,1)}, u32[]{:S(2)}, u32[]{:S(2)}) collective-permute-start(bf16[576,384]{1,0:T(8,128)(2,1)} %add.31), channel_id=1, source_target_pairs={{8,16},{9,17},{10,18},{11,19},{12,20},{13,21},{14,22},{15,23},{16,... | collective-permute-start | bytes 1327112 | tf_op jit(solution)/shard_map/ppermute | solution.py:41
  269.6 10.3 %collective-permute-start.32 = (bf16[128,1536]{1,0:T(8,128)(2,1)}, bf16[128,1536]{1,0:T(8,128)(2,1)}, u32[]{:S(2)}, u32[]{:S(2)}) collective-permute-start(bf16[128,1536]{1,0:T(8,128)(2,1)} %slice.104), channel_id=1, source_target_pairs={{0,4},{1,3},{2,6},{3,1},{4,0},{5,7},{6,2},{7,5},{8,12},{9,11},{10,... | collective-permute-start | bytes 1179656 | tf_op jit(solution)/shard_map/ppermute | solution.py:41
  270.2 9.7 %copy-start.12 = (bf16[576,384]{1,0:T(8,128)(2,1)S(1)}, bf16[576,384]{1,0:T(8,128)(2,1)}, u32[]{:S(2)}) copy-start(bf16[576,384]{1,0:T(8,128)(2,1)} %get-tuple-element.281.a) | copy-start | bytes 1327108
  270.2 22.9 %all-to-all-start.3 = ((bf16[8,48,1024]{2,1,0:T(8,128)(2,1)}), bf16[8,48,1024]{2,1,0:T(8,128)(2,1)S(1)}, u32[]{:S(2)}, u32[]{:S(2)}) async-start(bf16[8,48,1024]{2,1,0:T(8,128)(2,1)} %bitcast.52), calls=%async_computation.4 | async-start | bytes 1572864 | tf_op jit(solution)/shard_map/all_to_all | solution.py:73
  277.9 10.2 %copy-start.23 = (bf16[128,1536]{1,0:T(8,128)(2,1)S(1)}, bf16[128,1536]{1,0:T(8,128)(2,1)}, u32[]{:S(2)}) copy-start(bf16[128,1536]{1,0:T(8,128)(2,1)} %copy-done.22) | copy-start | bytes 1179652
  282.2 8.6 %copy-start.9 = (f32[128,1536]{1,0:T(8,128)S(1)}, f32[128,1536]{1,0:T(8,128)}, u32[]{:S(2)}) copy-start(f32[128,1536]{1,0:T(8,128)} %copy-done.8) | copy-start | bytes 2359300
  282.2 15.2 %collective-permute-start.34 = (bf16[576,384]{1,0:T(8,128)(2,1)}, bf16[576,384]{1,0:T(8,128)(2,1)}, u32[]{:S(2)}, u32[]{:S(2)}) collective-permute-start(bf16[576,384]{1,0:T(8,128)(2,1)} %get-tuple-element.295), channel_id=1, source_target_pairs={{0,8},{1,9},{2,10},{3,11},{4,12},{5,13},{6,14},{7,15},{8,0},{9,1},... | collective-permute-start | bytes 1327112 | tf_op jit(solution)/shard_map/ppermute | solution.py:41
  286.7 10.7 %collective-permute-start.35 = (bf16[576,384]{1,0:T(8,128)(2,1)}, bf16[576,384]{1,0:T(8,128)(2,1)}, u32[]{:S(2)}, u32[]{:S(2)}) collective-permute-start(bf16[576,384]{1,0:T(8,128)(2,1)} %get-tuple-element.296), channel_id=1, source_target_pairs={{8,16},{9,17},{10,18},{11,19},{12,20},{13,21},{14,22},{15,23},{16,... | collective-permute-start | bytes 1327112 | tf_op jit(solution)/shard_map/ppermute | solution.py:41
  290.0 7.4 %copy-start.14 = (bf16[576,384]{1,0:T(8,128)(2,1)S(1)}, bf16[576,384]{1,0:T(8,128)(2,1)}, u32[]{:S(2)}) copy-start(bf16[576,384]{1,0:T(8,128)(2,1)} %get-tuple-element.306.a) | copy-start | bytes 1327108
  290.8 12.5 %copy-start.20 = (bf16[48,4096]{1,0:T(8,128)(2,1)S(1)}, bf16[48,4096]{1,0:T(8,128)(2,1)}, u32[]{:S(2)}) copy-start(bf16[48,4096]{1,0:T(8,128)(2,1)} %wg.1) | copy-start | bytes 1179652
  290.8 12.5 %copy-start.21 = (bf16[48,4096]{1,0:T(8,128)(2,1)S(1)}, bf16[48,4096]{1,0:T(8,128)(2,1)}, u32[]{:S(2)}) copy-start(bf16[48,4096]{1,0:T(8,128)(2,1)} %wu.1) | copy-start | bytes 1179652
  290.8 12.5 %copy-start.34 = (bf16[48]{0:T(256)(128)(2,1)S(1)}, bf16[48]{0:T(256)(128)(2,1)}, u32[]{:S(2)}) copy-start(bf16[48]{0:T(256)(128)(2,1)} %param.31) | copy-start | bytes 292
  299.4 18.4 %collective-permute-start.36 = (bf16[48,1536]{1,0:T(8,128)(2,1)}, bf16[48,1536]{1,0:T(8,128)(2,1)S(1)}, u32[]{:S(2)}, u32[]{:S(2)}) collective-permute-start(bf16[48,1536]{1,0:T(8,128)(2,1)} %get-tuple-element.316), channel_id=1, source_target_pairs={{0,0},{8,1},{16,2},{24,3},{1,4},{9,5},{17,6},{25,7},{2,8},{10,9},{... | collective-permute-start | bytes 442376 | tf_op jit(solution)/shard_map/ppermute | solution.py:41
  303.3 12.4 %all-to-all-start = ((bf16[8,48,384]{2,1,0:T(8,128)(2,1)}), bf16[8,48,384]{2,1,0:T(8,128)(2,1)}, u32[]{:S(2)}, u32[]{:S(2)}) async-start(bf16[8,48,384]{2,1,0:T(8,128)(2,1)} %get-tuple-element.156), calls=%async_computation | async-start | bytes 589824 | tf_op jit(solution)/shard_map/cond/branch_1_fun/all_to_all | solution.py:73
  (16 other events, 36.6 us)
Sparse Core Ops, SparseCore 0:
  40.1 41.4 all-gather.2
  83.6 62.3 all-gather.4
  171.7 85.5 reduce-scatter.1

commit v3 on v2

--- a/solution.py
+++ b/solution.py
@@ -566,9 +566,12 @@
     lax.fori_loop(0, 4, one, 0, unroll=True)
 
 
-def project_kernel(att, full, wout, mine, theirs):
+def project_kernel(att, full, wout, theirs):
     fetch_out(full, wout)
     theirs[...] = dot(att[1], wout[...]).astype(BF)
+
+
+def project_own_kernel(att, wout, mine):
     mine[...] = dot(att[0], wout[...]).astype(BF)
 
 
@@ -849,11 +852,11 @@
             (shaped(width, WIDE), shaped(4, length, WIDE), shaped(2, tokens // 2, QW)),
             scratch=[pltpu.VMEM((length, width), BF)] + tables,
         )((meta, seq_len, span_order), flat(xa), flat(xb), attn_full, cos_table, sin_table)
-        wout, mine, other = kernel_call(
-            project_kernel, (shaped(QW, width), shaped(tokens // 2, width), shaped(tokens // 2, width))
-        )((), att, attn_full)
-        wqkv, qkv, att, wout, mine, other, e2 = fence(wqkv, qkv, att, wout, mine, other, e2)
+        wout, other = kernel_call(project_kernel, (shaped(QW, width), shaped(tokens // 2, width)))((), att, attn_full)
+        wqkv, qkv, att, wout, other, e2 = fence(wqkv, qkv, att, wout, other, e2)
         got = send(other, lay.core)
+        mine = kernel_call(project_own_kernel, shaped(tokens // 2, width))((), att, wout)
+        got, mine = fence(got, mine)
         r = halves(plus(mine, got))
         e0123 = jnp.stack([e01, e2])
         r, e0123 = fence(r, e0123)

time: 327 us -> 329 us (level)
  waiting for transfers between devices: 113 us -> 107 us
  starting transfers between devices: 75.1 us -> 79.5 us
    ppermute x37, waiting for transfers between devices: 97.2 us -> 91.9 us  [send(): return lax.ppermute(x, AXES, pairs)]
    ppermute x37, starting transfers between devices: 58.3 us -> 63.2 us  [send(): return lax.ppermute(x, AXES, pairs)]
    pallas_call x14 -> x15, Pallas kernels: 34.6 us -> 36.5 us  [call(): pl.pallas_call(body, out_shape=outs, in_specs=[SMEM] * len(scalars) + [VM...]
  transfers between devices with their start and end apart: 43 -> 43, of which waited for: 19 -> 18; matrix products, arithmetic and copies ran while one was open for 9% -> 8% of each run, Pallas kernels for 14% -> 15%
where the time goes in v3:
time: 329 us; the launch traced here: 326 us
  waiting for transfers between devices  107 us (33%)
  starting transfers between devices  79.5 us (24%)
  Pallas kernels  72.7 us (22%)
  blocking collectives  20.1 us (6%)
  local copies, waits for them, and re-layouts  16.5 us (5%)
  other arithmetic  16.3 us (5%)
  between operations  14.1 us (4%)
    ppermute x37, waiting for transfers between devices, send(): return lax.ppermute(x, AXES, pairs)  91.9 us
    ppermute x37, starting transfers between devices, send(): return lax.ppermute(x, AXES, pairs)  63.2 us
    pallas_call x15, Pallas kernels, call(): pl.pallas_call(body, out_shape=outs, in_specs=[SMEM] * len(scalars) + [VM...  36.5 us
    pallas_call x2, Pallas kernels, call(): pl.pallas_call(body, out_shape=outs, in_specs=[SMEM] * len(scalars) + [pl...  36.2 us
    all_to_all x1, blocking collectives, exchange(): lax.all_to_all(x, AXES, split_axis=0, concat_axis=0, tiled=True, axis_ind...  20.1 us
    all_to_all x3, starting transfers between devices, exchange(): lax.all_to_all(x, AXES, split_axis=0, concat_axis=0, tiled=True, axis_ind...  16.2 us
    all_gather x2, waiting for transfers between devices, spread(): lax.all_gather(x, AXES, axis=0, tiled=True, axis_index_groups=self.lines())  10.4 us
  transfers between devices with their start and end apart: 43, of which 18 were waited for; matrix products, arithmetic and copies ran while one was open for 8% of the time, Pallas kernels for 15%

profile of v3, /device:TPU:1, one launch (start us, length us, event | category | flops | bytes accessed | tf_op | source)
XLA Modules:
  0.0 326.5 jit_solution(4470285675988290195)
XLA Ops:
  7.2 2.2 collective-permute-start.19
  10.1 2.0 shard_map.230
  12.0 4.7 %all-to-all-start.2 = ((bf16[8,48,384]{2,1,0:T(8,128)(2,1)}), bf16[8,48,384]{2,1,0:T(8,128)(2,1)S(1)}, u32[]{:S(2)}, u32[]{:S(2)}) async-start(bf16[8,48,384]{2,1,0:T(8,128)(2,1)} %shard_map.230), calls=%async_computation.2 | async-start | bytes 589824 | tf_op jit(solution)/shard_map/all_to_all | solution.py:73
  16.7 5.9 %collective-permute-start.25 = (bf16[48,1536]{1,0:T(8,128)(2,1)}, bf16[48,1536]{1,0:T(8,128)(2,1)}, u32[]{:S(2)}, u32[]{:S(2)}) collective-permute-start(bf16[48,1536]{1,0:T(8,128)(2,1)} %param.30), channel_id=1, source_target_pairs={{0,0},{1,8},{2,16},{3,24},{4,1},{5,9},{6,17},{7,25},{8,2},{9,10},{... | collective-permute-start | bytes 442376 | tf_op jit(solution)/shard_map/ppermute | solution.py:41
  24.0 1.5 shard_map.231
  25.6 1.9 shard_map.232
  28.9 1.4 collective-permute-start.23
  33.5 6.4 %collective-permute-done.22.h3 = bf16[128,1536]{1,0:T(8,128)(2,1)S(1)} collective-permute-done((bf16[128,1536]{1,0:T(8,128)(2,1)S(1)}, bf16[128,1536]{1,0:T(8,128)(2,1)S(1)}, u32[]{:S(2)}, u32[]{:S(2)}) %collective-permute-start.22) | collective-permute-done | bytes 393248 | tf_op jit(solution)/shard_map/ppermute | solution.py:41
  40.6 30.4 %conditional.4 = (bf16[2,2,128,1536]{3,2,1,0:T(8,128)(2,1)}, bf16[2,2,128,1536]{3,2,1,0:T(8,128)(2,1)}, bf16[8,48,1024]{2,1,0:T(8,128)(2,1)S(1)}, bf16[2,128,1536]{2,1,0:T(8,128)(2,1)S(1)}) conditional(s32[]{:T(128)} %bitcast.35, () %tuple.60, (bf16[128,1536]{1,0:T(8,128)(2,1)}, bf16[128,1536]{1,0:T(8,128)(2,1)}, bf16[8,48,1024]{2,1,0:T(8,128)(2,1)S(1)}, ...), branch_computations={%region_0.1_spmd, %region_1.2_spmd} | conditional | flops 1572864 | bytes 18874520 | solution.py:48
  41.9 20.1 %all_to_all.18 = bf16[8,48,1024]{2,1,0:T(8,128)(2,1)S(1)} all-to-all(bf16[8,48,1024]{2,1,0:T(8,128)(2,1)S(1)} %get-tuple-element.78), channel_id=1, replica_groups={{0,1,2,3,4,5,6,7},{8,9,10,11,12,13,14,15},{16,17,18,19,20,21,22,23},{24..., dimensions={0} | all-to-all | bytes 1572864 | tf_op jit(solution)/shard_map/cond/branch_1_fun/all_to_all | solution.py:73
  62.0 1.3 pad_maximum_fusion
  64.1 6.9 %collective-permute-done.2 = bf16[128,1536]{1,0:T(8,128)(2,1)S(1)} collective-permute-done((bf16[128,1536]{1,0:T(8,128)(2,1)S(1)}, bf16[128,1536]{1,0:T(8,128)(2,1)S(1)}, u32[]{:S(2)}, u32[]{:S(2)}) %collective-permute-start.2) | collective-permute-done | bytes 393248 | tf_op jit(solution)/shard_map/cond/branch_1_fun/ppermute | solution.py:41
  71.1 10.4 %all-gather.3.cloned.1.call-done = bf16[2304,384]{1,0:T(8,128)(2,1)} async-done(((bf16[576,384]{1,0:T(8,128)(2,1)}), bf16[2304,384]{1,0:T(8,128)(2,1)}) %all-gather.3.cloned.1.call-update) | async-done | bytes 1769488 | tf_op jit(solution)/shard_map/all_gather | solution.py:83
  83.0 67.9 %conditional.5 = (bf16[1536,384]{1,0:T(8,128)(2,1)}, bf16[4,256,384]{2,1,0:T(8,128)(2,1)S(1)}, bf16[2,512,192]{2,1,0:T(8,128)(2,1)S(1)}, bf16[192,1536]{1,0:T(8,...) conditional(s32[]{:T(128)} %bitcast.35, () %tuple.59, ...), branch_computations={%region_2.3_spmd, %region_3.4_spmd} | conditional | flops 3145728 | bytes 68420128 | solution.py:48
  84.2 8.2 %branch_1_fun.7 = (bf16[1536,384]{1,0:T(8,128)(2,1)}, bf16[4,256,384]{2,1,0:T(8,128)(2,1)S(1)}, bf16[2,512,192]{2,1,0:T(8,128)(2,1)S(1)}) custom-call(s32[6]{0:T(128)S(1)} %get-tuple-element.87.meta, s32[4]{0:T(128)S(1)} %get-tuple-element.88.lens, s32[8]{0:T(128)S(1)} %get-tuple-element.89.spans, bf16[512,1536]{1,0:T(8,128)(2,1)} %bitcast.6.xa, ...), custom_call_target="tpu_custom_call" | custom-call | tf_op jit(solution)/shard_map/cond/branch_1_fun/pallas_call | solution.py:306
  92.4 1.8 branch_1_fun.8
  94.2 1.4 collective-permute-start.4
  95.6 2.8 branch_1_fun.9
  98.4 1.3 pad_maximum_fusion.3
  102.2 10.0 %collective-permute-done.5 = bf16[256,1536]{1,0:T(8,128)(2,1)S(1)} collective-permute-done((bf16[256,1536]{1,0:T(8,128)(2,1)S(1)}, bf16[256,1536]{1,0:T(8,128)(2,1)S(1)}, u32[]{:S(2)}, u32[]{:S(2)}) %collective-permute-start.5) | collective-permute-done | bytes 786464 | tf_op jit(solution)/shard_map/cond/branch_1_fun/ppermute | solution.py:41
  114.3 5.8 %collective-permute-done.7.b = bf16[128,1536]{1,0:T(8,128)(2,1)S(1)} collective-permute-done((bf16[128,1536]{1,0:T(8,128)(2,1)S(1)}, bf16[128,1536]{1,0:T(8,128)(2,1)S(1)}, u32[]{:S(2)}, u32[]{:S(2)}) %collective-permute-start.7) | collective-permute-done | bytes 393248 | tf_op jit(solution)/shard_map/cond/branch_1_fun/ppermute | solution.py:41
  120.9 2.1 branch_1_fun.10
  124.3 6.0 %collective-permute-done.8 = bf16[128,1536]{1,0:T(8,128)(2,1)S(1)} collective-permute-done((bf16[128,1536]{1,0:T(8,128)(2,1)}, bf16[128,1536]{1,0:T(8,128)(2,1)S(1)}, u32[]{:S(2)}, u32[]{:S(2)}) %collective-permute-start.8) | collective-permute-done | bytes 393248 | tf_op jit(solution)/shard_map/cond/branch_1_fun/ppermute | solution.py:41
  132.7 10.0 %collective-permute-done.9 = bf16[2,128,1536]{2,1,0:T(8,128)(2,1)S(1)} collective-permute-done((bf16[2,128,1536]{2,1,0:T(8,128)(2,1)S(1)}, bf16[2,128,1536]{2,1,0:T(8,128)(2,1)S(1)}, u32[]{:S(2)}, u32[]{:S(2)}) %collective-permute-start.9) | collective-permute-done | bytes 786464 | tf_op jit(solution)/shard_map/cond/branch_1_fun/ppermute | solution.py:41
  144.0 3.5 %collective-permute-start.10 = (bf16[2,2,128,1536]{3,2,1,0:T(8,128)(2,1)}, bf16[2,2,128,1536]{3,2,1,0:T(8,128)(2,1)}, u32[]{:S(2)}, u32[]{:S(2)}) collective-permute-start(bf16[2,2,128,1536]{3,2,1,0:T(8,128)(2,1)} %pad_maximum_fusion.4), channel_id=1, source_target_pairs={{0,1},{1,0},{2,3},{3,2},{4,5},{5,4},{6,7},{7,6},{8,9},{9,8},{10,11... | collective-permute-start | bytes 4718600 | tf_op jit(solution)/shard_map/cond/branch_1_fun/ppermute | solution.py:41
  147.4 3.4 %collective-permute-done.10 = bf16[2,2,128,1536]{3,2,1,0:T(8,128)(2,1)} collective-permute-done((bf16[2,2,128,1536]{3,2,1,0:T(8,128)(2,1)}, bf16[2,2,128,1536]{3,2,1,0:T(8,128)(2,1)}, u32[]{:S(2)}, u32[]{:S(2)}) %collective-permute-start.10) | collective-permute-done | bytes 1572896 | tf_op jit(solution)/shard_map/cond/branch_1_fun/ppermute | solution.py:41
  150.8 21.8 %shard_map.233 = (bf16[512,1536]{1,0:T(8,128)(2,1)}, bf16[512,1536]{1,0:T(8,128)(2,1)}, bf16[512,1536]{1,0:T(8,128)(2,1)}, bf16[512,1536]{1,0:T(8,128)(2,1)}, bf16[4,576,1024]{2,1,0:T(8,128)(2,1)}) custom-call(s32[6]{0:T(128)S(1)} %stack.99.meta, bf16[512,1536]{1,0:T(8,128)(2,1)} %get-tuple-element.264.h_ma, bf16[512,1536]{1,0:T(8,128)(2,1)} %get-tuple-element.265.h_mb, ...), custom_call_target="tpu_custom_call" | custom-call | tf_op jit(solution)/shard_map/pallas_call | solution.py:322
  172.6 71.0 %conditional.6 = (f32[128,1536]{1,0:T(8,128)S(1)}, bf16[512,1536]{1,0:T(8,128)(2,1)S(1)}, bf16[512,1536]{1,0:T(8,128)(2,1)S(1)}, bf16[128,1536]{1,0:T(8,128)(2,1...) conditional(s32[]{:T(128)} %bitcast.35, () %tuple.58, ...), branch_computations={%region_4.5_spmd, %region_5.6_spmd} | conditional | flops 5898240 | bytes 107741904 | solution.py:48
  173.1 1.8 convert_element_type.4
  174.9 1.4 collective-permute-done.11
  178.2 10.0 %collective-permute-done.12 = bf16[256,1536]{1,0:T(8,128)(2,1)S(1)} collective-permute-done((bf16[256,1536]{1,0:T(8,128)(2,1)S(1)}, bf16[256,1536]{1,0:T(8,128)(2,1)S(1)}, u32[]{:S(2)}, u32[]{:S(2)}) %collective-permute-start.12) | collective-permute-done | bytes 786464 | tf_op jit(solution)/shard_map/cond/branch_1_fun/ppermute | solution.py:41
  190.3 5.8 %collective-permute-done.13.b = bf16[128,1536]{1,0:T(8,128)(2,1)S(1)} collective-permute-done((bf16[128,1536]{1,0:T(8,128)(2,1)S(1)}, bf16[128,1536]{1,0:T(8,128)(2,1)S(1)}, u32[]{:S(2)}, u32[]{:S(2)}) %collective-permute-start.13) | collective-permute-done | bytes 393248 | tf_op jit(solution)/shard_map/cond/branch_1_fun/ppermute | solution.py:41
  196.9 2.2 branch_1_fun.11
  200.3 6.0 %collective-permute-done.14 = bf16[128,1536]{1,0:T(8,128)(2,1)S(1)} collective-permute-done((bf16[128,1536]{1,0:T(8,128)(2,1)}, bf16[128,1536]{1,0:T(8,128)(2,1)S(1)}, u32[]{:S(2)}, u32[]{:S(2)}) %collective-permute-start.14) | collective-permute-done | bytes 393248 | tf_op jit(solution)/shard_map/cond/branch_1_fun/ppermute | solution.py:41
  208.7 2.9 collective-permute-start.17
  211.6 7.1 %collective-permute-done.15 = bf16[2,128,1536]{2,1,0:T(8,128)(2,1)S(1)} collective-permute-done((bf16[2,128,1536]{2,1,0:T(8,128)(2,1)S(1)}, bf16[2,128,1536]{2,1,0:T(8,128)(2,1)S(1)}, u32[]{:S(2)}, u32[]{:S(2)}) %collective-permute-start.15) | collective-permute-done | bytes 786464 | tf_op jit(solution)/shard_map/cond/branch_1_fun/ppermute | solution.py:41
  218.9 3.4 %collective-permute-start.16 = (bf16[2,2,128,1536]{3,2,1,0:T(8,128)(2,1)S(1)}, bf16[2,2,128,1536]{3,2,1,0:T(8,128)(2,1)S(1)}, u32[]{:S(2)}, u32[]{:S(2)}) collective-permute-start(bf16[2,2,128,1536]{3,2,1,0:T(8,128)(2,1)S(1)} %pad_maximum_fusion.6), channel_id=1, source_target_pairs={{0,1},{1,0},{2,3},{3,2},{4,5},{5,4},{6,7},{7,6},{8,9},{9,8},{10,11... | collective-permute-start | bytes 4718600 | tf_op jit(solution)/shard_map/cond/branch_1_fun/ppermute | solution.py:41
  222.7 2.6 collective-permute-done.16
  227.0 14.4 %branch_1_fun.12 = (bf16[512,1536]{1,0:T(8,128)(2,1)S(1)}, bf16[512,1536]{1,0:T(8,128)(2,1)}, bf16[576,384]{1,0:T(8,128)(2,1)}, bf16[576,384]{1,0:T(8,128)(2,1)}...) custom-call(s32[6]{0:T(128)S(1)} %get-tuple-element.130.meta, s32[4]{0:T(128)S(1)} %get-tuple-element.131.lens, ...), custom_call_target="tpu_custom_call" | custom-call | tf_op jit(solution)/shard_map/cond/branch_1_fun/pallas_call | solution.py:322
  241.4 1.3 bitcast_add_fusion.1
  244.0 3.0 collective-permute-done.28
  250.8 5.8 %collective-permute-start.27 = (bf16[576,384]{1,0:T(8,128)(2,1)S(1)}, bf16[576,384]{1,0:T(8,128)(2,1)}, u32[]{:S(2)}, u32[]{:S(2)}) collective-permute-start(bf16[576,384]{1,0:T(8,128)(2,1)S(1)} %copy-done.14), channel_id=1, source_target_pairs={{0,8},{1,9},{2,10},{3,11},{4,12},{5,13},{6,14},{7,15},{24,16},{25,... | collective-permute-start | bytes 1327112 | tf_op jit(solution)/shard_map/ppermute | solution.py:41
  256.6 2.1 collective-permute-start.31
  259.9 2.1 slice.103
  262.0 2.8 collective-permute-done.27
  264.7 1.9 add.31
  266.6 1.4 collective-permute-start.30
  270.0 2.1 collective-permute-start.32
  272.1 5.5 %all-to-all-start.3 = ((bf16[8,48,1024]{2,1,0:T(8,128)(2,1)}), bf16[8,48,1024]{2,1,0:T(8,128)(2,1)S(1)}, u32[]{:S(2)}, u32[]{:S(2)}) async-start(bf16[8,48,1024]{2,1,0:T(8,128)(2,1)} %bitcast.52), calls=%async_computation.4 | async-start | bytes 1572864 | tf_op jit(solution)/shard_map/all_to_all | solution.py:73
  277.7 1.8 slice.105.u
  279.4 2.0 shard_map.235
  281.4 2.3 shard_map.234
  283.7 4.6 %collective-permute-start.34 = (bf16[576,384]{1,0:T(8,128)(2,1)}, bf16[576,384]{1,0:T(8,128)(2,1)}, u32[]{:S(2)}, u32[]{:S(2)}) collective-permute-start(bf16[576,384]{1,0:T(8,128)(2,1)} %get-tuple-element.295), channel_id=1, source_target_pairs={{0,8},{1,9},{2,10},{3,11},{4,12},{5,13},{6,14},{7,15},{8,0},{9,1},... | collective-permute-start | bytes 1327112 | tf_op jit(solution)/shard_map/ppermute | solution.py:41
  288.3 1.4 collective-permute-start.35
  289.7 1.9 shard_map.236
  292.4 2.3 shard_map.237
  294.7 4.3 %collective-permute-done.34.b = bf16[576,384]{1,0:T(8,128)(2,1)} collective-permute-done((bf16[576,384]{1,0:T(8,128)(2,1)}, bf16[576,384]{1,0:T(8,128)(2,1)}, u32[]{:S(2)}, u32[]{:S(2)}) %collective-permute-start.34) | collective-permute-done | bytes 442400 | tf_op jit(solution)/shard_map/ppermute | solution.py:41
  299.0 2.0 shard_map.238
  301.0 3.9 %collective-permute-start.36 = (bf16[48,1536]{1,0:T(8,128)(2,1)}, bf16[48,1536]{1,0:T(8,128)(2,1)S(1)}, u32[]{:S(2)}, u32[]{:S(2)}) collective-permute-start(bf16[48,1536]{1,0:T(8,128)(2,1)} %get-tuple-element.316), channel_id=1, source_target_pairs={{0,0},{8,1},{16,2},{24,3},{1,4},{9,5},{17,6},{25,7},{2,8},{10,9},{... | collective-permute-start | bytes 442376 | tf_op jit(solution)/shard_map/ppermute | solution.py:41
  305.0 12.2 %conditional.7 = (bf16[8,48,384]{2,1,0:T(8,128)(2,1)}, f32[48,4096]{1,0:T(8,128)}, f32[48,4096]{1,0:T(8,128)}, f32[48]{0:T(128)}) conditional(s32[]{:T(128)} %bitcast.35, () %tuple.71, (bf16[8,48,384]{2,1,0:T(8,128)(2,1)}, bf16[8,48,1024]{2,1,0:T(8,128)(2,1)S(1)}, bf16[48,4096]{1,0:T(8,128)(2,1)S(1)}, bf16[48,4096]{1,0:T(8,128)(2,1)S(1)}, ...), branch_computations={%region_7.8_spmd, %region_8.9_spmd} | conditional | bytes 1868014 | solution.py:48
  305.0 6.1 %all-to-all-start = ((bf16[8,48,384]{2,1,0:T(8,128)(2,1)}), bf16[8,48,384]{2,1,0:T(8,128)(2,1)}, u32[]{:S(2)}, u32[]{:S(2)}) async-start(bf16[8,48,384]{2,1,0:T(8,128)(2,1)} %get-tuple-element.156), calls=%async_computation | async-start | bytes 589824 | tf_op jit(solution)/shard_map/cond/branch_1_fun/all_to_all | solution.py:73
  311.0 1.4 branch_1_fun.13
  312.5 4.7 %all-to-all-done = bf16[8,48,384]{2,1,0:T(8,128)(2,1)} async-done(((bf16[8,48,384]{2,1,0:T(8,128)(2,1)}), bf16[8,48,384]{2,1,0:T(8,128)(2,1)}, u32[]{:S(2)}, u32[]{:S(2)}) %all-to-all-start) | async-done | bytes 294944 | tf_op jit(solution)/shard_map/cond/branch_1_fun/all_to_all | solution.py:73
  317.2 2.1 shard_map.239
  (158 shorter events, 42.6 us)
Async XLA Ops:
  7.2 18.4 %copy-start.7 = (bf16[2,64,1536]{2,1,0:T(8,128)(2,1)S(1)}, bf16[2,64,1536]{2,1,0:T(8,128)(2,1)}, u32[]{:S(2)}) copy-start(bf16[2,64,1536]{2,1,0:T(8,128)(2,1)} %param.23) | copy-start | bytes 1179652
  7.2 18.4 %copy-start.33 = (s32[8]{0:T(128)S(1)}, s32[8]{0:T(128)}, u32[]{:S(2)}) copy-start(s32[8]{0:T(128)} %spans.3) | copy-start | bytes 100
  7.2 20.3 %collective-permute-start.19 = (bf16[128,1536]{1,0:T(8,128)(2,1)}, bf16[128,1536]{1,0:T(8,128)(2,1)S(1)}, u32[]{:S(2)}, u32[]{:S(2)}) collective-permute-start(bf16[128,1536]{1,0:T(8,128)(2,1)} %h0.1), channel_id=1, source_target_pairs={{0,8},{1,9},{2,10},{3,11},{4,12},{5,13},{6,14},{7,15},{8,0},{9,1},... | collective-permute-start | bytes 1179656 | tf_op jit(solution)/shard_map/ppermute | solution.py:41
  9.4 18.2 %collective-permute-start.20 = (bf16[128,1536]{1,0:T(8,128)(2,1)}, bf16[128,1536]{1,0:T(8,128)(2,1)S(1)}, u32[]{:S(2)}, u32[]{:S(2)}) collective-permute-start(bf16[128,1536]{1,0:T(8,128)(2,1)} %h0.1), channel_id=1, source_target_pairs={{8,16},{9,17},{10,18},{11,19},{12,20},{13,21},{14,22},{15,23},{16,... | collective-permute-start | bytes 1179656 | tf_op jit(solution)/shard_map/ppermute | solution.py:41
  12.0 15.5 %all-to-all-start.2 = ((bf16[8,48,384]{2,1,0:T(8,128)(2,1)}), bf16[8,48,384]{2,1,0:T(8,128)(2,1)S(1)}, u32[]{:S(2)}, u32[]{:S(2)}) async-start(bf16[8,48,384]{2,1,0:T(8,128)(2,1)} %shard_map.230), calls=%async_computation.2 | async-start | bytes 589824 | tf_op jit(solution)/shard_map/all_to_all | solution.py:73
  16.7 64.8 %all-gather.3.cloned.1.call-start = ((), (), s32[]{:S(2)}) async-start(), calls=%async_computation.5 | async-start | bytes 2211840 | tf_op jit(solution)/shard_map/all_gather | solution.py:83
  16.7 13.7 %collective-permute-start.25 = (bf16[48,1536]{1,0:T(8,128)(2,1)}, bf16[48,1536]{1,0:T(8,128)(2,1)}, u32[]{:S(2)}, u32[]{:S(2)}) collective-permute-start(bf16[48,1536]{1,0:T(8,128)(2,1)} %param.30), channel_id=1, source_target_pairs={{0,0},{1,8},{2,16},{3,24},{4,1},{5,9},{6,17},{7,25},{8,2},{9,10},{... | collective-permute-start | bytes 442376 | tf_op jit(solution)/shard_map/ppermute | solution.py:41
  22.7 4.9 %collective-permute-start.21 = (s32[2]{0:T(128)}, s32[2]{0:T(128)S(1)}, u32[]{:S(2)}, u32[]{:S(2)}) collective-permute-start(s32[2]{0:T(128)} %lens.3), channel_id=1, source_target_pairs={{0,4},{1,5},{2,6},{3,7},{4,0},{5,1},{6,2},{7,3},{8,12},{9,13},{10,... | collective-permute-start | bytes 32 | tf_op jit(solution)/shard_map/ppermute | solution.py:41
  24.0 16.0 %copy-start.35 = (s32[2]{0:T(128)S(1)}, s32[2]{0:T(128)}, u32[]{:S(2)}) copy-start(s32[2]{0:T(128)} %lens.3) | copy-start | bytes 28
  27.5 12.5 %copy-start.24 = (bf16[128,1536]{1,0:T(8,128)(2,1)}, bf16[128,1536]{1,0:T(8,128)(2,1)S(1)}, u32[]{:S(2)}) copy-start(bf16[128,1536]{1,0:T(8,128)(2,1)S(1)} %get-tuple-element.256) | copy-start | bytes 1179652
  27.5 12.5 %copy-start.28 = (bf16[128,1536]{1,0:T(8,128)(2,1)}, bf16[128,1536]{1,0:T(8,128)(2,1)S(1)}, u32[]{:S(2)}) copy-start(bf16[128,1536]{1,0:T(8,128)(2,1)S(1)} %collective-permute-done.19.h1) | copy-start | bytes 1179652
  27.6 12.5 %copy-start.29 = (bf16[128,1536]{1,0:T(8,128)(2,1)}, bf16[128,1536]{1,0:T(8,128)(2,1)S(1)}, u32[]{:S(2)}) copy-start(bf16[128,1536]{1,0:T(8,128)(2,1)S(1)} %collective-permute-done.20.h2) | copy-start | bytes 1179652
  27.6 12.3 %collective-permute-start.22 = (bf16[128,1536]{1,0:T(8,128)(2,1)S(1)}, bf16[128,1536]{1,0:T(8,128)(2,1)S(1)}, u32[]{:S(2)}, u32[]{:S(2)}) collective-permute-start(bf16[128,1536]{1,0:T(8,128)(2,1)S(1)} %collective-permute-done.20.h2), channel_id=1, source_target_pairs={{8,0},{9,1},{10,2},{11,3},{12,4},{13,5},{14,6},{15,7},{16,24},{17,... | collective-permute-start | bytes 1179656 | tf_op jit(solution)/shard_map/ppermute | solution.py:41
  28.9 11.0 %collective-permute-start.23 = (bf16[128,1536]{1,0:T(8,128)(2,1)S(1)}, bf16[128,1536]{1,0:T(8,128)(2,1)}, u32[]{:S(2)}, u32[]{:S(2)}) collective-permute-start(bf16[128,1536]{1,0:T(8,128)(2,1)S(1)} %collective-permute-done.19.h1), channel_id=1, source_target_pairs={{8,16},{9,17},{10,18},{11,19},{12,20},{13,21},{14,22},{15,23},{16,... | collective-permute-start | bytes 1179656 | tf_op jit(solution)/shard_map/ppermute | solution.py:41
  30.3 9.6 %collective-permute-start.24 = (bf16[128,1536]{1,0:T(8,128)(2,1)}, bf16[128,1536]{1,0:T(8,128)(2,1)}, u32[]{:S(2)}, u32[]{:S(2)}) collective-permute-start(bf16[128,1536]{1,0:T(8,128)(2,1)} %get-tuple-element.250), channel_id=1, source_target_pairs={{0,4},{1,3},{2,6},{3,1},{4,0},{5,7},{6,2},{7,5},{8,12},{9,11},{10,... | collective-permute-start | bytes 1179656 | tf_op jit(solution)/shard_map/ppermute | solution.py:41
  33.5 6.4 %copy-start.27 = (bf16[576,384]{1,0:T(8,128)(2,1)}, bf16[576,384]{1,0:T(8,128)(2,1)S(1)}, u32[]{:S(2)}) copy-start(bf16[576,384]{1,0:T(8,128)(2,1)S(1)} %slice_dynamic-update-slice_fusion) | copy-start | bytes 1327108
  39.9 110.9 %all-gather.5.cloned.1.call-start = ((), (), s32[]{:S(2)}) async-start(), calls=%async_computation.6 | async-start | bytes 3932160 | tf_op jit(solution)/shard_map/all_gather | solution.py:83
  41.8 20.1 %collective-permute-start = (bf16[2,128,1536]{2,1,0:T(8,128)(2,1)S(1)}, bf16[2,128,1536]{2,1,0:T(8,128)(2,1)S(1)}, u32[]{:S(2)}, u32[]{:S(2)}) collective-permute-start(bf16[2,128,1536]{2,1,0:T(8,128)(2,1)S(1)} %pad_maximum_fusion.1), channel_id=1, source_target_pairs={{0,2},{1,5},{2,0},{3,7},{4,6},{5,1},{6,4},{7,3},{8,10},{9,13},{10,... | collective-permute-start | bytes 2359304 | tf_op jit(solution)/shard_map/cond/branch_1_fun/ppermute | solution.py:41
  63.3 7.7 %collective-permute-start.1 = (bf16[2,2,128,1536]{3,2,1,0:T(8,128)(2,1)}, bf16[2,2,128,1536]{3,2,1,0:T(8,128)(2,1)}, u32[]{:S(2)}, u32[]{:S(2)}) collective-permute-start(bf16[2,2,128,1536]{3,2,1,0:T(8,128)(2,1)} %pad_maximum_fusion), channel_id=1, source_target_pairs={{0,1},{1,0},{2,3},{3,2},{4,5},{5,4},{6,7},{7,6},{8,9},{9,8},{10,11... | collective-permute-start | bytes 4718600 | tf_op jit(solution)/shard_map/cond/branch_1_fun/ppermute | solution.py:41
  63.9 7.0 %collective-permute-start.2 = (bf16[128,1536]{1,0:T(8,128)(2,1)S(1)}, bf16[128,1536]{1,0:T(8,128)(2,1)S(1)}, u32[]{:S(2)}, u32[]{:S(2)}) collective-permute-start(bf16[128,1536]{1,0:T(8,128)(2,1)S(1)} %get-tuple-element.82), channel_id=1, source_target_pairs={{0,4},{1,3},{2,6},{3,1},{4,0},{5,7},{6,2},{7,5},{8,12},{9,11},{10,... | collective-permute-start | bytes 1179656 | tf_op jit(solution)/shard_map/cond/branch_1_fun/ppermute | solution.py:41
  71.1 10.5 %copy-start.8 = (bf16[8,48,1024]{2,1,0:T(8,128)(2,1)}, bf16[8,48,1024]{2,1,0:T(8,128)(2,1)S(1)}, u32[]{:S(2)}) copy-start(bf16[8,48,1024]{2,1,0:T(8,128)(2,1)S(1)} %get-tuple-element.268) | copy-start | bytes 2359300
  81.5 178.4 %reduce-scatter.2.cloned.1.call-start = ((), (), s32[]{:S(2)}) async-start(), calls=%async_computation.7 | async-start | bytes 5898240 | tf_op jit(solution)/shard_map/reduce_scatter | solution.py:89
  81.6 69.3 %collective-permute-start.26 = (bf16[128,1536]{1,0:T(8,128)(2,1)}, bf16[128,1536]{1,0:T(8,128)(2,1)}, u32[]{:S(2)}, u32[]{:S(2)}) collective-permute-start(bf16[128,1536]{1,0:T(8,128)(2,1)} %collective-permute-done.23.h4), channel_id=1, source_target_pairs={{8,0},{9,1},{10,2},{11,3},{12,4},{13,5},{14,6},{15,7},{16,24},{17,... | collective-permute-start | bytes 1179656 | tf_op jit(solution)/shard_map/ppermute | solution.py:41
  83.0 11.3 %collective-permute-start.3 = (bf16[2,128,1536]{2,1,0:T(8,128)(2,1)S(1)}, bf16[2,128,1536]{2,1,0:T(8,128)(2,1)S(1)}, u32[]{:S(2)}, u32[]{:S(2)}) collective-permute-start(bf16[2,128,1536]{2,1,0:T(8,128)(2,1)S(1)} %get-tuple-element.100), channel_id=1, source_target_pairs={{0,2},{1,5},{2,0},{3,7},{4,6},{5,1},{6,4},{7,3},{8,10},{9,13},{10,... | collective-permute-start | bytes 2359304 | tf_op jit(solution)/shard_map/cond/branch_1_fun/ppermute | solution.py:41
  84.2 8.3 %copy-start.2 = (bf16[2304,384]{1,0:T(8,128)(2,1)S(1)}, bf16[2304,384]{1,0:T(8,128)(2,1)}, u32[]{:S(2)}) copy-start(bf16[2304,384]{1,0:T(8,128)(2,1)} %get-tuple-element.92) | copy-start | bytes 5308420 | tf_op jit(solution)/shard_map/cond
  92.4 6.0 %copy-start = (bf16[2,512,192]{2,1,0:T(8,128)(2,1)}, bf16[2,512,192]{2,1,0:T(8,128)(2,1)S(1)}, u32[]{:S(2)}) copy-start(bf16[2,512,192]{2,1,0:T(8,128)(2,1)S(1)} %get-tuple-element.351.att) | copy-start | bytes 1179652 | tf_op jit(solution)/shard_map/cond
  94.2 5.5 %collective-permute-start.4 = (bf16[512,1536]{1,0:T(8,128)(2,1)}, bf16[512,1536]{1,0:T(8,128)(2,1)S(1)}, u32[]{:S(2)}, u32[]{:S(2)}) collective-permute-start(bf16[512,1536]{1,0:T(8,128)(2,1)} %get-tuple-element.106), channel_id=1, source_target_pairs={{0,1},{1,0},{2,3},{3,2},{4,5},{5,4},{6,7},{7,6},{8,9},{9,8},{10,11... | collective-permute-start | bytes 4718600 | tf_op jit(solution)/shard_map/cond/branch_1_fun/ppermute | solution.py:41
  100.8 11.4 %collective-permute-start.6 = (bf16[2,2,128,1536]{3,2,1,0:T(8,128)(2,1)}, bf16[2,2,128,1536]{3,2,1,0:T(8,128)(2,1)}, u32[]{:S(2)}, u32[]{:S(2)}) collective-permute-start(bf16[2,2,128,1536]{3,2,1,0:T(8,128)(2,1)} %pad_maximum_fusion.3), channel_id=1, source_target_pairs={{0,1},{1,0},{2,3},{3,2},{4,5},{5,4},{6,7},{7,6},{8,9},{9,8},{10,11... | collective-permute-start | bytes 4718600 | tf_op jit(solution)/shard_map/cond/branch_1_fun/ppermute | solution.py:41
  100.9 11.3 %collective-permute-start.5 = (bf16[256,1536]{1,0:T(8,128)(2,1)S(1)}, bf16[256,1536]{1,0:T(8,128)(2,1)S(1)}, u32[]{:S(2)}, u32[]{:S(2)}) collective-permute-start(bf16[256,1536]{1,0:T(8,128)(2,1)S(1)} %slice_bitcast_fusion), channel_id=1, source_target_pairs={{0,2},{1,5},{2,0},{3,7},{4,6},{5,1},{6,4},{7,3},{8,10},{9,13},{10,... | collective-permute-start | bytes 2359304 | tf_op jit(solution)/shard_map/cond/branch_1_fun/ppermute | solution.py:41
  113.1 7.0 %collective-permute-start.7 = (bf16[128,1536]{1,0:T(8,128)(2,1)S(1)}, bf16[128,1536]{1,0:T(8,128)(2,1)S(1)}, u32[]{:S(2)}, u32[]{:S(2)}) collective-permute-start(bf16[128,1536]{1,0:T(8,128)(2,1)S(1)} %get-tuple-element.323), channel_id=1, source_target_pairs={{0,4},{1,3},{2,6},{3,1},{4,0},{5,7},{6,2},{7,5},{8,12},{9,11},{10,... | collective-permute-start | bytes 1179656 | tf_op jit(solution)/shard_map/cond/branch_1_fun/ppermute | solution.py:41
  123.1 7.2 %collective-permute-start.8 = (bf16[128,1536]{1,0:T(8,128)(2,1)}, bf16[128,1536]{1,0:T(8,128)(2,1)S(1)}, u32[]{:S(2)}, u32[]{:S(2)}) collective-permute-start(bf16[128,1536]{1,0:T(8,128)(2,1)} %get-tuple-element.116), channel_id=1, source_target_pairs={{0,4},{1,3},{2,6},{3,1},{4,0},{5,7},{6,2},{7,5},{8,12},{9,11},{10,... | collective-permute-start | bytes 1179656 | tf_op jit(solution)/shard_map/cond/branch_1_fun/ppermute | solution.py:41
  131.4 11.3 %collective-permute-start.9 = (bf16[2,128,1536]{2,1,0:T(8,128)(2,1)S(1)}, bf16[2,128,1536]{2,1,0:T(8,128)(2,1)S(1)}, u32[]{:S(2)}, u32[]{:S(2)}) collective-permute-start(bf16[2,128,1536]{2,1,0:T(8,128)(2,1)S(1)} %get-tuple-element.322), channel_id=1, source_target_pairs={{0,2},{1,5},{2,0},{3,7},{4,6},{5,1},{6,4},{7,3},{8,10},{9,13},{10,... | collective-permute-start | bytes 2359304 | tf_op jit(solution)/shard_map/cond/branch_1_fun/ppermute | solution.py:41
  142.7 8.1 %copy-start.1 = (bf16[2,512,192]{2,1,0:T(8,128)(2,1)S(1)}, bf16[2,512,192]{2,1,0:T(8,128)(2,1)}, u32[]{:S(2)}) copy-start(bf16[2,512,192]{2,1,0:T(8,128)(2,1)} %copy-done) | copy-start | bytes 1179652 | tf_op jit(solution)/shard_map/cond
  144.0 6.9 %collective-permute-start.10 = (bf16[2,2,128,1536]{3,2,1,0:T(8,128)(2,1)}, bf16[2,2,128,1536]{3,2,1,0:T(8,128)(2,1)}, u32[]{:S(2)}, u32[]{:S(2)}) collective-permute-start(bf16[2,2,128,1536]{3,2,1,0:T(8,128)(2,1)} %pad_maximum_fusion.4), channel_id=1, source_target_pairs={{0,1},{1,0},{2,3},{3,2},{4,5},{5,4},{6,7},{7,6},{8,9},{9,8},{10,11... | collective-permute-start | bytes 4718600 | tf_op jit(solution)/shard_map/cond/branch_1_fun/ppermute | solution.py:41
  172.7 3.7 %collective-permute-start.11 = (bf16[512,1536]{1,0:T(8,128)(2,1)}, bf16[512,1536]{1,0:T(8,128)(2,1)S(1)}, u32[]{:S(2)}, u32[]{:S(2)}) collective-permute-start(bf16[512,1536]{1,0:T(8,128)(2,1)} %get-tuple-element.121), channel_id=1, source_target_pairs={{0,1},{1,0},{2,3},{3,2},{4,5},{5,4},{6,7},{7,6},{8,9},{9,8},{10,11... | collective-permute-start | bytes 4718600 | tf_op jit(solution)/shard_map/cond/branch_1_fun/ppermute | solution.py:41
  176.9 20.0 %copy-start.25 = (bf16[128,1536]{1,0:T(8,128)(2,1)S(1)}, bf16[128,1536]{1,0:T(8,128)(2,1)}, u32[]{:S(2)}) copy-start(bf16[128,1536]{1,0:T(8,128)(2,1)} %get-tuple-element.118.g_res) | copy-start | bytes 1179652 | tf_op jit(solution)/shard_map/cond
  176.9 11.3 %collective-permute-start.12 = (bf16[256,1536]{1,0:T(8,128)(2,1)S(1)}, bf16[256,1536]{1,0:T(8,128)(2,1)S(1)}, u32[]{:S(2)}, u32[]{:S(2)}) collective-permute-start(bf16[256,1536]{1,0:T(8,128)(2,1)S(1)} %slice.93), channel_id=1, source_target_pairs={{0,2},{1,5},{2,0},{3,7},{4,6},{5,1},{6,4},{7,3},{8,10},{9,13},{10,... | collective-permute-start | bytes 2359304 | tf_op jit(solution)/shard_map/cond/branch_1_fun/ppermute | solution.py:41
  189.1 7.0 %collective-permute-start.13 = (bf16[128,1536]{1,0:T(8,128)(2,1)S(1)}, bf16[128,1536]{1,0:T(8,128)(2,1)S(1)}, u32[]{:S(2)}, u32[]{:S(2)}) collective-permute-start(bf16[128,1536]{1,0:T(8,128)(2,1)S(1)} %get-tuple-element.329), channel_id=1, source_target_pairs={{0,4},{1,3},{2,6},{3,1},{4,0},{5,7},{6,2},{7,5},{8,12},{9,11},{10,... | collective-permute-start | bytes 1179656 | tf_op jit(solution)/shard_map/cond/branch_1_fun/ppermute | solution.py:41
  199.1 9.6 %copy-start.36 = (bf16[512,1536]{1,0:T(8,128)(2,1)S(1)}, bf16[512,1536]{1,0:T(8,128)(2,1)}, u32[]{:S(2)}) copy-start(bf16[512,1536]{1,0:T(8,128)(2,1)} %get-tuple-element.128) | copy-start | bytes 4718596 | tf_op jit(solution)/shard_map/cond
  199.1 7.2 %collective-permute-start.14 = (bf16[128,1536]{1,0:T(8,128)(2,1)}, bf16[128,1536]{1,0:T(8,128)(2,1)S(1)}, u32[]{:S(2)}, u32[]{:S(2)}) collective-permute-start(bf16[128,1536]{1,0:T(8,128)(2,1)} %get-tuple-element.126), channel_id=1, source_target_pairs={{0,4},{1,3},{2,6},{3,1},{4,0},{5,7},{6,2},{7,5},{8,12},{9,11},{10,... | collective-permute-start | bytes 1179656 | tf_op jit(solution)/shard_map/cond/branch_1_fun/ppermute | solution.py:41
  207.4 11.3 %collective-permute-start.15 = (bf16[2,128,1536]{2,1,0:T(8,128)(2,1)S(1)}, bf16[2,128,1536]{2,1,0:T(8,128)(2,1)S(1)}, u32[]{:S(2)}, u32[]{:S(2)}) collective-permute-start(bf16[2,128,1536]{2,1,0:T(8,128)(2,1)S(1)} %get-tuple-element.328), channel_id=1, source_target_pairs={{0,2},{1,5},{2,0},{3,7},{4,6},{5,1},{6,4},{7,3},{8,10},{9,13},{10,... | collective-permute-start | bytes 2359304 | tf_op jit(solution)/shard_map/cond/branch_1_fun/ppermute | solution.py:41
  208.7 13.6 %collective-permute-start.17 = (bf16[512,1536]{1,0:T(8,128)(2,1)S(1)}, bf16[512,1536]{1,0:T(8,128)(2,1)S(1)}, u32[]{:S(2)}, u32[]{:S(2)}) collective-permute-start(bf16[512,1536]{1,0:T(8,128)(2,1)S(1)} %copy-done.36), channel_id=1, source_target_pairs={{0,1},{1,0},{2,3},{3,2},{4,5},{5,4},{6,7},{7,6},{8,9},{9,8},{10,11... | collective-permute-start | bytes 4718600 | tf_op jit(solution)/shard_map/cond/branch_1_fun/ppermute | solution.py:41
  218.9 6.5 %collective-permute-start.16 = (bf16[2,2,128,1536]{3,2,1,0:T(8,128)(2,1)S(1)}, bf16[2,2,128,1536]{3,2,1,0:T(8,128)(2,1)S(1)}, u32[]{:S(2)}, u32[]{:S(2)}) collective-permute-start(bf16[2,2,128,1536]{3,2,1,0:T(8,128)(2,1)S(1)} %pad_maximum_fusion.6), channel_id=1, source_target_pairs={{0,1},{1,0},{2,3},{3,2},{4,5},{5,4},{6,7},{7,6},{8,9},{9,8},{10,11... | collective-permute-start | bytes 4718600 | tf_op jit(solution)/shard_map/cond/branch_1_fun/ppermute | solution.py:41
  225.4 16.0 %collective-permute-start.18 = (bf16[256,1536]{1,0:T(8,128)(2,1)S(1)}, bf16[256,1536]{1,0:T(8,128)(2,1)}, u32[]{:S(2)}, u32[]{:S(2)}) collective-permute-start(bf16[256,1536]{1,0:T(8,128)(2,1)S(1)} %slice_bitcast_fusion.1), channel_id=1, source_target_pairs={{0,2},{1,5},{2,0},{3,7},{4,6},{5,1},{6,4},{7,3},{8,10},{9,13},{10,... | collective-permute-start | bytes 2359304 | tf_op jit(solution)/shard_map/cond/branch_1_fun/ppermute | solution.py:41
  243.6 3.5 %collective-permute-start.28 = (bf16[512,1536]{1,0:T(8,128)(2,1)S(1)}, bf16[512,1536]{1,0:T(8,128)(2,1)S(1)}, u32[]{:S(2)}, u32[]{:S(2)}) collective-permute-start(bf16[512,1536]{1,0:T(8,128)(2,1)S(1)} %get-tuple-element.283), channel_id=1, source_target_pairs={{0,1},{1,0},{2,3},{3,2},{4,5},{5,4},{6,7},{7,6},{8,9},{9,8},{10,11... | collective-permute-start | bytes 4718600 | tf_op jit(solution)/shard_map/ppermute | solution.py:41
  249.6 18.5 %copy-start.4 = (bf16[512,1536]{1,0:T(8,128)(2,1)S(1)}, bf16[512,1536]{1,0:T(8,128)(2,1)}, u32[]{:S(2)}) copy-start(bf16[512,1536]{1,0:T(8,128)(2,1)} %copy-done.3) | copy-start | bytes 4718596
  249.6 15.2 %collective-permute-start.29 = (bf16[256,1536]{1,0:T(8,128)(2,1)}, bf16[256,1536]{1,0:T(8,128)(2,1)}, u32[]{:S(2)}, u32[]{:S(2)}) collective-permute-start(bf16[256,1536]{1,0:T(8,128)(2,1)} %slice.102), channel_id=1, source_target_pairs={{0,2},{1,5},{2,0},{3,7},{4,6},{5,1},{6,4},{7,3},{8,10},{9,13},{10,... | collective-permute-start | bytes 2359304 | tf_op jit(solution)/shard_map/ppermute | solution.py:41
  250.8 14.0 %collective-permute-start.27 = (bf16[576,384]{1,0:T(8,128)(2,1)S(1)}, bf16[576,384]{1,0:T(8,128)(2,1)}, u32[]{:S(2)}, u32[]{:S(2)}) collective-permute-start(bf16[576,384]{1,0:T(8,128)(2,1)S(1)} %copy-done.14), channel_id=1, source_target_pairs={{0,8},{1,9},{2,10},{3,11},{4,12},{5,13},{6,14},{7,15},{24,16},{25,... | collective-permute-start | bytes 1327112 | tf_op jit(solution)/shard_map/ppermute | solution.py:41
  256.6 24.8 %collective-permute-start.31 = (bf16[576,384]{1,0:T(8,128)(2,1)}, bf16[576,384]{1,0:T(8,128)(2,1)}, u32[]{:S(2)}, u32[]{:S(2)}) collective-permute-start(bf16[576,384]{1,0:T(8,128)(2,1)} %get-tuple-element.289.c), channel_id=1, source_target_pairs={{0,8},{1,9},{2,10},{3,11},{4,12},{5,13},{6,14},{7,15},{24,16},{25,... | collective-permute-start | bytes 1327112 | tf_op jit(solution)/shard_map/ppermute | solution.py:41
  258.7 22.7 %collective-permute-start.33 = (bf16[128,1536]{1,0:T(8,128)(2,1)}, bf16[128,1536]{1,0:T(8,128)(2,1)}, u32[]{:S(2)}, u32[]{:S(2)}) collective-permute-start(bf16[128,1536]{1,0:T(8,128)(2,1)} %get-tuple-element.292), channel_id=1, source_target_pairs={{0,4},{1,3},{2,6},{3,1},{4,0},{5,7},{6,2},{7,5},{8,12},{9,11},{10,... | collective-permute-start | bytes 1179656 | tf_op jit(solution)/shard_map/ppermute | solution.py:41
  266.6 14.8 %collective-permute-start.30 = (bf16[576,384]{1,0:T(8,128)(2,1)}, bf16[576,384]{1,0:T(8,128)(2,1)}, u32[]{:S(2)}, u32[]{:S(2)}) collective-permute-start(bf16[576,384]{1,0:T(8,128)(2,1)} %add.31), channel_id=1, source_target_pairs={{8,16},{9,17},{10,18},{11,19},{12,20},{13,21},{14,22},{15,23},{16,... | collective-permute-start | bytes 1327112 | tf_op jit(solution)/shard_map/ppermute | solution.py:41
  270.0 11.4 %collective-permute-start.32 = (bf16[128,1536]{1,0:T(8,128)(2,1)}, bf16[128,1536]{1,0:T(8,128)(2,1)}, u32[]{:S(2)}, u32[]{:S(2)}) collective-permute-start(bf16[128,1536]{1,0:T(8,128)(2,1)} %slice.104), channel_id=1, source_target_pairs={{0,4},{1,3},{2,6},{3,1},{4,0},{5,7},{6,2},{7,5},{8,12},{9,11},{10,... | collective-permute-start | bytes 1179656 | tf_op jit(solution)/shard_map/ppermute | solution.py:41
  272.1 9.3 %copy-start.13 = (bf16[576,384]{1,0:T(8,128)(2,1)S(1)}, bf16[576,384]{1,0:T(8,128)(2,1)}, u32[]{:S(2)}) copy-start(bf16[576,384]{1,0:T(8,128)(2,1)} %get-tuple-element.281.a) | copy-start | bytes 1327108
  272.1 22.6 %all-to-all-start.3 = ((bf16[8,48,1024]{2,1,0:T(8,128)(2,1)}), bf16[8,48,1024]{2,1,0:T(8,128)(2,1)S(1)}, u32[]{:S(2)}, u32[]{:S(2)}) async-start(bf16[8,48,1024]{2,1,0:T(8,128)(2,1)} %bitcast.52), calls=%async_computation.4 | async-start | bytes 1572864 | tf_op jit(solution)/shard_map/all_to_all | solution.py:73
  279.4 10.3 %copy-start.23 = (bf16[128,1536]{1,0:T(8,128)(2,1)S(1)}, bf16[128,1536]{1,0:T(8,128)(2,1)}, u32[]{:S(2)}) copy-start(bf16[128,1536]{1,0:T(8,128)(2,1)} %copy-done.22) | copy-start | bytes 1179652
  283.7 8.7 %copy-start.10 = (f32[128,1536]{1,0:T(8,128)S(1)}, f32[128,1536]{1,0:T(8,128)}, u32[]{:S(2)}) copy-start(f32[128,1536]{1,0:T(8,128)} %copy-done.9) | copy-start | bytes 2359300
  283.7 15.3 %collective-permute-start.34 = (bf16[576,384]{1,0:T(8,128)(2,1)}, bf16[576,384]{1,0:T(8,128)(2,1)}, u32[]{:S(2)}, u32[]{:S(2)}) collective-permute-start(bf16[576,384]{1,0:T(8,128)(2,1)} %get-tuple-element.295), channel_id=1, source_target_pairs={{0,8},{1,9},{2,10},{3,11},{4,12},{5,13},{6,14},{7,15},{8,0},{9,1},... | collective-permute-start | bytes 1327112 | tf_op jit(solution)/shard_map/ppermute | solution.py:41
  288.3 10.7 %collective-permute-start.35 = (bf16[576,384]{1,0:T(8,128)(2,1)}, bf16[576,384]{1,0:T(8,128)(2,1)}, u32[]{:S(2)}, u32[]{:S(2)}) collective-permute-start(bf16[576,384]{1,0:T(8,128)(2,1)} %get-tuple-element.296), channel_id=1, source_target_pairs={{8,16},{9,17},{10,18},{11,19},{12,20},{13,21},{14,22},{15,23},{16,... | collective-permute-start | bytes 1327112 | tf_op jit(solution)/shard_map/ppermute | solution.py:41
  291.6 7.4 %copy-start.15 = (bf16[576,384]{1,0:T(8,128)(2,1)S(1)}, bf16[576,384]{1,0:T(8,128)(2,1)}, u32[]{:S(2)}) copy-start(bf16[576,384]{1,0:T(8,128)(2,1)} %get-tuple-element.306.a) | copy-start | bytes 1327108
  292.4 12.5 %copy-start.20 = (bf16[48,4096]{1,0:T(8,128)(2,1)S(1)}, bf16[48,4096]{1,0:T(8,128)(2,1)}, u32[]{:S(2)}) copy-start(bf16[48,4096]{1,0:T(8,128)(2,1)} %wg.1) | copy-start | bytes 1179652
  292.4 12.5 %copy-start.21 = (bf16[48,4096]{1,0:T(8,128)(2,1)S(1)}, bf16[48,4096]{1,0:T(8,128)(2,1)}, u32[]{:S(2)}) copy-start(bf16[48,4096]{1,0:T(8,128)(2,1)} %wu.1) | copy-start | bytes 1179652
  292.4 12.5 %copy-start.34 = (bf16[48]{0:T(256)(128)(2,1)S(1)}, bf16[48]{0:T(256)(128)(2,1)}, u32[]{:S(2)}) copy-start(bf16[48]{0:T(256)(128)(2,1)} %param.31) | copy-start | bytes 292
  301.0 18.2 %collective-permute-start.36 = (bf16[48,1536]{1,0:T(8,128)(2,1)}, bf16[48,1536]{1,0:T(8,128)(2,1)S(1)}, u32[]{:S(2)}, u32[]{:S(2)}) collective-permute-start(bf16[48,1536]{1,0:T(8,128)(2,1)} %get-tuple-element.316), channel_id=1, source_target_pairs={{0,0},{8,1},{16,2},{24,3},{1,4},{9,5},{17,6},{25,7},{2,8},{10,9},{... | collective-permute-start | bytes 442376 | tf_op jit(solution)/shard_map/ppermute | solution.py:41
  305.0 12.2 %all-to-all-start = ((bf16[8,48,384]{2,1,0:T(8,128)(2,1)}), bf16[8,48,384]{2,1,0:T(8,128)(2,1)}, u32[]{:S(2)}, u32[]{:S(2)}) async-start(bf16[8,48,384]{2,1,0:T(8,128)(2,1)} %get-tuple-element.156), calls=%async_computation | async-start | bytes 589824 | tf_op jit(solution)/shard_map/cond/branch_1_fun/all_to_all | solution.py:73
  (16 other events, 35.4 us)
Sparse Core Ops, SparseCore 0:
  40.1 41.4 all-gather.2
  83.6 62.3 all-gather.4
  172.7 85.9 reduce-scatter.1
